TPU v7x, 32 devices: a whole 2x2x4 slice. The times are simulated.
32 devices in a mesh: seq: 16 (over z, x, core), head: 2 (over y).
Axes of the slice: x: 2, y: 2, z: 4, core: 2. Of those that a mesh axis runs over, the one named last changes fastest.
Arguments:
- queries: bfloat16 [1024, 16384], P('seq', 'head'), may hold values from -12 to 12
- keys: bfloat16 [1024, 1024], P('seq', 'head'), may hold values from -12 to 12
- values: bfloat16 [1024, 1024], P('seq', 'head'), may hold values from -6 to 6
- q_feature: bfloat16 [128, 128, 64], P('head'), may hold values from -1.1953125 to 1.1953125
- k_feature: bfloat16 [128, 128, 64], P('head'), may hold values from -1.1953125 to 1.1953125
- window_factor: float32 [128], P('head'), may hold values from 0.3 to 0.9
Outputs:
- mixed: bfloat16 [1024, 16384], P(('seq', 'head'))
All inputs are finite; a program needn't handle non-finite values.
Results may differ from a plain program's by a relative error of at most 0.005.
Values may be sent and summed in bfloat16 or wider, within the bound.
No kernel may reach another device: no remote copies, remote signals or barrier semaphores. Data moves between devices by JAX's collectives and lax.ppermute only.
A program may use at most 192 MiB of HBM per device.

v0:
```python
import math

import jax
import jax.numpy as jnp
from jax import lax
from jax.experimental import pallas as pl
from jax.experimental.pallas import tpu as pltpu
from jax.sharding import PartitionSpec as P

DH = 128
WINDOW = 64
F32 = jnp.float32
BF16 = jnp.bfloat16


def dot_t(a, b):
    return lax.dot_general(a, b, (((1,), (1,)), ((), ())), preferred_element_type=F32)


def features_t(logits):
    top = jnp.max(logits, axis=0, keepdims=True)
    low = jnp.min(logits, axis=0, keepdims=True)
    up = jnp.exp(logits - top)
    down = jnp.exp(low - logits)
    up = up * (1.0 / jnp.sum(up, axis=0, keepdims=True))
    down = down * (1.0 / jnp.sum(down, axis=0, keepdims=True))
    return jnp.concatenate([up.astype(BF16), down.astype(BF16)], axis=0)


def mix_kernel(
    place_ref, q_ref, k_ref, v_ref, wq_ref, wk_ref, ratio_ref, out_ref, fk_scr, state_scr
):
    tok = q_ref.shape[0]
    heads, feat, dh = wq_ref.shape
    seen = fk_scr.shape[1]
    place = place_ref[0]
    first_head = pl.program_id(0) * heads

    weights = wk_ref[...].reshape(heads * feat, dh)
    for start in range(0, seen, 256):
        size = min(256, seen - start)
        logits = dot_t(weights, k_ref[start : start + size, :])
        for h in range(heads):
            fk_scr[h * 2 * feat : (h + 1) * 2 * feat, start : start + size] = features_t(
                logits[h * feat : (h + 1) * feat]
            )
    row = lax.broadcasted_iota(jnp.int32, (seen, dh), 0)
    kept = row < (place - 1) * tok
    v_seen = jnp.where(kept, v_ref[:seen, :].astype(F32), 0.0).astype(BF16)
    ones_seen = jnp.where(kept, 1.0, 0.0).astype(BF16)
    v_seen = jnp.concatenate([v_seen, ones_seen], axis=1)
    state_scr[...] = jnp.dot(fk_scr[...], v_seen, preferred_element_type=F32).astype(BF16)

    before = pl.multiple_of(jnp.maximum(place - 1, 0) * tok, tok)
    own = pl.multiple_of(place * tok, tok)
    k_ext = jnp.concatenate([k_ref[pl.ds(before, tok), :], k_ref[pl.ds(own, tok), :]], axis=0)
    v_ext = jnp.concatenate([v_ref[pl.ds(before, tok), :], v_ref[pl.ds(own, tok), :]], axis=0)
    v_ext = jnp.concatenate([v_ext, jnp.ones_like(v_ext)], axis=1)
    row = lax.broadcasted_iota(jnp.int32, (tok, 2 * tok), 0)
    col = lax.broadcasted_iota(jnp.int32, (tok, 2 * tok), 1)
    valid = (col >= tok) | (place > 0)
    inside = (col > row) & (col <= row + WINDOW) & valid
    causal = (col <= row) & valid
    lane = lax.broadcasted_iota(jnp.int32, (tok, 2 * feat), 1)
    left = lane < feat
    side_r = lax.broadcasted_iota(jnp.int32, (2 * feat, 2 * feat), 0) < feat
    side_c = lax.broadcasted_iota(jnp.int32, (2 * feat, 2 * feat), 1) < feat
    halves = jnp.where(side_r == side_c, 1.0, 0.0).astype(BF16)

    for h in range(heads):
        q = q_ref[:, h * dh : (h + 1) * dh]
        wq = wq_ref[h]
        logits = dot_t(q, jnp.concatenate([wq, -wq], axis=0))
        top_l = jnp.max(jnp.where(left, logits, -jnp.inf), axis=1, keepdims=True)
        top_r = jnp.max(jnp.where(left, -jnp.inf, logits), axis=1, keepdims=True)
        expd = jnp.exp(logits - jnp.where(left, top_l, top_r)).astype(BF16)
        total = jnp.dot(expd, halves, preferred_element_type=F32)
        fq = (expd.astype(F32) / total).astype(BF16)
        fk = features_t(dot_t(wk_ref[h], k_ext))
        linear = jnp.dot(fq, fk, preferred_element_type=F32)
        scores = dot_t(q, k_ext) * (1.0 / math.sqrt(dh))
        masked = jnp.where(inside, scores, -jnp.inf)
        top = jnp.max(masked, axis=1, keepdims=True)
        soft = jnp.exp(masked - top) * ratio_ref[first_head + h]
        weight = jnp.where(causal, linear, soft).astype(BF16)
        both = jnp.dot(weight, v_ext, preferred_element_type=F32) + jnp.dot(
            fq, state_scr[h * 2 * feat : (h + 1) * 2 * feat, :], preferred_element_type=F32
        )
        out_ref[:, h * dh : (h + 1) * dh] = (both[:, :dh] / both[:, dh:]).astype(BF16)


def mix(place, queries, kv, wq, wk, ratio, group):
    tok = queries.shape[0]
    local_heads, feat, dh = wq.shape
    groups = local_heads // group
    tokens = kv.shape[0]
    seen = tokens - 2 * tok
    return pl.pallas_call(
        mix_kernel,
        grid_spec=pltpu.PrefetchScalarGridSpec(
            num_scalar_prefetch=1,
            grid=(groups,),
            in_specs=[
                pl.BlockSpec((tok, group * dh), lambda g, p: (0, g)),
                pl.BlockSpec((tokens, dh), lambda g, p: (0, g)),
                pl.BlockSpec((tokens, dh), lambda g, p: (0, groups + g)),
                pl.BlockSpec((group, feat, dh), lambda g, p: (g, 0, 0)),
                pl.BlockSpec((group, feat, dh), lambda g, p: (g, 0, 0)),
                pl.BlockSpec(memory_space=pltpu.SMEM),
            ],
            out_specs=pl.BlockSpec((tok, group * dh), lambda g, p: (0, g)),
            scratch_shapes=[
                pltpu.VMEM((group * 2 * feat, seen), BF16),
                pltpu.VMEM((group * 2 * feat, 2 * dh), BF16),
            ],
        ),
        out_shape=jax.ShapeDtypeStruct(queries.shape, BF16),
        compiler_params=pltpu.CompilerParams(vmem_limit_bytes=48 * 2**20),
        cost_estimate=pl.CostEstimate(
            flops=2 * local_heads * tokens * 3 * feat * 2 * dh,
            bytes_accessed=8 * 2**20,
            transcendentals=local_heads * tokens * 2 * feat,
        ),
    )(place, queries, kv, kv, wq, wk, ratio)


WAYS = 4

EARLY = pl.CostEstimate(flops=10**10, bytes_accessed=10**8, transcendentals=0)
EARLY_KERNELS = ("pack_kv", "pack_q", "pair_kv", "stack_kv")


SLOTS = (
    ((0, 0), (0, 0)),
    ((2, 0), (0, 1)),
    ((0, 1), (2, 0)),
    ((3, 0), (1, 1)),
    ((1, 1), (3, 0)),
    ((2, 1), (2, 1)),
    ((3, 1), (3, 1)),
    ((1, 0), (1, 0)),
)


def slot_of(n, odd):
    return [jnp.where(odd == 1, b, a) if a != b else a for a, b in zip(*SLOTS[n])]


def spot():
    at = lax.axis_index("seq")
    return lax.rem(at, WAYS), lax.div(at, WAYS)


def aligned(at, step):
    return pl.ds(pl.multiple_of(at * step, step), step)


def with_ones(values, kept=True):
    here = jnp.where(kept, 1.0, 0.0).astype(BF16)
    return jnp.concatenate([values, jnp.full(values.shape, here)], axis=1)


def pack_kv_kernel(k_ref, v_ref, k_away_ref, v_away_ref, own_ref, away_ref):
    odd = lax.rem(spot()[0], 2)
    for k, v, ref in ((k_ref, v_ref, own_ref), (k_away_ref, v_away_ref, away_ref)):
        for d in range(2):
            at = aligned(odd ^ d, DH)
            ref[:, 2 * d * DH : (2 * d + 1) * DH] = k[:, at]
            ref[:, (2 * d + 1) * DH : (2 * d + 2) * DH] = v[:, at]


def pair_kernel(own_ref, got_ref, out_ref):
    tok = own_ref.shape[0]
    out_ref[:tok, :] = own_ref[:, 2 * DH :]
    out_ref[tok:, :] = got_ref[:, 2 * DH :]


def stack_kernel(own_ref, got_ref, pair_ref, out_ref):
    tok = own_ref.shape[0]
    place = spot()[0]
    out_ref[aligned(place, tok), :] = own_ref[:, : 2 * DH]
    out_ref[aligned(place ^ 2, tok), :] = got_ref[:, : 2 * DH]
    out_ref[aligned(place ^ 1, tok), :] = pair_ref[:tok, :]
    out_ref[aligned(place ^ 3, tok), :] = pair_ref[tok:, :]


def pack_q_kernel(q_ref, *out_refs):
    place = spot()[0]
    for d, out in enumerate(out_refs):
        out[...] = q_ref[:, aligned(place ^ d, out.shape[1])]


def weights_kernel(wq_ref, factor_ref, both_ref, ratio_ref):
    heads = both_ref.shape[0]
    shape = (heads, factor_ref.shape[1])
    head = lax.broadcasted_iota(jnp.int32, shape, 0) + spot()[0] * heads
    ratio = jnp.broadcast_to((1.0 - factor_ref[...]) / factor_ref[...], shape)
    ratio = jnp.where(lax.broadcasted_iota(jnp.int32, shape, 1) == head, ratio, 0.0)
    ratio = jnp.sum(ratio, axis=1, keepdims=True)
    ratio_ref[...] = jnp.broadcast_to(ratio, ratio_ref.shape)
    for h in range(heads):
        wq = wq_ref[h].T
        both_ref[h] = jnp.concatenate([wq, -wq], axis=1)


def join_kernel(slots, *refs):
    got, out_ref, sems = refs[: len(slots)], *refs[-2:]
    width = got[0].shape[1]
    place, side = spot()[0], lax.axis_index("head")
    copies = []
    for n, ref in zip(slots, got):
        dr, dy = slot_of(n, lax.rem(place, 2) ^ (SLOTS[n][0][0] & 1))
        at = aligned((side ^ dy) * WAYS + (place ^ dr), width)
        copies.append(pltpu.make_async_copy(ref, out_ref.at[:, at], sems.at[len(copies)]))
    for copy in copies:
        copy.start()
    for copy in copies:
        copy.wait()


def write_key_features(keys, wk_ref, fk_ref):
    heads, feat, dh = wk_ref.shape
    logits = dot_t(wk_ref[...].reshape(heads * feat, dh), keys)
    for h in range(heads):
        part = logits[h * feat : (h + 1) * feat]
        top = jnp.max(part, axis=0, keepdims=True)
        low = jnp.min(part, axis=0, keepdims=True)
        for n, shifted in enumerate((part - top, low - part)):
            row = (2 * h + n) * feat
            expd = jnp.exp(shifted.astype(BF16))
            total = expd[: feat // 4]
            for q in range(1, 4):
                total = total + expd[q * feat // 4 : (q + 1) * feat // 4]
            total = jnp.sum(total.astype(F32), axis=0, keepdims=True)
            fk_ref[row : row + feat, :] = expd * pl.reciprocal(total).astype(BF16)


def own_features_kernel(own_ref, wk_ref, fk_ref):
    write_key_features(own_ref[:, :DH], wk_ref, fk_ref.at[:, own_ref.shape[0] :])


def last_features_kernel(last_ref, wk_ref, _, fk_ref, past_ref, step_ref):
    size = last_ref.shape[0]
    half = size // 2
    level = spot()[1]

    @pl.when(level == 0)
    def _():
        fk_ref[:, :size] = jnp.zeros((fk_ref.shape[0], size), BF16)
        for ref in (past_ref, step_ref):
            ref[...] = jnp.zeros_like(ref)

    @pl.when(level > 0)
    def _():
        write_key_features(last_ref[:, :DH], wk_ref, fk_ref.at[:, :size])
        for at, ref in ((0, past_ref), (half, step_ref)):
            ref[...] = jnp.dot(
                fk_ref[:, at : at + half],
                with_ones(last_ref[at : at + half, DH:]),
                preferred_element_type=F32,
            )


def past_kernel(before_ref, wk_ref, sum_ref, past_ref, fk_scr):
    level = spot()[1]

    @pl.when(level < 2)
    def _():
        past_ref[...] = sum_ref[...]

    @pl.when(level >= 2)
    def _():
        write_key_features(before_ref[:, :DH], wk_ref, fk_scr)
        past_ref[...] = sum_ref[...] + jnp.dot(
            fk_scr[...], with_ones(before_ref[:, DH:]), preferred_element_type=F32
        )


def query_features_kernel(a_ref, b_ref, w_ref, ratio_ref, q_out, fq_out, exp_scr):
    tok = a_ref.shape[0]
    heads, dh, both = w_ref.shape
    half = 2 * tok
    place = spot()[0]
    for d, ref in enumerate((a_ref, b_ref)):
        row = pl.multiple_of(lax.rem(place ^ d, 2) * tok, tok)
        for h in range(heads):
            q_out[pl.ds(h * half + row, tok), :] = ref[:, h * dh : (h + 1) * dh]
    rows_of = [slice(h * half, (h + 1) * half) for h in range(heads)]
    left = lax.broadcasted_iota(jnp.int32, (half, both), 1) < both // 2
    for h, rows in enumerate(rows_of):
        logits = jnp.dot(q_out[rows, :], w_ref[h], preferred_element_type=F32)
        top_l = jnp.max(jnp.where(left, logits, -jnp.inf), axis=1, keepdims=True)
        top_r = jnp.max(jnp.where(left, -jnp.inf, logits), axis=1, keepdims=True)
        exp_scr[rows, :] = jnp.exp((logits - jnp.where(left, top_l, top_r)).astype(BF16))
    side_r = lax.broadcasted_iota(jnp.int32, (both, both), 0) < both // 2
    side_c = lax.broadcasted_iota(jnp.int32, (both, both), 1) < both // 2
    halves = jnp.where(side_r == side_c, 1.0, 0.0).astype(BF16)
    total = jnp.dot(exp_scr[...], halves, preferred_element_type=F32)
    for h, rows in enumerate(rows_of):
        scale = pl.reciprocal(total[rows], approx=True) * ratio_ref[h : h + 1, :]
        fq_out[rows, :] = (exp_scr[rows, :].astype(F32) * scale).astype(BF16)


def near_kernel(other, q_ref, fq_ref, last_ref, own_ref, fk_ref, near_ref, kv_scr, w_scr):
    half, dh = last_ref.shape[0] // 2, q_ref.shape[1]
    heads = q_ref.shape[0] // half
    feats = fq_ref.shape[1]
    place, level = spot()
    u = lax.div(place, 2) ^ other
    kv_scr[:half, :] = last_ref[half:, :]
    kv_scr[half:, :] = own_ref[...]
    at = pl.ds(pl.multiple_of(u * half, half), 2 * half)
    keys, values = kv_scr[at, :dh], kv_scr[at, dh:]
    fk_at = pl.ds(pl.multiple_of((u + 1) * half, half), 2 * half)
    known = (level > 0) | (u > 0)
    cut = half - WINDOW
    row = lax.broadcasted_iota(jnp.int32, (WINDOW, 2 * half), 0)
    col = lax.broadcasted_iota(jnp.int32, (WINDOW, 2 * half), 1)
    inside = (col > row + cut) & (col <= row + half) & ((col >= half) | known)
    causal = (col <= row + cut)[:, :half]
    row, col = row[:, :half], col[:, :half]
    inside_low = (col > row) & (col <= row + WINDOW)
    causal_low = col <= row
    scores = dot_t(q_ref[...], keys)
    scale = math.log2(math.e) / math.sqrt(dh)

    def window(part, kept):
        masked = jnp.where(kept, part, -jnp.inf)
        top = jnp.max(masked, axis=1, keepdims=True)
        return jnp.exp2(((masked - top) * scale).astype(BF16))

    for h in range(heads):
        here = slice(h * half, (h + 1) * half)
        up, low = slice(h * half, h * half + cut), slice(h * half + cut, (h + 1) * half)
        linear = jnp.dot(
            fq_ref[here, :],
            fk_ref[h * feats : (h + 1) * feats, fk_at],
            preferred_element_type=F32,
        )
        soft = window(scores[up], inside)
        w_scr[up, :half] = soft[:, :half] + jnp.where(causal, linear[:cut, :half], 0.0).astype(BF16)
        w_scr[up, half:] = soft[:, half:]
        soft = window(scores[low, half:], inside_low)
        w_scr[low, :half] = linear[cut:, :half].astype(BF16)
        w_scr[low, half:] = soft + jnp.where(causal_low, linear[cut:, half:], 0.0).astype(BF16)
    values = jnp.concatenate(
        [with_ones(values[:half], known), with_ones(values[half:])], axis=0
    )
    near_ref[...] = jnp.dot(w_scr[...], values, preferred_element_type=F32)


def mix_kernel_of_level(*refs):
    near_refs, fq_refs, (past_ref, step_ref, wk_ref) = refs[:2], refs[2:4], refs[4:7]
    first_ref, refs = refs[7], refs[8:]
    out_refs, (fk_scr, state_scr, out_scr) = refs[:-3], refs[-3:]
    rows, dh = near_refs[0].shape[0], near_refs[0].shape[1] // 2
    feats = fq_refs[0].shape[1]
    heads = past_ref.shape[0] // feats
    half = rows // heads
    place, level = spot()
    side = lax.axis_index("head")
    u = lax.div(place, 2)

    @pl.when(level < 3)
    def _():
        state_scr[0] = past_ref[...].astype(BF16)
        state_scr[1] = (past_ref[...] + step_ref[...]).astype(BF16)

    @pl.when(level >= 3)
    def _():
        write_key_features(first_ref[:, :dh], wk_ref, fk_scr)
        state = past_ref[...] + jnp.dot(
            fk_scr[...], with_ones(first_ref[:, dh:]), preferred_element_type=F32
        )
        state_scr[0] = state.astype(BF16)
        state_scr[1] = (state + step_ref[...]).astype(BF16)

    part = out_refs[0].shape[0]
    for other in (1, 0):
        for h in range(heads):
            here = slice(h * half, (h + 1) * half)
            far = jnp.dot(
                fq_refs[other][here, :],
                state_scr[u ^ other, h * feats : (h + 1) * feats, :],
                preferred_element_type=F32,
            )
            both = near_refs[other][here, :] + far
            out_scr[aligned(u ^ other, half), h * dh : (h + 1) * dh] = (
                both[:, :dh] * pl.reciprocal(both[:, dh:], approx=True)
            ).astype(BF16)
    for n, ref in enumerate(out_refs):
        dr, dy = slot_of(n, lax.rem(place, 2))
        ref[...] = out_scr[aligned((place ^ dr) * 2 + (side ^ dy), part), :]


def whole_spec(space=pltpu.VMEM):
    return pl.BlockSpec(memory_space=space)


def call(kernel, ins, outs, name, scratch=(), limit=4, out_type=BF16, aliases={}):
    return pl.pallas_call(
        kernel,
        in_specs=[whole_spec() for _ in ins],
        out_specs=[whole_spec() for _ in outs],
        out_shape=[
            jax.ShapeDtypeStruct(s, out_type[n] if isinstance(out_type, list) else out_type)
            for n, s in enumerate(outs)
        ],
        scratch_shapes=list(scratch),
        input_output_aliases=aliases,
        cost_estimate=EARLY if name in EARLY_KERNELS else None,
        compiler_params=pltpu.CompilerParams(vmem_limit_bytes=limit * 2**20),
        name=name,
    )(*ins)


def by_levels(queries, keys, values, wq, wk, factor):
    tok, width = queries.shape
    local_heads, feat, dh = wq.shape
    heads = local_heads // WAYS
    seq, sides = lax.axis_size("seq"), lax.axis_size("head")
    half = 2 * tok
    rows, states = heads * half, heads * 2 * feat

    def partner(x, dr, dy=0):
        pairs = [
            (i * sides + j, (i // WAYS * WAYS + (i % WAYS ^ dr)) * sides + (j ^ dy))
            for i in range(seq)
            for j in range(sides)
        ]
        return lax.ppermute(x, ("seq", "head"), pairs)

    def levels_back(x, by):
        pairs = [(i, i + by * WAYS) for i in range(seq - by * WAYS)]
        return lax.ppermute(x, "seq", pairs)

    place = lax.rem(lax.axis_index("seq"), WAYS)
    ours = place // 2 * 2 * dh
    cuts = [
        lax.dynamic_slice_in_dim(x, at, 2 * dh, 1)
        for at in (ours, 2 * dh - ours)
        for x in (keys, values)
    ]
    own, away = call(pack_kv_kernel, cuts, [(tok, 4 * dh)] * 2, "pack_kv")
    got = partner(away, 2)
    queries, away = lax.optimization_barrier((queries, away))
    q = list(call(pack_q_kernel, [queries], [(tok, width // WAYS)] * WAYS, "pack_q"))
    q[2], q[3] = partner(q[2], 2), partner(q[3], 3)
    (pair,) = call(pair_kernel, [own, got], [(half, 2 * dh)], "pair_kv")
    pair, q[1], wq, wk = lax.optimization_barrier((pair, q[1], wq, wk))
    pair, q[1] = partner(pair, 1), partner(q[1], 1)
    wq, wk = [lax.dynamic_slice_in_dim(w, place * heads, heads) for w in (wq, wk)]
    pair, wq, wk = lax.optimization_barrier((pair, wq, wk))
    (kv,) = call(stack_kernel, [own, got, pair], [(2 * half, 2 * dh)], "stack_kv")
    last, before = levels_back(kv, 1), levels_back(kv, 2)
    wq, kv, q[1] = lax.optimization_barrier((wq, kv, q[1]))
    (fk,) = call(own_features_kernel, [kv, wk], [(states, 4 * half)], "own_features", limit=16)
    wq, ratio = call(
        weights_kernel,
        [wq, factor.reshape(1, local_heads)],
        [(heads, dh, 2 * feat), (heads, 2 * feat)],
        "weights",
        out_type=[BF16, F32],
    )
    far_kv, fk, wq = lax.optimization_barrier((kv, fk, wq))
    first = levels_back(far_kv, 3)

    def query_features(a, b):
        return call(
            query_features_kernel,
            [a, b, wq, ratio],
            [(rows, dh), (rows, 2 * feat)],
            "query_features",
            [pltpu.VMEM((rows, 2 * feat), BF16)],
            12,
        )

    def near(other, q_rows, fq):
        return call(
            lambda *refs: near_kernel(other, *refs),
            [q_rows, fq, last, kv, fk],
            [(rows, 2 * dh)],
            "near",
            [
                pltpu.VMEM((3 * half, 2 * dh), BF16),
                pltpu.VMEM((rows, 2 * half), BF16),
            ],
            16,
            F32,
        )[0]

    q_own, fq_own = query_features(q[0], q[1])
    last, fq_own, fk = lax.optimization_barrier((last, fq_own, fk))
    fk, past, step = call(
        last_features_kernel,
        [last, wk, fk],
        [(states, 4 * half), (states, 2 * dh), (states, 2 * dh)],
        "last_features",
        limit=20,
        out_type=[BF16, F32, F32],
        aliases={2: 0},
    )
    near_own = near(0, q_own, fq_own)
    q[2], q[3], near_own = lax.optimization_barrier((q[2], q[3], near_own))
    q_other, fq_other = query_features(q[2], q[3])
    near_other = near(1, q_other, fq_other)
    before, near_other = lax.optimization_barrier((before, near_other))
    (past,) = call(
        past_kernel,
        [before, wk, past],
        [(states, 2 * dh)],
        "past",
        [pltpu.VMEM((states, 2 * half), BF16)],
        16,
        F32,
    )
    first, past = lax.optimization_barrier((first, past))
    part = tok // sides
    outs = call(
        mix_kernel_of_level,
        [near_own, near_other, fq_own, fq_other, past, step, wk, first],
        [(part, heads * dh)] * (WAYS * sides),
        "mix_level",
        [
            pltpu.VMEM((states, 2 * half), BF16),
            pltpu.VMEM((2, states, 2 * dh), BF16),
            pltpu.VMEM((2 * half, heads * dh), BF16),
        ],
        24,
    )

    def sent(x, slot):
        pairs = []
        for i in range(seq):
            dr, dy = slot[i % 2]
            to = i // WAYS * WAYS + (i % WAYS ^ dr)
            pairs += [(i * sides + j, to * sides + (j ^ dy)) for j in range(sides)]
        return lax.ppermute(x, ("seq", "head"), pairs)

    outs = list(outs)
    for n in range(1, 6):
        outs[n] = sent(outs[n], SLOTS[n])
    for n, ahead in ((6, 2), (7, 1)):
        outs[n], outs[ahead] = lax.optimization_barrier((outs[n], outs[ahead]))
        outs[n] = sent(outs[n], SLOTS[n])

    def joined(slots, into):
        return pl.pallas_call(
            lambda *refs: join_kernel(slots, *refs),
            in_specs=[whole_spec()] * len(slots) + [whole_spec(pltpu.HBM)] * len(into),
            out_specs=whole_spec(pltpu.HBM),
            out_shape=jax.ShapeDtypeStruct((part, sides * WAYS * heads * dh), BF16),
            input_output_aliases={len(slots): 0} if into else {},
            scratch_shapes=[pltpu.SemaphoreType.DMA((len(slots),))],
            compiler_params=pltpu.CompilerParams(vmem_limit_bytes=4 * 2**20),
            name="join",
        )(*[outs[n] for n in slots], *into)

    return joined((4, 5, 6, 7), [joined((0, 1, 2, 3), [])])


def by_blocks(queries, keys, values, wq, wk, ratio):
    group = wq.shape[0] // (keys.shape[1] // DH)
    place = lax.axis_index("seq").astype(jnp.int32).reshape(1)
    kv = lax.all_gather(jnp.concatenate([keys, values], axis=1), "seq", tiled=True)
    out = mix(place, queries, kv, wq, wk, ratio, group)
    return lax.all_to_all(out, "head", split_axis=0, concat_axis=1, tiled=True)


def local(queries, keys, values, q_feature, k_feature, window_factor):
    tok = queries.shape[0]
    seq, sides = lax.axis_size("seq"), lax.axis_size("head")
    wq, wk = jnp.swapaxes(q_feature, 1, 2), jnp.swapaxes(k_feature, 1, 2)
    if keys.shape[1] == WAYS * DH and seq == 4 * WAYS and sides == 2 and tok == WINDOW:
        return by_levels(queries, keys, values, wq, wk, window_factor)
    ratio = window_factor / (1.0 - window_factor)
    return by_blocks(queries, keys, values, wq, wk, ratio)


def solution(mesh):
    return jax.shard_map(
        local,
        mesh=mesh,
        in_specs=(
            P("seq", "head"),
            P("seq", "head"),
            P("seq", "head"),
            P("head", None, None),
            P("head", None, None),
            P("head"),
        ),
        out_specs=P(("seq", "head"), None),
        check_vma=False,
    )
```

profile of v0, /device:TPU:27, one launch (start us, length us, event | category | flops | bytes accessed | tf_op | source)
XLA Modules:
  0.0 41.7 jit_solution(13706650520467589139)
XLA Ops:
  0.0 0.9 %constant_dynamic-slice_fusion.2 = (bf16[64,256]{1,0:T(8,128)(2,1)S(1)}, bf16[64,256]{1,0:T(8,128)(2,1)S(1)}, bf16[64,256]{1,0:T(8,128)(2,1)S(1)}, bf16[64,256]{1,0:T(8,128)(2,1)S(1)}) fusion(bf16[64,512]{1,0:T(8,128)(2,1)} %param.8, s32[]{:T(128)S(6)} %select_n.19, s32[]{:T(128)S(6)} %select_n.18, bf16[64,512]{1,0:T(8,128)(2,1)} %param.7), kind=kLoop, calls=%fused_computation.2 | loop fusion | bytes 262152 | tf_op jit(solution)/shard_map/dynamic_slice | solution.py:440
  1.0 0.3 collective-permute-start.2
  1.3 0.8 %copy-done.2 = bf16[64,8192]{1,0:T(8,128)(2,1)S(1)} copy-done((bf16[64,8192]{1,0:T(8,128)(2,1)S(1)}, bf16[64,8192]{1,0:T(8,128)(2,1)}, u32[]{:S(2)}) %copy-start.2) | copy-done | bytes 1048600
  2.2 0.4 %collective-permute-start = (bf16[64,2048]{1,0:T(8,128)(2,1)S(1)}, bf16[64,2048]{1,0:T(8,128)(2,1)S(1)}, u32[]{:S(2)}, u32[]{:S(2)}) collective-permute-start(bf16[64,2048]{1,0:T(8,128)(2,1)S(1)} %get-tuple-element.58), channel_id=1, source_target_pairs={{0,4},{1,5},{2,6},{3,7},{4,0},{5,1},{6,2},{7,3},{8,12},{9,13},{10,... | collective-permute-start | bytes 786440 | tf_op jit(solution)/shard_map/ppermute | solution.py:431
  2.6 1.9 %collective-permute-start.1 = (bf16[64,2048]{1,0:T(8,128)(2,1)S(1)}, bf16[64,2048]{1,0:T(8,128)(2,1)S(1)}, u32[]{:S(2)}, u32[]{:S(2)}) collective-permute-start(bf16[64,2048]{1,0:T(8,128)(2,1)S(1)} %get-tuple-element.59), channel_id=1, source_target_pairs={{0,6},{1,7},{2,4},{3,5},{4,2},{5,3},{6,0},{7,1},{8,14},{9,15},{10,... | collective-permute-start | bytes 786440 | tf_op jit(solution)/shard_map/ppermute | solution.py:431
  4.6 2.0 %collective-permute-start.3 = (bf16[128,256]{1,0:T(8,128)(2,1)S(1)}, bf16[128,256]{1,0:T(8,128)(2,1)S(1)}, u32[]{:S(2)}, u32[]{:S(2)}) collective-permute-start(bf16[128,256]{1,0:T(8,128)(2,1)S(1)} %pair_kv.1), channel_id=1, source_target_pairs={{0,2},{1,3},{2,0},{3,1},{4,6},{5,7},{6,4},{7,5},{8,10},{9,11},{10,... | collective-permute-start | bytes 196616 | tf_op jit(solution)/shard_map/ppermute | solution.py:431
  6.8 1.0 %constant_dynamic-slice_fusion.1.wq_ref = bf16[16,64,128]{2,1,0:T(8,128)(2,1)S(1)} fusion(bf16[64,64,128]{2,1,0:T(8,128)(2,1)} %bitcast.5, s32[]{:T(128)S(6)} %select_n.20), kind=kLoop, calls=%fused_computation.1 | loop fusion | bytes 524292 | tf_op jit(solution)/shard_map/dynamic_slice | solution.py:452
  7.8 1.3 %collective-permute-start.5 = (bf16[256,256]{1,0:T(8,128)(2,1)S(1)}, bf16[256,256]{1,0:T(8,128)(2,1)S(1)}, u32[]{:S(2)}, u32[]{:S(2)}) collective-permute-start(bf16[256,256]{1,0:T(8,128)(2,1)S(1)} %stack_kv.1.own_ref.refs_3_), channel_id=1, source_target_pairs={{0,8},{2,10},{4,12},{6,14},{8,16},{10,18},{12,20},{14,22},{16,24},... | collective-permute-start | bytes 393224 | tf_op jit(solution)/shard_map/ppermute | solution.py:435
  9.1 1.3 %collective-permute-start.6 = (bf16[256,256]{1,0:T(8,128)(2,1)S(1)}, bf16[256,256]{1,0:T(8,128)(2,1)S(1)}, u32[]{:S(2)}, u32[]{:S(2)}) collective-permute-start(bf16[256,256]{1,0:T(8,128)(2,1)S(1)} %stack_kv.1.own_ref.refs_3_), channel_id=1, source_target_pairs={{0,16},{2,18},{4,20},{6,22},{8,24},{10,26},{12,28},{14,30},{1,17},... | collective-permute-start | bytes 393224 | tf_op jit(solution)/shard_map/ppermute | solution.py:435
  10.4 0.7 %own_features.1._ = bf16[2048,512]{1,0:T(8,128)(2,1)S(1)} custom-call(bf16[256,256]{1,0:T(8,128)(2,1)S(1)} %stack_kv.1.own_ref.refs_3_, bf16[16,64,128]{2,1,0:T(8,128)(2,1)S(1)} %constant_dynamic-slice_fusion.wk_ref.refs_6_), custom_call_target="tpu_custom_call" | custom-call | tf_op jit(solution)/shard_map/own_features/pallas_call | solution.py:401
  11.1 0.4 weights.1
  11.5 1.3 %collective-permute-start.7 = (bf16[256,256]{1,0:T(8,128)(2,1)S(1)}, bf16[256,256]{1,0:T(8,128)(2,1)S(1)}, u32[]{:S(2)}, u32[]{:S(2)}) collective-permute-start(bf16[256,256]{1,0:T(8,128)(2,1)S(1)} %stack_kv.1.own_ref.refs_3_), channel_id=1, source_target_pairs={{0,24},{2,26},{4,28},{6,30},{1,25},{3,27},{5,29},{7,31}} | collective-permute-start | bytes 393224 | tf_op jit(solution)/shard_map/ppermute | solution.py:435
  12.8 1.1 %query_features.2 = (bf16[2048,128]{1,0:T(8,128)(2,1)S(1)}, bf16[2048,128]{1,0:T(8,128)(2,1)S(1)}) custom-call(bf16[64,2048]{1,0:T(8,128)(2,1)S(1)} %get-tuple-element.60.a_ref, bf16[64,2048]{1,0:T(8,128)(2,1)S(1)} %collective-permute-done.4.b_ref, bf16[16,128,128]{2,1,0:T(8,128)(2,1)S(1)} %get-tuple-element.74.w_ref, f32[16,128]{1,0:T(8,128)S(1)} %get-tuple-element.75.ratio_ref), custom_call_target="tpu_custom_call" | custom-call | tf_op jit(solution)/shard_map/query_features/pallas_call | solution.py:401
  13.9 0.4 collective-permute-done.5.last_ref.refs_2_
  14.3 1.3 %last_features.1 = (bf16[2048,512]{1,0:T(8,128)(2,1)S(1)}, f32[2048,256]{1,0:T(8,128)S(1)}, f32[2048,256]{1,0:T(8,128)S(1)}) custom-call(bf16[256,256]{1,0:T(8,128)(2,1)S(1)} %collective-permute-done.5.last_ref.refs_2_, bf16[16,64,128]{2,1,0:T(8,128)(2,1)S(1)} %constant_dynamic-slice_fusion.wk_ref.refs_6_, ...), custom_call_target="tpu_custom_call", output_to_operand_aliasing={{0}: (2, {})} | custom-call | tf_op jit(solution)/shard_map/last_features/pallas_call | solution.py:401
  15.6 1.1 %near.2.refs_0_ = f32[2048,256]{1,0:T(8,128)S(1)} custom-call(bf16[2048,128]{1,0:T(8,128)(2,1)S(1)} %get-tuple-element.76.refs_0_, bf16[2048,128]{1,0:T(8,128)(2,1)S(1)} %get-tuple-element.79.refs_1_.refs_2_, bf16[256,256]{1,0:T(8,128)(2,1)S(1)} %collective-permute-done.5.last_ref.refs_2_, bf16[256,256]{1,0:T(8,128)(2,1)S(1)} %stack_kv.1.own_ref.refs_3_, ...), custom_call_target="tpu_custom_call" | custom-call | tf_op jit(solution)/shard_map/near/pallas_call | solution.py:401
  16.8 1.1 %query_features.3 = (bf16[2048,128]{1,0:T(8,128)(2,1)S(1)}, bf16[2048,128]{1,0:T(8,128)(2,1)S(1)}) custom-call(bf16[64,2048]{1,0:T(8,128)(2,1)S(1)} %collective-permute-done.a_ref, bf16[64,2048]{1,0:T(8,128)(2,1)S(1)} %collective-permute-done.1.b_ref, bf16[16,128,128]{2,1,0:T(8,128)(2,1)S(1)} %get-tuple-element.74.w_ref, ...), custom_call_target="tpu_custom_call" | custom-call | tf_op jit(solution)/shard_map/query_features/pallas_call | solution.py:401
  18.0 1.1 %near.3.refs_1_ = f32[2048,256]{1,0:T(8,128)S(1)} custom-call(bf16[2048,128]{1,0:T(8,128)(2,1)S(1)} %get-tuple-element.86.refs_0_, bf16[2048,128]{1,0:T(8,128)(2,1)S(1)} %get-tuple-element.87.refs_1_.refs_3_, bf16[256,256]{1,0:T(8,128)(2,1)S(1)} %collective-permute-done.5.last_ref.refs_2_, bf16[256,256]{1,0:T(8,128)(2,1)S(1)} %stack_kv.1.own_ref.refs_3_, ...), custom_call_target="tpu_custom_call" | custom-call | tf_op jit(solution)/shard_map/near/pallas_call | solution.py:401
  19.0 4.0 %collective-permute-done.6.before_ref = bf16[256,256]{1,0:T(8,128)(2,1)S(1)} collective-permute-done((bf16[256,256]{1,0:T(8,128)(2,1)S(1)}, bf16[256,256]{1,0:T(8,128)(2,1)S(1)}, u32[]{:S(2)}, u32[]{:S(2)}) %collective-permute-start.6) | collective-permute-done | bytes 131104 | tf_op jit(solution)/shard_map/ppermute | solution.py:435
  23.1 1.0 %past.1.refs_4_ = f32[2048,256]{1,0:T(8,128)S(1)} custom-call(bf16[256,256]{1,0:T(8,128)(2,1)S(1)} %collective-permute-done.6.before_ref, bf16[16,64,128]{2,1,0:T(8,128)(2,1)S(1)} %constant_dynamic-slice_fusion.wk_ref.refs_6_, f32[2048,256]{1,0:T(8,128)S(1)} %get-tuple-element.91.sum_ref), custom_call_target="tpu_custom_call" | custom-call | tf_op jit(solution)/shard_map/past/pallas_call | solution.py:401
  24.1 1.8 %mix_level.1 = (bf16[32,2048]{1,0:T(8,128)(2,1)S(1)}, bf16[32,2048]{1,0:T(8,128)(2,1)S(1)}, bf16[32,2048]{1,0:T(8,128)(2,1)S(1)}, bf16[32,2048]{1,0:T(8,128)(2,1...) custom-call(f32[2048,256]{1,0:T(8,128)S(1)} %near.2.refs_0_, ...), custom_call_target="tpu_custom_call" | custom-call | tf_op jit(solution)/shard_map/mix_level/pallas_call | solution.py:401
  25.9 1.3 %collective-permute-start.12 = (bf16[32,2048]{1,0:T(8,128)(2,1)S(1)}, bf16[32,2048]{1,0:T(8,128)(2,1)S(1)}, u32[]{:S(2)}, u32[]{:S(2)}) collective-permute-start(bf16[32,2048]{1,0:T(8,128)(2,1)S(1)} %get-tuple-element.101), channel_id=1, source_target_pairs={{0,4},{1,5},{2,3},{3,2},{4,0},{5,1},{6,7},{7,6},{8,12},{9,13},{10,... | collective-permute-start | bytes 393224 | tf_op jit(solution)/shard_map/ppermute | solution.py:538
  27.3 1.5 %collective-permute-start.14 = (bf16[32,2048]{1,0:T(8,128)(2,1)S(1)}, bf16[32,2048]{1,0:T(8,128)(2,1)S(1)}, u32[]{:S(2)}, u32[]{:S(2)}) collective-permute-start(bf16[32,2048]{1,0:T(8,128)(2,1)S(1)} %get-tuple-element.106), channel_id=1, source_target_pairs={{0,6},{1,7},{2,1},{3,0},{4,2},{5,3},{6,5},{7,4},{8,14},{9,15},{10,... | collective-permute-start | bytes 393224 | tf_op jit(solution)/shard_map/ppermute | solution.py:538
  28.9 1.1 %collective-permute-start.8 = (bf16[32,2048]{1,0:T(8,128)(2,1)S(1)}, bf16[32,2048]{1,0:T(8,128)(2,1)S(1)}, u32[]{:S(2)}, u32[]{:S(2)}) collective-permute-start(bf16[32,2048]{1,0:T(8,128)(2,1)S(1)} %get-tuple-element.95), channel_id=1, source_target_pairs={{0,3},{1,2},{2,4},{3,5},{4,7},{5,6},{6,0},{7,1},{8,11},{9,10},{10,... | collective-permute-start | bytes 393224 | tf_op jit(solution)/shard_map/ppermute | solution.py:538
  30.0 1.2 %collective-permute-start.9 = (bf16[32,2048]{1,0:T(8,128)(2,1)S(1)}, bf16[32,2048]{1,0:T(8,128)(2,1)S(1)}, u32[]{:S(2)}, u32[]{:S(2)}) collective-permute-start(bf16[32,2048]{1,0:T(8,128)(2,1)S(1)} %get-tuple-element.96), channel_id=1, source_target_pairs={{0,5},{1,4},{2,7},{3,6},{4,1},{5,0},{6,3},{7,2},{8,13},{9,12},{10,... | collective-permute-start | bytes 393224 | tf_op jit(solution)/shard_map/ppermute | solution.py:538
  31.1 1.5 %collective-permute-done.10.refs_2_ = bf16[32,2048]{1,0:T(8,128)(2,1)S(1)} collective-permute-done((bf16[32,2048]{1,0:T(8,128)(2,1)S(1)}, bf16[32,2048]{1,0:T(8,128)(2,1)S(1)}, u32[]{:S(2)}, u32[]{:S(2)}) %collective-permute-start.10) | collective-permute-done | bytes 131104 | tf_op jit(solution)/shard_map/ppermute | solution.py:538
  32.7 0.5 %collective-permute-start.13 = (bf16[32,2048]{1,0:T(8,128)(2,1)S(1)}, bf16[32,2048]{1,0:T(8,128)(2,1)S(1)}, u32[]{:S(2)}, u32[]{:S(2)}) collective-permute-start(bf16[32,2048]{1,0:T(8,128)(2,1)S(1)} %get-tuple-element.102), channel_id=1, source_target_pairs={{0,2},{1,3},{2,0},{3,1},{4,6},{5,7},{6,4},{7,5},{8,10},{9,11},{10,... | collective-permute-start | bytes 393224 | tf_op jit(solution)/shard_map/ppermute | solution.py:538
  33.2 2.5 %collective-permute-start.11 = (bf16[32,2048]{1,0:T(8,128)(2,1)S(1)}, bf16[32,2048]{1,0:T(8,128)(2,1)S(1)}, u32[]{:S(2)}, u32[]{:S(2)}) collective-permute-start(bf16[32,2048]{1,0:T(8,128)(2,1)S(1)} %get-tuple-element.99), channel_id=1, source_target_pairs={{0,7},{1,6},{2,5},{3,4},{4,3},{5,2},{6,1},{7,0},{8,15},{9,14},{10,... | collective-permute-start | bytes 393224 | tf_op jit(solution)/shard_map/ppermute | solution.py:538
  35.7 0.8 %join.2.refs_4_ = bf16[32,16384]{1,0:T(8,128)(2,1)} custom-call(bf16[32,2048]{1,0:T(8,128)(2,1)S(1)} %get-tuple-element.103.refs_0_, bf16[32,2048]{1,0:T(8,128)(2,1)S(1)} %collective-permute-done.12.refs_1_, bf16[32,2048]{1,0:T(8,128)(2,1)S(1)} %collective-permute-done.10.refs_2_, bf16[32,2048]{1,0:T(8,128)(2,1)S(1)} %collective-permute-done.14.refs_3_), custom_call_target="tpu_custom_call" | custom-call | tf_op jit(solution)/shard_map/join/pallas_call | solution.py:548
  36.5 1.5 %collective-permute-done.9.refs_1_ = bf16[32,2048]{1,0:T(8,128)(2,1)S(1)} collective-permute-done((bf16[32,2048]{1,0:T(8,128)(2,1)S(1)}, bf16[32,2048]{1,0:T(8,128)(2,1)S(1)}, u32[]{:S(2)}, u32[]{:S(2)}) %collective-permute-start.9) | collective-permute-done | bytes 131104 | tf_op jit(solution)/shard_map/ppermute | solution.py:538
  38.1 2.8 %collective-permute-done.11.refs_2_ = bf16[32,2048]{1,0:T(8,128)(2,1)S(1)} collective-permute-done((bf16[32,2048]{1,0:T(8,128)(2,1)S(1)}, bf16[32,2048]{1,0:T(8,128)(2,1)S(1)}, u32[]{:S(2)}, u32[]{:S(2)}) %collective-permute-start.11) | collective-permute-done | bytes 131104 | tf_op jit(solution)/shard_map/ppermute | solution.py:538
  40.9 0.8 %join.3 = bf16[32,16384]{1,0:T(8,128)(2,1)} custom-call(bf16[32,2048]{1,0:T(8,128)(2,1)S(1)} %collective-permute-done.8.refs_0_, bf16[32,2048]{1,0:T(8,128)(2,1)S(1)} %collective-permute-done.9.refs_1_, bf16[32,2048]{1,0:T(8,128)(2,1)S(1)} %collective-permute-done.11.refs_2_, ...), custom_call_target="tpu_custom_call", output_to_operand_aliasing={{}: (4, {})} | custom-call | tf_op jit(solution)/shard_map/join/pallas_call | solution.py:548
  (22 shorter events, 0.5 us)
Async XLA Ops:
  0.0 4.6 %copy-start = (bf16[64,128,64]{1,2,0:T(8,128)(2,1)S(1)}, bf16[64,128,64]{1,2,0:T(8,128)(2,1)}, u32[]{:S(2)}) copy-start(bf16[64,128,64]{1,2,0:T(8,128)(2,1)} %param.10) | copy-start | bytes 3145732
  0.9 1.2 %copy-start.2 = (bf16[64,8192]{1,0:T(8,128)(2,1)S(1)}, bf16[64,8192]{1,0:T(8,128)(2,1)}, u32[]{:S(2)}) copy-start(bf16[64,8192]{1,0:T(8,128)(2,1)} %q_ref) | copy-start | bytes 3145732
  1.0 3.6 %collective-permute-start.2 = (bf16[64,512]{1,0:T(8,128)(2,1)S(1)}, bf16[64,512]{1,0:T(8,128)(2,1)S(1)}, u32[]{:S(2)}, u32[]{:S(2)}) collective-permute-start(bf16[64,512]{1,0:T(8,128)(2,1)S(1)} %get-tuple-element.56), channel_id=1, source_target_pairs={{0,4},{1,5},{2,6},{3,7},{4,0},{5,1},{6,2},{7,3},{8,12},{9,13},{10,... | collective-permute-start | bytes 196616 | tf_op jit(solution)/shard_map/ppermute | solution.py:431
  2.2 14.5 %collective-permute-start = (bf16[64,2048]{1,0:T(8,128)(2,1)S(1)}, bf16[64,2048]{1,0:T(8,128)(2,1)S(1)}, u32[]{:S(2)}, u32[]{:S(2)}) collective-permute-start(bf16[64,2048]{1,0:T(8,128)(2,1)S(1)} %get-tuple-element.58), channel_id=1, source_target_pairs={{0,4},{1,5},{2,6},{3,7},{4,0},{5,1},{6,2},{7,3},{8,12},{9,13},{10,... | collective-permute-start | bytes 786440 | tf_op jit(solution)/shard_map/ppermute | solution.py:431
  2.6 14.2 %collective-permute-start.1 = (bf16[64,2048]{1,0:T(8,128)(2,1)S(1)}, bf16[64,2048]{1,0:T(8,128)(2,1)S(1)}, u32[]{:S(2)}, u32[]{:S(2)}) collective-permute-start(bf16[64,2048]{1,0:T(8,128)(2,1)S(1)} %get-tuple-element.59), channel_id=1, source_target_pairs={{0,6},{1,7},{2,4},{3,5},{4,2},{5,3},{6,0},{7,1},{8,14},{9,15},{10,... | collective-permute-start | bytes 786440 | tf_op jit(solution)/shard_map/ppermute | solution.py:431
  4.6 3.1 %collective-permute-start.3 = (bf16[128,256]{1,0:T(8,128)(2,1)S(1)}, bf16[128,256]{1,0:T(8,128)(2,1)S(1)}, u32[]{:S(2)}, u32[]{:S(2)}) collective-permute-start(bf16[128,256]{1,0:T(8,128)(2,1)S(1)} %pair_kv.1), channel_id=1, source_target_pairs={{0,2},{1,3},{2,0},{3,1},{4,6},{5,7},{6,4},{7,5},{8,10},{9,11},{10,... | collective-permute-start | bytes 196616 | tf_op jit(solution)/shard_map/ppermute | solution.py:431
  6.7 3.7 %collective-permute-start.4 = (bf16[64,2048]{1,0:T(8,128)(2,1)S(1)}, bf16[64,2048]{1,0:T(8,128)(2,1)S(1)}, u32[]{:S(2)}, u32[]{:S(2)}) collective-permute-start(bf16[64,2048]{1,0:T(8,128)(2,1)S(1)} %get-tuple-element.68), channel_id=1, source_target_pairs={{0,2},{1,3},{2,0},{3,1},{4,6},{5,7},{6,4},{7,5},{8,10},{9,11},{10,... | collective-permute-start | bytes 786440 | tf_op jit(solution)/shard_map/ppermute | solution.py:431
  7.8 3.3 %copy-start.1 = (f32[64]{0:T(128)S(1)}, f32[64]{0:T(128)}, u32[]{:S(2)}) copy-start(f32[64]{0:T(128)} %param.11) | copy-start | bytes 772
  7.8 6.5 %collective-permute-start.5 = (bf16[256,256]{1,0:T(8,128)(2,1)S(1)}, bf16[256,256]{1,0:T(8,128)(2,1)S(1)}, u32[]{:S(2)}, u32[]{:S(2)}) collective-permute-start(bf16[256,256]{1,0:T(8,128)(2,1)S(1)} %stack_kv.1.own_ref.refs_3_), channel_id=1, source_target_pairs={{0,8},{2,10},{4,12},{6,14},{8,16},{10,18},{12,20},{14,22},{16,24},... | collective-permute-start | bytes 393224 | tf_op jit(solution)/shard_map/ppermute | solution.py:435
  9.1 14.0 %collective-permute-start.6 = (bf16[256,256]{1,0:T(8,128)(2,1)S(1)}, bf16[256,256]{1,0:T(8,128)(2,1)S(1)}, u32[]{:S(2)}, u32[]{:S(2)}) collective-permute-start(bf16[256,256]{1,0:T(8,128)(2,1)S(1)} %stack_kv.1.own_ref.refs_3_), channel_id=1, source_target_pairs={{0,16},{2,18},{4,20},{6,22},{8,24},{10,26},{12,28},{14,30},{1,17},... | collective-permute-start | bytes 393224 | tf_op jit(solution)/shard_map/ppermute | solution.py:435
  11.5 12.6 %collective-permute-start.7 = (bf16[256,256]{1,0:T(8,128)(2,1)S(1)}, bf16[256,256]{1,0:T(8,128)(2,1)S(1)}, u32[]{:S(2)}, u32[]{:S(2)}) collective-permute-start(bf16[256,256]{1,0:T(8,128)(2,1)S(1)} %stack_kv.1.own_ref.refs_3_), channel_id=1, source_target_pairs={{0,24},{2,26},{4,28},{6,30},{1,25},{3,27},{5,29},{7,31}} | collective-permute-start | bytes 393224 | tf_op jit(solution)/shard_map/ppermute | solution.py:435
  25.9 5.2 %collective-permute-start.12 = (bf16[32,2048]{1,0:T(8,128)(2,1)S(1)}, bf16[32,2048]{1,0:T(8,128)(2,1)S(1)}, u32[]{:S(2)}, u32[]{:S(2)}) collective-permute-start(bf16[32,2048]{1,0:T(8,128)(2,1)S(1)} %get-tuple-element.101), channel_id=1, source_target_pairs={{0,4},{1,5},{2,3},{3,2},{4,0},{5,1},{6,7},{7,6},{8,12},{9,13},{10,... | collective-permute-start | bytes 393224 | tf_op jit(solution)/shard_map/ppermute | solution.py:538
  27.2 5.5 %collective-permute-start.10 = (bf16[32,2048]{1,0:T(8,128)(2,1)S(1)}, bf16[32,2048]{1,0:T(8,128)(2,1)S(1)}, u32[]{:S(2)}, u32[]{:S(2)}) collective-permute-start(bf16[32,2048]{1,0:T(8,128)(2,1)S(1)} %get-tuple-element.98), channel_id=1, source_target_pairs={{0,1},{1,0},{2,6},{3,7},{4,5},{5,4},{6,2},{7,3},{8,9},{9,8},{10,14... | collective-permute-start | bytes 393224 | tf_op jit(solution)/shard_map/ppermute | solution.py:538
  27.3 8.4 %collective-permute-start.14 = (bf16[32,2048]{1,0:T(8,128)(2,1)S(1)}, bf16[32,2048]{1,0:T(8,128)(2,1)S(1)}, u32[]{:S(2)}, u32[]{:S(2)}) collective-permute-start(bf16[32,2048]{1,0:T(8,128)(2,1)S(1)} %get-tuple-element.106), channel_id=1, source_target_pairs={{0,6},{1,7},{2,1},{3,0},{4,2},{5,3},{6,5},{7,4},{8,14},{9,15},{10,... | collective-permute-start | bytes 393224 | tf_op jit(solution)/shard_map/ppermute | solution.py:538
  28.9 7.7 %collective-permute-start.8 = (bf16[32,2048]{1,0:T(8,128)(2,1)S(1)}, bf16[32,2048]{1,0:T(8,128)(2,1)S(1)}, u32[]{:S(2)}, u32[]{:S(2)}) collective-permute-start(bf16[32,2048]{1,0:T(8,128)(2,1)S(1)} %get-tuple-element.95), channel_id=1, source_target_pairs={{0,3},{1,2},{2,4},{3,5},{4,7},{5,6},{6,0},{7,1},{8,11},{9,10},{10,... | collective-permute-start | bytes 393224 | tf_op jit(solution)/shard_map/ppermute | solution.py:538
  30.0 8.1 %collective-permute-start.9 = (bf16[32,2048]{1,0:T(8,128)(2,1)S(1)}, bf16[32,2048]{1,0:T(8,128)(2,1)S(1)}, u32[]{:S(2)}, u32[]{:S(2)}) collective-permute-start(bf16[32,2048]{1,0:T(8,128)(2,1)S(1)} %get-tuple-element.96), channel_id=1, source_target_pairs={{0,5},{1,4},{2,7},{3,6},{4,1},{5,0},{6,3},{7,2},{8,13},{9,12},{10,... | collective-permute-start | bytes 393224 | tf_op jit(solution)/shard_map/ppermute | solution.py:538
  32.7 5.4 %collective-permute-start.13 = (bf16[32,2048]{1,0:T(8,128)(2,1)S(1)}, bf16[32,2048]{1,0:T(8,128)(2,1)S(1)}, u32[]{:S(2)}, u32[]{:S(2)}) collective-permute-start(bf16[32,2048]{1,0:T(8,128)(2,1)S(1)} %get-tuple-element.102), channel_id=1, source_target_pairs={{0,2},{1,3},{2,0},{3,1},{4,6},{5,7},{6,4},{7,5},{8,10},{9,11},{10,... | collective-permute-start | bytes 393224 | tf_op jit(solution)/shard_map/ppermute | solution.py:538
  33.2 7.7 %collective-permute-start.11 = (bf16[32,2048]{1,0:T(8,128)(2,1)S(1)}, bf16[32,2048]{1,0:T(8,128)(2,1)S(1)}, u32[]{:S(2)}, u32[]{:S(2)}) collective-permute-start(bf16[32,2048]{1,0:T(8,128)(2,1)S(1)} %get-tuple-element.99), channel_id=1, source_target_pairs={{0,7},{1,6},{2,5},{3,4},{4,3},{5,2},{6,1},{7,0},{8,15},{9,14},{10,... | collective-permute-start | bytes 393224 | tf_op jit(solution)/shard_map/ppermute | solution.py:538
where the time goes:
time: 42.1 us; the launch traced here: 41.7 us
  starting transfers between devices  17 us (40%)
  Pallas kernels  11.4 us (27%)
  waiting for transfers between devices  10.4 us (25%)
  local copies, waits for them, and re-layouts  2.76 us (7%)
    pallas_call x13, Pallas kernels, call(): pl.pallas_call(kernel, in_specs=[whole_spec() for _ in ins], out_specs=[w...  9.75 us
    ppermute x7, starting transfers between devices, sent(): return lax.ppermute(x, ('seq', 'head'), pairs)  8.28 us
    ppermute x7, waiting for transfers between devices, sent(): return lax.ppermute(x, ('seq', 'head'), pairs)  5.85 us
    ppermute x5, starting transfers between devices, partner(): return lax.ppermute(x, ('seq', 'head'), pairs)  4.82 us
    ppermute x3, waiting for transfers between devices, levels_back(): return lax.ppermute(x, 'seq', pairs)  4.42 us
    ppermute x3, starting transfers between devices, levels_back(): return lax.ppermute(x, 'seq', pairs)  3.88 us
    pallas_call x2, Pallas kernels, joined(): pl.pallas_call(lambda *refs: join_kernel(slots, *refs), in_specs=[whole_s...  1.64 us
    dynamic_slice x2, local copies, waits for them, and re-layouts, by_levels(): lax.dynamic_slice_in_dim(w, place * heads, heads)  0.99 us
  transfers between devices with their start and end apart: 15, of which 6 were waited for; matrix products, arithmetic and copies ran while one was open for 2% of the time, Pallas kernels for 21%

commit v1 on v0

--- a/solution.py
+++ b/solution.py
@@ -134,11 +134,11 @@
     ((0, 0), (0, 0)),
     ((2, 0), (0, 1)),
     ((0, 1), (2, 0)),
+    ((1, 0), (1, 0)),
+    ((2, 1), (2, 1)),
     ((3, 0), (1, 1)),
+    ((3, 1), (3, 1)),
     ((1, 1), (3, 0)),
-    ((2, 1), (2, 1)),
-    ((3, 1), (3, 1)),
-    ((1, 0), (1, 0)),
 )
 
 
@@ -462,8 +462,6 @@
         "weights",
         out_type=[BF16, F32],
     )
-    far_kv, fk, wq = lax.optimization_barrier((kv, fk, wq))
-    first = levels_back(far_kv, 3)
 
     def query_features(a, b):
         return call(
@@ -490,6 +488,8 @@
         )[0]
 
     q_own, fq_own = query_features(q[0], q[1])
+    far_kv, fk, fq_own = lax.optimization_barrier((kv, fk, fq_own))
+    first = levels_back(far_kv, 3)
     last, fq_own, fk = lax.optimization_barrier((last, fq_own, fk))
     fk, past, step = call(
         last_features_kernel,
@@ -540,9 +540,8 @@
     outs = list(outs)
     for n in range(1, 6):
         outs[n] = sent(outs[n], SLOTS[n])
-    for n, ahead in ((6, 2), (7, 1)):
-        outs[n], outs[ahead] = lax.optimization_barrier((outs[n], outs[ahead]))
-        outs[n] = sent(outs[n], SLOTS[n])
+    outs[6], outs[7], outs[3] = lax.optimization_barrier((outs[6], outs[7], outs[3]))
+    outs[6], outs[7] = sent(outs[6], SLOTS[6]), sent(outs[7], SLOTS[7])
 
     def joined(slots, into):
         return pl.pallas_call(

time: 42.1 us -> 42.7 us (1.014)
  waiting for transfers between devices: 10.4 us -> 12.2 us
  starting transfers between devices: 17 us -> 16 us
    ppermute x7, waiting for transfers between devices: 5.85 us -> 7.67 us  [sent(): return lax.ppermute(x, ('seq', 'head'), pairs)]
    ppermute x7, starting transfers between devices: 8.28 us -> 7.29 us  [sent(): return lax.ppermute(x, ('seq', 'head'), pairs)]
  transfers between devices with their start and end apart: 15 -> 15, of which waited for: 6 -> 7; matrix products, arithmetic and copies ran while one was open for 2% -> 2% of each run, Pallas kernels for 21% -> 20%
where the time goes in v1:
time: 42.7 us; the launch traced here: 42.5 us
  starting transfers between devices  16 us (37%)
  waiting for transfers between devices  12.2 us (29%)
  Pallas kernels  11.4 us (27%)
  local copies, waits for them, and re-layouts  2.76 us (6%)
    pallas_call x13, Pallas kernels, call(): pl.pallas_call(kernel, in_specs=[whole_spec() for _ in ins], out_specs=[w...  9.75 us
    ppermute x7, waiting for transfers between devices, sent(): return lax.ppermute(x, ('seq', 'head'), pairs)  7.67 us
    ppermute x7, starting transfers between devices, sent(): return lax.ppermute(x, ('seq', 'head'), pairs)  7.29 us
    ppermute x5, starting transfers between devices, partner(): return lax.ppermute(x, ('seq', 'head'), pairs)  4.82 us
    ppermute x3, waiting for transfers between devices, levels_back(): return lax.ppermute(x, 'seq', pairs)  4.42 us
    ppermute x3, starting transfers between devices, levels_back(): return lax.ppermute(x, 'seq', pairs)  3.88 us
    pallas_call x2, Pallas kernels, joined(): pl.pallas_call(lambda *refs: join_kernel(slots, *refs), in_specs=[whole_s...  1.64 us
    dynamic_slice x2, local copies, waits for them, and re-layouts, by_levels(): lax.dynamic_slice_in_dim(w, place * heads, heads)  0.99 us
  transfers between devices with their start and end apart: 15, of which 7 were waited for; matrix products, arithmetic and copies ran while one was open for 2% of the time, Pallas kernels for 20%

profile of v1, /device:TPU:27, one launch (start us, length us, event | category | flops | bytes accessed | tf_op | source)
XLA Modules:
  0.0 42.5 jit_solution(1950752537660639627)
XLA Ops:
  0.0 0.9 %constant_dynamic-slice_fusion.2 = (bf16[64,256]{1,0:T(8,128)(2,1)S(1)}, bf16[64,256]{1,0:T(8,128)(2,1)S(1)}, bf16[64,256]{1,0:T(8,128)(2,1)S(1)}, bf16[64,256]{1,0:T(8,128)(2,1)S(1)}) fusion(bf16[64,512]{1,0:T(8,128)(2,1)} %param.8, s32[]{:T(128)S(6)} %select_n.19, s32[]{:T(128)S(6)} %select_n.18, bf16[64,512]{1,0:T(8,128)(2,1)} %param.7), kind=kLoop, calls=%fused_computation.2 | loop fusion | bytes 262152 | tf_op jit(solution)/shard_map/dynamic_slice | solution.py:440
  1.0 0.3 collective-permute-start.2
  1.3 0.8 %copy-done.2 = bf16[64,8192]{1,0:T(8,128)(2,1)S(1)} copy-done((bf16[64,8192]{1,0:T(8,128)(2,1)S(1)}, bf16[64,8192]{1,0:T(8,128)(2,1)}, u32[]{:S(2)}) %copy-start.2) | copy-done | bytes 1048600
  2.2 0.4 %collective-permute-start = (bf16[64,2048]{1,0:T(8,128)(2,1)S(1)}, bf16[64,2048]{1,0:T(8,128)(2,1)S(1)}, u32[]{:S(2)}, u32[]{:S(2)}) collective-permute-start(bf16[64,2048]{1,0:T(8,128)(2,1)S(1)} %get-tuple-element.57), channel_id=1, source_target_pairs={{0,4},{1,5},{2,6},{3,7},{4,0},{5,1},{6,2},{7,3},{8,12},{9,13},{10,... | collective-permute-start | bytes 786440 | tf_op jit(solution)/shard_map/ppermute | solution.py:431
  2.6 1.9 %collective-permute-start.1 = (bf16[64,2048]{1,0:T(8,128)(2,1)S(1)}, bf16[64,2048]{1,0:T(8,128)(2,1)S(1)}, u32[]{:S(2)}, u32[]{:S(2)}) collective-permute-start(bf16[64,2048]{1,0:T(8,128)(2,1)S(1)} %get-tuple-element.58), channel_id=1, source_target_pairs={{0,6},{1,7},{2,4},{3,5},{4,2},{5,3},{6,0},{7,1},{8,14},{9,15},{10,... | collective-permute-start | bytes 786440 | tf_op jit(solution)/shard_map/ppermute | solution.py:431
  4.6 2.0 %collective-permute-start.3 = (bf16[128,256]{1,0:T(8,128)(2,1)S(1)}, bf16[128,256]{1,0:T(8,128)(2,1)S(1)}, u32[]{:S(2)}, u32[]{:S(2)}) collective-permute-start(bf16[128,256]{1,0:T(8,128)(2,1)S(1)} %pair_kv.1), channel_id=1, source_target_pairs={{0,2},{1,3},{2,0},{3,1},{4,6},{5,7},{6,4},{7,5},{8,10},{9,11},{10,... | collective-permute-start | bytes 196616 | tf_op jit(solution)/shard_map/ppermute | solution.py:431
  6.8 1.0 %constant_dynamic-slice_fusion.1.wq_ref = bf16[16,64,128]{2,1,0:T(8,128)(2,1)S(1)} fusion(bf16[64,64,128]{2,1,0:T(8,128)(2,1)} %bitcast.5, s32[]{:T(128)S(6)} %select_n.20), kind=kLoop, calls=%fused_computation.1 | loop fusion | bytes 524292 | tf_op jit(solution)/shard_map/dynamic_slice | solution.py:452
  7.8 1.3 %collective-permute-start.5 = (bf16[256,256]{1,0:T(8,128)(2,1)S(1)}, bf16[256,256]{1,0:T(8,128)(2,1)S(1)}, u32[]{:S(2)}, u32[]{:S(2)}) collective-permute-start(bf16[256,256]{1,0:T(8,128)(2,1)S(1)} %stack_kv.1.own_ref.refs_3_), channel_id=1, source_target_pairs={{0,8},{2,10},{4,12},{6,14},{8,16},{10,18},{12,20},{14,22},{16,24},... | collective-permute-start | bytes 393224 | tf_op jit(solution)/shard_map/ppermute | solution.py:435
  9.1 1.3 %collective-permute-start.6 = (bf16[256,256]{1,0:T(8,128)(2,1)S(1)}, bf16[256,256]{1,0:T(8,128)(2,1)S(1)}, u32[]{:S(2)}, u32[]{:S(2)}) collective-permute-start(bf16[256,256]{1,0:T(8,128)(2,1)S(1)} %stack_kv.1.own_ref.refs_3_), channel_id=1, source_target_pairs={{0,16},{2,18},{4,20},{6,22},{8,24},{10,26},{12,28},{14,30},{1,17},... | collective-permute-start | bytes 393224 | tf_op jit(solution)/shard_map/ppermute | solution.py:435
  10.4 0.7 %own_features.1._ = bf16[2048,512]{1,0:T(8,128)(2,1)S(1)} custom-call(bf16[256,256]{1,0:T(8,128)(2,1)S(1)} %stack_kv.1.own_ref.refs_3_, bf16[16,64,128]{2,1,0:T(8,128)(2,1)S(1)} %constant_dynamic-slice_fusion.wk_ref.refs_6_), custom_call_target="tpu_custom_call" | custom-call | tf_op jit(solution)/shard_map/own_features/pallas_call | solution.py:401
  11.1 0.4 weights.1
  11.5 1.1 %query_features.2 = (bf16[2048,128]{1,0:T(8,128)(2,1)S(1)}, bf16[2048,128]{1,0:T(8,128)(2,1)S(1)}) custom-call(bf16[64,2048]{1,0:T(8,128)(2,1)S(1)} %get-tuple-element.59.a_ref, bf16[64,2048]{1,0:T(8,128)(2,1)S(1)} %collective-permute-done.4.b_ref, bf16[16,128,128]{2,1,0:T(8,128)(2,1)S(1)} %get-tuple-element.70.w_ref, f32[16,128]{1,0:T(8,128)S(1)} %get-tuple-element.71.ratio_ref), custom_call_target="tpu_custom_call" | custom-call | tf_op jit(solution)/shard_map/query_features/pallas_call | solution.py:401
  12.6 1.3 %collective-permute-start.7 = (bf16[256,256]{1,0:T(8,128)(2,1)S(1)}, bf16[256,256]{1,0:T(8,128)(2,1)S(1)}, u32[]{:S(2)}, u32[]{:S(2)}) collective-permute-start(bf16[256,256]{1,0:T(8,128)(2,1)S(1)} %stack_kv.1.own_ref.refs_3_), channel_id=1, source_target_pairs={{0,24},{2,26},{4,28},{6,30},{1,25},{3,27},{5,29},{7,31}} | collective-permute-start | bytes 393224 | tf_op jit(solution)/shard_map/ppermute | solution.py:435
  13.9 0.4 collective-permute-done.5.last_ref.refs_2_
  14.3 1.3 %last_features.1 = (bf16[2048,512]{1,0:T(8,128)(2,1)S(1)}, f32[2048,256]{1,0:T(8,128)S(1)}, f32[2048,256]{1,0:T(8,128)S(1)}) custom-call(bf16[256,256]{1,0:T(8,128)(2,1)S(1)} %collective-permute-done.5.last_ref.refs_2_, bf16[16,64,128]{2,1,0:T(8,128)(2,1)S(1)} %constant_dynamic-slice_fusion.wk_ref.refs_6_, ...), custom_call_target="tpu_custom_call", output_to_operand_aliasing={{0}: (2, {})} | custom-call | tf_op jit(solution)/shard_map/last_features/pallas_call | solution.py:401
  15.6 1.1 %near.2.refs_0_ = f32[2048,256]{1,0:T(8,128)S(1)} custom-call(bf16[2048,128]{1,0:T(8,128)(2,1)S(1)} %get-tuple-element.72.refs_0_, bf16[2048,128]{1,0:T(8,128)(2,1)S(1)} %get-tuple-element.78.refs_1_.refs_2_, bf16[256,256]{1,0:T(8,128)(2,1)S(1)} %collective-permute-done.5.last_ref.refs_2_, bf16[256,256]{1,0:T(8,128)(2,1)S(1)} %stack_kv.1.own_ref.refs_3_, ...), custom_call_target="tpu_custom_call" | custom-call | tf_op jit(solution)/shard_map/near/pallas_call | solution.py:401
  16.8 1.1 %query_features.3 = (bf16[2048,128]{1,0:T(8,128)(2,1)S(1)}, bf16[2048,128]{1,0:T(8,128)(2,1)S(1)}) custom-call(bf16[64,2048]{1,0:T(8,128)(2,1)S(1)} %collective-permute-done.a_ref, bf16[64,2048]{1,0:T(8,128)(2,1)S(1)} %collective-permute-done.1.b_ref, bf16[16,128,128]{2,1,0:T(8,128)(2,1)S(1)} %get-tuple-element.70.w_ref, ...), custom_call_target="tpu_custom_call" | custom-call | tf_op jit(solution)/shard_map/query_features/pallas_call | solution.py:401
  18.0 1.1 %near.3.refs_1_ = f32[2048,256]{1,0:T(8,128)S(1)} custom-call(bf16[2048,128]{1,0:T(8,128)(2,1)S(1)} %get-tuple-element.85.refs_0_, bf16[2048,128]{1,0:T(8,128)(2,1)S(1)} %get-tuple-element.86.refs_1_.refs_3_, bf16[256,256]{1,0:T(8,128)(2,1)S(1)} %collective-permute-done.5.last_ref.refs_2_, bf16[256,256]{1,0:T(8,128)(2,1)S(1)} %stack_kv.1.own_ref.refs_3_, ...), custom_call_target="tpu_custom_call" | custom-call | tf_op jit(solution)/shard_map/near/pallas_call | solution.py:401
  19.0 4.0 %collective-permute-done.6.before_ref = bf16[256,256]{1,0:T(8,128)(2,1)S(1)} collective-permute-done((bf16[256,256]{1,0:T(8,128)(2,1)S(1)}, bf16[256,256]{1,0:T(8,128)(2,1)S(1)}, u32[]{:S(2)}, u32[]{:S(2)}) %collective-permute-start.6) | collective-permute-done | bytes 131104 | tf_op jit(solution)/shard_map/ppermute | solution.py:435
  23.1 1.0 %past.1.refs_4_ = f32[2048,256]{1,0:T(8,128)S(1)} custom-call(bf16[256,256]{1,0:T(8,128)(2,1)S(1)} %collective-permute-done.6.before_ref, bf16[16,64,128]{2,1,0:T(8,128)(2,1)S(1)} %constant_dynamic-slice_fusion.wk_ref.refs_6_, f32[2048,256]{1,0:T(8,128)S(1)} %get-tuple-element.90.sum_ref), custom_call_target="tpu_custom_call" | custom-call | tf_op jit(solution)/shard_map/past/pallas_call | solution.py:401
  24.1 1.8 %mix_level.1 = (bf16[32,2048]{1,0:T(8,128)(2,1)S(1)}, bf16[32,2048]{1,0:T(8,128)(2,1)S(1)}, bf16[32,2048]{1,0:T(8,128)(2,1)S(1)}, bf16[32,2048]{1,0:T(8,128)(2,1...) custom-call(f32[2048,256]{1,0:T(8,128)S(1)} %near.2.refs_0_, ...), custom_call_target="tpu_custom_call" | custom-call | tf_op jit(solution)/shard_map/mix_level/pallas_call | solution.py:401
  25.9 0.9 %collective-permute-start.10 = (bf16[32,2048]{1,0:T(8,128)(2,1)S(1)}, bf16[32,2048]{1,0:T(8,128)(2,1)S(1)}, u32[]{:S(2)}, u32[]{:S(2)}) collective-permute-start(bf16[32,2048]{1,0:T(8,128)(2,1)S(1)} %get-tuple-element.98), channel_id=1, source_target_pairs={{0,2},{1,3},{2,0},{3,1},{4,6},{5,7},{6,4},{7,5},{8,10},{9,11},{10,... | collective-permute-start | bytes 393224 | tf_op jit(solution)/shard_map/ppermute | solution.py:538
  26.8 1.2 %collective-permute-start.13 = (bf16[32,2048]{1,0:T(8,128)(2,1)S(1)}, bf16[32,2048]{1,0:T(8,128)(2,1)S(1)}, u32[]{:S(2)}, u32[]{:S(2)}) collective-permute-start(bf16[32,2048]{1,0:T(8,128)(2,1)S(1)} %get-tuple-element.102), channel_id=1, source_target_pairs={{0,4},{1,5},{2,3},{3,2},{4,0},{5,1},{6,7},{7,6},{8,12},{9,13},{10,... | collective-permute-start | bytes 393224 | tf_op jit(solution)/shard_map/ppermute | solution.py:538
  28.2 1.3 %collective-permute-start.8 = (bf16[32,2048]{1,0:T(8,128)(2,1)S(1)}, bf16[32,2048]{1,0:T(8,128)(2,1)S(1)}, u32[]{:S(2)}, u32[]{:S(2)}) collective-permute-start(bf16[32,2048]{1,0:T(8,128)(2,1)S(1)} %get-tuple-element.94), channel_id=1, source_target_pairs={{0,5},{1,4},{2,7},{3,6},{4,1},{5,0},{6,3},{7,2},{8,13},{9,12},{10,... | collective-permute-start | bytes 393224 | tf_op jit(solution)/shard_map/ppermute | solution.py:538
  29.5 2.0 %collective-permute-start.9 = (bf16[32,2048]{1,0:T(8,128)(2,1)S(1)}, bf16[32,2048]{1,0:T(8,128)(2,1)S(1)}, u32[]{:S(2)}, u32[]{:S(2)}) collective-permute-start(bf16[32,2048]{1,0:T(8,128)(2,1)S(1)} %get-tuple-element.95), channel_id=1, source_target_pairs={{0,6},{1,7},{2,1},{3,0},{4,2},{5,3},{6,5},{7,4},{8,14},{9,15},{10,... | collective-permute-start | bytes 393224 | tf_op jit(solution)/shard_map/ppermute | solution.py:538
  31.5 0.7 %collective-permute-start.11 = (bf16[32,2048]{1,0:T(8,128)(2,1)S(1)}, bf16[32,2048]{1,0:T(8,128)(2,1)S(1)}, u32[]{:S(2)}, u32[]{:S(2)}) collective-permute-start(bf16[32,2048]{1,0:T(8,128)(2,1)S(1)} %get-tuple-element.99), channel_id=1, source_target_pairs={{0,7},{1,6},{2,5},{3,4},{4,3},{5,2},{6,1},{7,0},{8,15},{9,14},{10,... | collective-permute-start | bytes 393224 | tf_op jit(solution)/shard_map/ppermute | solution.py:538
  32.2 1.0 %collective-permute-start.12 = (bf16[32,2048]{1,0:T(8,128)(2,1)S(1)}, bf16[32,2048]{1,0:T(8,128)(2,1)S(1)}, u32[]{:S(2)}, u32[]{:S(2)}) collective-permute-start(bf16[32,2048]{1,0:T(8,128)(2,1)S(1)} %get-tuple-element.100), channel_id=1, source_target_pairs={{0,3},{1,2},{2,4},{3,5},{4,7},{5,6},{6,0},{7,1},{8,11},{9,10},{10,... | collective-permute-start | bytes 393224 | tf_op jit(solution)/shard_map/ppermute | solution.py:538
  33.5 0.8 %join.2.refs_4_ = bf16[32,16384]{1,0:T(8,128)(2,1)} custom-call(bf16[32,2048]{1,0:T(8,128)(2,1)S(1)} %get-tuple-element.101.refs_0_, bf16[32,2048]{1,0:T(8,128)(2,1)S(1)} %collective-permute-done.13.refs_1_, bf16[32,2048]{1,0:T(8,128)(2,1)S(1)} %collective-permute-done.14.refs_2_, bf16[32,2048]{1,0:T(8,128)(2,1)S(1)} %collective-permute-done.10.refs_3_), custom_call_target="tpu_custom_call" | custom-call | tf_op jit(solution)/shard_map/join/pallas_call | solution.py:547
  34.3 1.7 %collective-permute-done.8.refs_0_ = bf16[32,2048]{1,0:T(8,128)(2,1)S(1)} collective-permute-done((bf16[32,2048]{1,0:T(8,128)(2,1)S(1)}, bf16[32,2048]{1,0:T(8,128)(2,1)S(1)}, u32[]{:S(2)}, u32[]{:S(2)}) %collective-permute-start.8) | collective-permute-done | bytes 131104 | tf_op jit(solution)/shard_map/ppermute | solution.py:538
  36.1 3.1 %collective-permute-done.9.refs_1_ = bf16[32,2048]{1,0:T(8,128)(2,1)S(1)} collective-permute-done((bf16[32,2048]{1,0:T(8,128)(2,1)S(1)}, bf16[32,2048]{1,0:T(8,128)(2,1)S(1)}, u32[]{:S(2)}, u32[]{:S(2)}) %collective-permute-start.9) | collective-permute-done | bytes 131104 | tf_op jit(solution)/shard_map/ppermute | solution.py:538
  39.2 2.5 %collective-permute-done.11.refs_2_ = bf16[32,2048]{1,0:T(8,128)(2,1)S(1)} collective-permute-done((bf16[32,2048]{1,0:T(8,128)(2,1)S(1)}, bf16[32,2048]{1,0:T(8,128)(2,1)S(1)}, u32[]{:S(2)}, u32[]{:S(2)}) %collective-permute-start.11) | collective-permute-done | bytes 131104 | tf_op jit(solution)/shard_map/ppermute | solution.py:538
  41.7 0.8 %join.3 = bf16[32,16384]{1,0:T(8,128)(2,1)} custom-call(bf16[32,2048]{1,0:T(8,128)(2,1)S(1)} %collective-permute-done.8.refs_0_, bf16[32,2048]{1,0:T(8,128)(2,1)S(1)} %collective-permute-done.9.refs_1_, bf16[32,2048]{1,0:T(8,128)(2,1)S(1)} %collective-permute-done.11.refs_2_, ...), custom_call_target="tpu_custom_call", output_to_operand_aliasing={{}: (4, {})} | custom-call | tf_op jit(solution)/shard_map/join/pallas_call | solution.py:547
  (22 shorter events, 0.8 us)
Async XLA Ops:
  0.0 4.6 %copy-start = (bf16[64,128,64]{1,2,0:T(8,128)(2,1)S(1)}, bf16[64,128,64]{1,2,0:T(8,128)(2,1)}, u32[]{:S(2)}) copy-start(bf16[64,128,64]{1,2,0:T(8,128)(2,1)} %param.10) | copy-start | bytes 3145732
  0.9 1.2 %copy-start.2 = (bf16[64,8192]{1,0:T(8,128)(2,1)S(1)}, bf16[64,8192]{1,0:T(8,128)(2,1)}, u32[]{:S(2)}) copy-start(bf16[64,8192]{1,0:T(8,128)(2,1)} %q_ref) | copy-start | bytes 3145732
  1.0 3.6 %collective-permute-start.2 = (bf16[64,512]{1,0:T(8,128)(2,1)S(1)}, bf16[64,512]{1,0:T(8,128)(2,1)S(1)}, u32[]{:S(2)}, u32[]{:S(2)}) collective-permute-start(bf16[64,512]{1,0:T(8,128)(2,1)S(1)} %get-tuple-element.55), channel_id=1, source_target_pairs={{0,4},{1,5},{2,6},{3,7},{4,0},{5,1},{6,2},{7,3},{8,12},{9,13},{10,... | collective-permute-start | bytes 196616 | tf_op jit(solution)/shard_map/ppermute | solution.py:431
  2.2 14.5 %collective-permute-start = (bf16[64,2048]{1,0:T(8,128)(2,1)S(1)}, bf16[64,2048]{1,0:T(8,128)(2,1)S(1)}, u32[]{:S(2)}, u32[]{:S(2)}) collective-permute-start(bf16[64,2048]{1,0:T(8,128)(2,1)S(1)} %get-tuple-element.57), channel_id=1, source_target_pairs={{0,4},{1,5},{2,6},{3,7},{4,0},{5,1},{6,2},{7,3},{8,12},{9,13},{10,... | collective-permute-start | bytes 786440 | tf_op jit(solution)/shard_map/ppermute | solution.py:431
  2.6 14.2 %collective-permute-start.1 = (bf16[64,2048]{1,0:T(8,128)(2,1)S(1)}, bf16[64,2048]{1,0:T(8,128)(2,1)S(1)}, u32[]{:S(2)}, u32[]{:S(2)}) collective-permute-start(bf16[64,2048]{1,0:T(8,128)(2,1)S(1)} %get-tuple-element.58), channel_id=1, source_target_pairs={{0,6},{1,7},{2,4},{3,5},{4,2},{5,3},{6,0},{7,1},{8,14},{9,15},{10,... | collective-permute-start | bytes 786440 | tf_op jit(solution)/shard_map/ppermute | solution.py:431
  4.6 3.1 %collective-permute-start.3 = (bf16[128,256]{1,0:T(8,128)(2,1)S(1)}, bf16[128,256]{1,0:T(8,128)(2,1)S(1)}, u32[]{:S(2)}, u32[]{:S(2)}) collective-permute-start(bf16[128,256]{1,0:T(8,128)(2,1)S(1)} %pair_kv.1), channel_id=1, source_target_pairs={{0,2},{1,3},{2,0},{3,1},{4,6},{5,7},{6,4},{7,5},{8,10},{9,11},{10,... | collective-permute-start | bytes 196616 | tf_op jit(solution)/shard_map/ppermute | solution.py:431
  6.7 3.7 %collective-permute-start.4 = (bf16[64,2048]{1,0:T(8,128)(2,1)S(1)}, bf16[64,2048]{1,0:T(8,128)(2,1)S(1)}, u32[]{:S(2)}, u32[]{:S(2)}) collective-permute-start(bf16[64,2048]{1,0:T(8,128)(2,1)S(1)} %get-tuple-element.67), channel_id=1, source_target_pairs={{0,2},{1,3},{2,0},{3,1},{4,6},{5,7},{6,4},{7,5},{8,10},{9,11},{10,... | collective-permute-start | bytes 786440 | tf_op jit(solution)/shard_map/ppermute | solution.py:431
  7.8 3.3 %copy-start.1 = (f32[64]{0:T(128)S(1)}, f32[64]{0:T(128)}, u32[]{:S(2)}) copy-start(f32[64]{0:T(128)} %param.11) | copy-start | bytes 772
  7.8 6.5 %collective-permute-start.5 = (bf16[256,256]{1,0:T(8,128)(2,1)S(1)}, bf16[256,256]{1,0:T(8,128)(2,1)S(1)}, u32[]{:S(2)}, u32[]{:S(2)}) collective-permute-start(bf16[256,256]{1,0:T(8,128)(2,1)S(1)} %stack_kv.1.own_ref.refs_3_), channel_id=1, source_target_pairs={{0,8},{2,10},{4,12},{6,14},{8,16},{10,18},{12,20},{14,22},{16,24},... | collective-permute-start | bytes 393224 | tf_op jit(solution)/shard_map/ppermute | solution.py:435
  9.1 14.0 %collective-permute-start.6 = (bf16[256,256]{1,0:T(8,128)(2,1)S(1)}, bf16[256,256]{1,0:T(8,128)(2,1)S(1)}, u32[]{:S(2)}, u32[]{:S(2)}) collective-permute-start(bf16[256,256]{1,0:T(8,128)(2,1)S(1)} %stack_kv.1.own_ref.refs_3_), channel_id=1, source_target_pairs={{0,16},{2,18},{4,20},{6,22},{8,24},{10,26},{12,28},{14,30},{1,17},... | collective-permute-start | bytes 393224 | tf_op jit(solution)/shard_map/ppermute | solution.py:435
  12.6 11.4 %collective-permute-start.7 = (bf16[256,256]{1,0:T(8,128)(2,1)S(1)}, bf16[256,256]{1,0:T(8,128)(2,1)S(1)}, u32[]{:S(2)}, u32[]{:S(2)}) collective-permute-start(bf16[256,256]{1,0:T(8,128)(2,1)S(1)} %stack_kv.1.own_ref.refs_3_), channel_id=1, source_target_pairs={{0,24},{2,26},{4,28},{6,30},{1,25},{3,27},{5,29},{7,31}} | collective-permute-start | bytes 393224 | tf_op jit(solution)/shard_map/ppermute | solution.py:435
  25.9 5.6 %collective-permute-start.10 = (bf16[32,2048]{1,0:T(8,128)(2,1)S(1)}, bf16[32,2048]{1,0:T(8,128)(2,1)S(1)}, u32[]{:S(2)}, u32[]{:S(2)}) collective-permute-start(bf16[32,2048]{1,0:T(8,128)(2,1)S(1)} %get-tuple-element.98), channel_id=1, source_target_pairs={{0,2},{1,3},{2,0},{3,1},{4,6},{5,7},{6,4},{7,5},{8,10},{9,11},{10,... | collective-permute-start | bytes 393224 | tf_op jit(solution)/shard_map/ppermute | solution.py:538
  26.8 5.4 %collective-permute-start.13 = (bf16[32,2048]{1,0:T(8,128)(2,1)S(1)}, bf16[32,2048]{1,0:T(8,128)(2,1)S(1)}, u32[]{:S(2)}, u32[]{:S(2)}) collective-permute-start(bf16[32,2048]{1,0:T(8,128)(2,1)S(1)} %get-tuple-element.102), channel_id=1, source_target_pairs={{0,4},{1,5},{2,3},{3,2},{4,0},{5,1},{6,7},{7,6},{8,12},{9,13},{10,... | collective-permute-start | bytes 393224 | tf_op jit(solution)/shard_map/ppermute | solution.py:538
  28.0 5.5 %collective-permute-start.14 = (bf16[32,2048]{1,0:T(8,128)(2,1)S(1)}, bf16[32,2048]{1,0:T(8,128)(2,1)S(1)}, u32[]{:S(2)}, u32[]{:S(2)}) collective-permute-start(bf16[32,2048]{1,0:T(8,128)(2,1)S(1)} %get-tuple-element.103), channel_id=1, source_target_pairs={{0,1},{1,0},{2,6},{3,7},{4,5},{5,4},{6,2},{7,3},{8,9},{9,8},{10,14... | collective-permute-start | bytes 393224 | tf_op jit(solution)/shard_map/ppermute | solution.py:538
  28.2 7.9 %collective-permute-start.8 = (bf16[32,2048]{1,0:T(8,128)(2,1)S(1)}, bf16[32,2048]{1,0:T(8,128)(2,1)S(1)}, u32[]{:S(2)}, u32[]{:S(2)}) collective-permute-start(bf16[32,2048]{1,0:T(8,128)(2,1)S(1)} %get-tuple-element.94), channel_id=1, source_target_pairs={{0,5},{1,4},{2,7},{3,6},{4,1},{5,0},{6,3},{7,2},{8,13},{9,12},{10,... | collective-permute-start | bytes 393224 | tf_op jit(solution)/shard_map/ppermute | solution.py:538
  29.5 9.7 %collective-permute-start.9 = (bf16[32,2048]{1,0:T(8,128)(2,1)S(1)}, bf16[32,2048]{1,0:T(8,128)(2,1)S(1)}, u32[]{:S(2)}, u32[]{:S(2)}) collective-permute-start(bf16[32,2048]{1,0:T(8,128)(2,1)S(1)} %get-tuple-element.95), channel_id=1, source_target_pairs={{0,6},{1,7},{2,1},{3,0},{4,2},{5,3},{6,5},{7,4},{8,14},{9,15},{10,... | collective-permute-start | bytes 393224 | tf_op jit(solution)/shard_map/ppermute | solution.py:538
  31.5 10.2 %collective-permute-start.11 = (bf16[32,2048]{1,0:T(8,128)(2,1)S(1)}, bf16[32,2048]{1,0:T(8,128)(2,1)S(1)}, u32[]{:S(2)}, u32[]{:S(2)}) collective-permute-start(bf16[32,2048]{1,0:T(8,128)(2,1)S(1)} %get-tuple-element.99), channel_id=1, source_target_pairs={{0,7},{1,6},{2,5},{3,4},{4,3},{5,2},{6,1},{7,0},{8,15},{9,14},{10,... | collective-permute-start | bytes 393224 | tf_op jit(solution)/shard_map/ppermute | solution.py:538
  32.2 9.5 %collective-permute-start.12 = (bf16[32,2048]{1,0:T(8,128)(2,1)S(1)}, bf16[32,2048]{1,0:T(8,128)(2,1)S(1)}, u32[]{:S(2)}, u32[]{:S(2)}) collective-permute-start(bf16[32,2048]{1,0:T(8,128)(2,1)S(1)} %get-tuple-element.100), channel_id=1, source_target_pairs={{0,3},{1,2},{2,4},{3,5},{4,7},{5,6},{6,0},{7,1},{8,11},{9,10},{10,... | collective-permute-start | bytes 393224 | tf_op jit(solution)/shard_map/ppermute | solution.py:538

commit v2 on v1

--- a/solution.py
+++ b/solution.py
@@ -261,18 +261,18 @@
             )
 
 
-def past_kernel(before_ref, wk_ref, sum_ref, past_ref, fk_scr):
+def past_kernel(first_ref, wk_ref, sum_ref, past_ref, fk_scr):
     level = spot()[1]
 
-    @pl.when(level < 2)
+    @pl.when(level < 3)
     def _():
         past_ref[...] = sum_ref[...]
 
-    @pl.when(level >= 2)
+    @pl.when(level >= 3)
     def _():
-        write_key_features(before_ref[:, :DH], wk_ref, fk_scr)
+        write_key_features(first_ref[:, :DH], wk_ref, fk_scr)
         past_ref[...] = sum_ref[...] + jnp.dot(
-            fk_scr[...], with_ones(before_ref[:, DH:]), preferred_element_type=F32
+            fk_scr[...], with_ones(first_ref[:, DH:]), preferred_element_type=F32
         )
 
 
@@ -351,7 +351,7 @@
 
 def mix_kernel_of_level(*refs):
     near_refs, fq_refs, (past_ref, step_ref, wk_ref) = refs[:2], refs[2:4], refs[4:7]
-    first_ref, refs = refs[7], refs[8:]
+    before_ref, refs = refs[7], refs[8:]
     out_refs, (fk_scr, state_scr, out_scr) = refs[:-3], refs[-3:]
     rows, dh = near_refs[0].shape[0], near_refs[0].shape[1] // 2
     feats = fq_refs[0].shape[1]
@@ -361,16 +361,16 @@
     side = lax.axis_index("head")
     u = lax.div(place, 2)
 
-    @pl.when(level < 3)
+    @pl.when(level < 2)
     def _():
         state_scr[0] = past_ref[...].astype(BF16)
         state_scr[1] = (past_ref[...] + step_ref[...]).astype(BF16)
 
-    @pl.when(level >= 3)
+    @pl.when(level >= 2)
     def _():
-        write_key_features(first_ref[:, :dh], wk_ref, fk_scr)
+        write_key_features(before_ref[:, :dh], wk_ref, fk_scr)
         state = past_ref[...] + jnp.dot(
-            fk_scr[...], with_ones(first_ref[:, dh:]), preferred_element_type=F32
+            fk_scr[...], with_ones(before_ref[:, dh:]), preferred_element_type=F32
         )
         state_scr[0] = state.astype(BF16)
         state_scr[1] = (state + step_ref[...]).astype(BF16)
@@ -452,8 +452,9 @@
     wq, wk = [lax.dynamic_slice_in_dim(w, place * heads, heads) for w in (wq, wk)]
     pair, wq, wk = lax.optimization_barrier((pair, wq, wk))
     (kv,) = call(stack_kernel, [own, got, pair], [(2 * half, 2 * dh)], "stack_kv")
-    last, before = levels_back(kv, 1), levels_back(kv, 2)
+    last, first = levels_back(kv, 1), levels_back(kv, 3)
     wq, kv, q[1] = lax.optimization_barrier((wq, kv, q[1]))
+    before = levels_back(kv, 2)
     (fk,) = call(own_features_kernel, [kv, wk], [(states, 4 * half)], "own_features", limit=16)
     wq, ratio = call(
         weights_kernel,
@@ -488,8 +489,6 @@
         )[0]
 
     q_own, fq_own = query_features(q[0], q[1])
-    far_kv, fk, fq_own = lax.optimization_barrier((kv, fk, fq_own))
-    first = levels_back(far_kv, 3)
     last, fq_own, fk = lax.optimization_barrier((last, fq_own, fk))
     fk, past, step = call(
         last_features_kernel,
@@ -504,21 +503,21 @@
     q[2], q[3], near_own = lax.optimization_barrier((q[2], q[3], near_own))
     q_other, fq_other = query_features(q[2], q[3])
     near_other = near(1, q_other, fq_other)
-    before, near_other = lax.optimization_barrier((before, near_other))
+    first, near_other = lax.optimization_barrier((first, near_other))
     (past,) = call(
         past_kernel,
-        [before, wk, past],
+        [first, wk, past],
         [(states, 2 * dh)],
         "past",
         [pltpu.VMEM((states, 2 * half), BF16)],
         16,
         F32,
     )
-    first, past = lax.optimization_barrier((first, past))
+    before, past = lax.optimization_barrier((before, past))
     part = tok // sides
     outs = call(
         mix_kernel_of_level,
-        [near_own, near_other, fq_own, fq_other, past, step, wk, first],
+        [near_own, near_other, fq_own, fq_other, past, step, wk, before],
         [(part, heads * dh)] * (WAYS * sides),
         "mix_level",
         [

time: 42.7 us -> 42.1 us (0.986)
  transfers between devices with their start and end apart: 15 -> 15, of which waited for: 7 -> 7; matrix products, arithmetic and copies ran while one was open for 2% -> 2% of each run, Pallas kernels for 20% -> 21%
where the time goes in v2:
time: 42.1 us; the launch traced here: 41.9 us
  starting transfers between devices  15.6 us (37%)
  waiting for transfers between devices  11.9 us (28%)
  Pallas kernels  11.4 us (27%)
  local copies, waits for them, and re-layouts  2.76 us (7%)
    pallas_call x13, Pallas kernels, call(): pl.pallas_call(kernel, in_specs=[whole_spec() for _ in ins], out_specs=[w...  9.75 us
    ppermute x7, waiting for transfers between devices, sent(): return lax.ppermute(x, ('seq', 'head'), pairs)  7.67 us
    ppermute x7, starting transfers between devices, sent(): return lax.ppermute(x, ('seq', 'head'), pairs)  6.93 us
    ppermute x5, starting transfers between devices, partner(): return lax.ppermute(x, ('seq', 'head'), pairs)  4.82 us
    ppermute x3, waiting for transfers between devices, levels_back(): return lax.ppermute(x, 'seq', pairs)  4.15 us
    ppermute x3, starting transfers between devices, levels_back(): return lax.ppermute(x, 'seq', pairs)  3.88 us
    pallas_call x2, Pallas kernels, joined(): pl.pallas_call(lambda *refs: join_kernel(slots, *refs), in_specs=[whole_s...  1.64 us
    dynamic_slice x2, local copies, waits for them, and re-layouts, by_levels(): lax.dynamic_slice_in_dim(w, place * heads, heads)  0.99 us
  transfers between devices with their start and end apart: 15, of which 7 were waited for; matrix products, arithmetic and copies ran while one was open for 2% of the time, Pallas kernels for 21%

profile of v2, /device:TPU:27, one launch (start us, length us, event | category | flops | bytes accessed | tf_op | source)
XLA Modules:
  0.0 41.9 jit_solution(12841243104381305640)
XLA Ops:
  0.0 0.9 %constant_dynamic-slice_fusion.2 = (bf16[64,256]{1,0:T(8,128)(2,1)S(1)}, bf16[64,256]{1,0:T(8,128)(2,1)S(1)}, bf16[64,256]{1,0:T(8,128)(2,1)S(1)}, bf16[64,256]{1,0:T(8,128)(2,1)S(1)}) fusion(bf16[64,512]{1,0:T(8,128)(2,1)} %param.8, s32[]{:T(128)S(6)} %select_n.19, s32[]{:T(128)S(6)} %select_n.18, bf16[64,512]{1,0:T(8,128)(2,1)} %param.7), kind=kLoop, calls=%fused_computation.2 | loop fusion | bytes 262152 | tf_op jit(solution)/shard_map/dynamic_slice | solution.py:440
  1.0 0.3 collective-permute-start.2
  1.3 0.8 %copy-done.2 = bf16[64,8192]{1,0:T(8,128)(2,1)S(1)} copy-done((bf16[64,8192]{1,0:T(8,128)(2,1)S(1)}, bf16[64,8192]{1,0:T(8,128)(2,1)}, u32[]{:S(2)}) %copy-start.2) | copy-done | bytes 1048600
  2.2 0.4 %collective-permute-start = (bf16[64,2048]{1,0:T(8,128)(2,1)S(1)}, bf16[64,2048]{1,0:T(8,128)(2,1)S(1)}, u32[]{:S(2)}, u32[]{:S(2)}) collective-permute-start(bf16[64,2048]{1,0:T(8,128)(2,1)S(1)} %get-tuple-element.54), channel_id=1, source_target_pairs={{0,4},{1,5},{2,6},{3,7},{4,0},{5,1},{6,2},{7,3},{8,12},{9,13},{10,... | collective-permute-start | bytes 786440 | tf_op jit(solution)/shard_map/ppermute | solution.py:431
  2.6 1.9 %collective-permute-start.1 = (bf16[64,2048]{1,0:T(8,128)(2,1)S(1)}, bf16[64,2048]{1,0:T(8,128)(2,1)S(1)}, u32[]{:S(2)}, u32[]{:S(2)}) collective-permute-start(bf16[64,2048]{1,0:T(8,128)(2,1)S(1)} %get-tuple-element.55), channel_id=1, source_target_pairs={{0,6},{1,7},{2,4},{3,5},{4,2},{5,3},{6,0},{7,1},{8,14},{9,15},{10,... | collective-permute-start | bytes 786440 | tf_op jit(solution)/shard_map/ppermute | solution.py:431
  4.6 2.0 %collective-permute-start.3 = (bf16[128,256]{1,0:T(8,128)(2,1)S(1)}, bf16[128,256]{1,0:T(8,128)(2,1)S(1)}, u32[]{:S(2)}, u32[]{:S(2)}) collective-permute-start(bf16[128,256]{1,0:T(8,128)(2,1)S(1)} %pair_kv.1), channel_id=1, source_target_pairs={{0,2},{1,3},{2,0},{3,1},{4,6},{5,7},{6,4},{7,5},{8,10},{9,11},{10,... | collective-permute-start | bytes 196616 | tf_op jit(solution)/shard_map/ppermute | solution.py:431
  6.8 1.0 %constant_dynamic-slice_fusion.1.wq_ref = bf16[16,64,128]{2,1,0:T(8,128)(2,1)S(1)} fusion(bf16[64,64,128]{2,1,0:T(8,128)(2,1)} %bitcast.5, s32[]{:T(128)S(6)} %select_n.20), kind=kLoop, calls=%fused_computation.1 | loop fusion | bytes 524292 | tf_op jit(solution)/shard_map/dynamic_slice | solution.py:452
  7.8 1.3 %collective-permute-start.5 = (bf16[256,256]{1,0:T(8,128)(2,1)S(1)}, bf16[256,256]{1,0:T(8,128)(2,1)S(1)}, u32[]{:S(2)}, u32[]{:S(2)}) collective-permute-start(bf16[256,256]{1,0:T(8,128)(2,1)S(1)} %stack_kv.1.own_ref.refs_3_), channel_id=1, source_target_pairs={{0,8},{2,10},{4,12},{6,14},{8,16},{10,18},{12,20},{14,22},{16,24},... | collective-permute-start | bytes 393224 | tf_op jit(solution)/shard_map/ppermute | solution.py:435
  9.1 1.3 %collective-permute-start.6 = (bf16[256,256]{1,0:T(8,128)(2,1)S(1)}, bf16[256,256]{1,0:T(8,128)(2,1)S(1)}, u32[]{:S(2)}, u32[]{:S(2)}) collective-permute-start(bf16[256,256]{1,0:T(8,128)(2,1)S(1)} %stack_kv.1.own_ref.refs_3_), channel_id=1, source_target_pairs={{0,24},{2,26},{4,28},{6,30},{1,25},{3,27},{5,29},{7,31}} | collective-permute-start | bytes 393224 | tf_op jit(solution)/shard_map/ppermute | solution.py:435
  10.4 1.3 %collective-permute-start.7 = (bf16[256,256]{1,0:T(8,128)(2,1)S(1)}, bf16[256,256]{1,0:T(8,128)(2,1)S(1)}, u32[]{:S(2)}, u32[]{:S(2)}) collective-permute-start(bf16[256,256]{1,0:T(8,128)(2,1)S(1)} %stack_kv.1.own_ref.refs_3_), channel_id=1, source_target_pairs={{0,16},{2,18},{4,20},{6,22},{8,24},{10,26},{12,28},{14,30},{1,17},... | collective-permute-start | bytes 393224 | tf_op jit(solution)/shard_map/ppermute | solution.py:435
  11.7 0.7 %own_features.1._ = bf16[2048,512]{1,0:T(8,128)(2,1)S(1)} custom-call(bf16[256,256]{1,0:T(8,128)(2,1)S(1)} %stack_kv.1.own_ref.refs_3_, bf16[16,64,128]{2,1,0:T(8,128)(2,1)S(1)} %constant_dynamic-slice_fusion.wk_ref.refs_6_), custom_call_target="tpu_custom_call" | custom-call | tf_op jit(solution)/shard_map/own_features/pallas_call | solution.py:401
  12.4 0.4 weights.1
  12.8 1.1 %query_features.2 = (bf16[2048,128]{1,0:T(8,128)(2,1)S(1)}, bf16[2048,128]{1,0:T(8,128)(2,1)S(1)}) custom-call(bf16[64,2048]{1,0:T(8,128)(2,1)S(1)} %get-tuple-element.56.a_ref, bf16[64,2048]{1,0:T(8,128)(2,1)S(1)} %collective-permute-done.4.b_ref, bf16[16,128,128]{2,1,0:T(8,128)(2,1)S(1)} %get-tuple-element.67.w_ref, f32[16,128]{1,0:T(8,128)S(1)} %get-tuple-element.68.ratio_ref), custom_call_target="tpu_custom_call" | custom-call | tf_op jit(solution)/shard_map/query_features/pallas_call | solution.py:401
  13.9 0.4 collective-permute-done.5.last_ref.refs_2_
  14.3 1.3 %last_features.1 = (bf16[2048,512]{1,0:T(8,128)(2,1)S(1)}, f32[2048,256]{1,0:T(8,128)S(1)}, f32[2048,256]{1,0:T(8,128)S(1)}) custom-call(bf16[256,256]{1,0:T(8,128)(2,1)S(1)} %collective-permute-done.5.last_ref.refs_2_, bf16[16,64,128]{2,1,0:T(8,128)(2,1)S(1)} %constant_dynamic-slice_fusion.wk_ref.refs_6_, ...), custom_call_target="tpu_custom_call", output_to_operand_aliasing={{0}: (2, {})} | custom-call | tf_op jit(solution)/shard_map/last_features/pallas_call | solution.py:401
  15.6 1.1 %near.2.refs_0_ = f32[2048,256]{1,0:T(8,128)S(1)} custom-call(bf16[2048,128]{1,0:T(8,128)(2,1)S(1)} %get-tuple-element.69.refs_0_, bf16[2048,128]{1,0:T(8,128)(2,1)S(1)} %get-tuple-element.73.refs_1_.refs_2_, bf16[256,256]{1,0:T(8,128)(2,1)S(1)} %collective-permute-done.5.last_ref.refs_2_, bf16[256,256]{1,0:T(8,128)(2,1)S(1)} %stack_kv.1.own_ref.refs_3_, ...), custom_call_target="tpu_custom_call" | custom-call | tf_op jit(solution)/shard_map/near/pallas_call | solution.py:401
  16.8 1.1 %query_features.3 = (bf16[2048,128]{1,0:T(8,128)(2,1)S(1)}, bf16[2048,128]{1,0:T(8,128)(2,1)S(1)}) custom-call(bf16[64,2048]{1,0:T(8,128)(2,1)S(1)} %collective-permute-done.a_ref, bf16[64,2048]{1,0:T(8,128)(2,1)S(1)} %collective-permute-done.1.b_ref, bf16[16,128,128]{2,1,0:T(8,128)(2,1)S(1)} %get-tuple-element.67.w_ref, ...), custom_call_target="tpu_custom_call" | custom-call | tf_op jit(solution)/shard_map/query_features/pallas_call | solution.py:401
  18.0 1.1 %near.3.refs_1_ = f32[2048,256]{1,0:T(8,128)S(1)} custom-call(bf16[2048,128]{1,0:T(8,128)(2,1)S(1)} %get-tuple-element.80.refs_0_, bf16[2048,128]{1,0:T(8,128)(2,1)S(1)} %get-tuple-element.81.refs_1_.refs_3_, bf16[256,256]{1,0:T(8,128)(2,1)S(1)} %collective-permute-done.5.last_ref.refs_2_, bf16[256,256]{1,0:T(8,128)(2,1)S(1)} %stack_kv.1.own_ref.refs_3_, ...), custom_call_target="tpu_custom_call" | custom-call | tf_op jit(solution)/shard_map/near/pallas_call | solution.py:401
  19.1 1.0 %past.1.refs_4_ = f32[2048,256]{1,0:T(8,128)S(1)} custom-call(bf16[256,256]{1,0:T(8,128)(2,1)S(1)} %collective-permute-done.6.first_ref, bf16[16,64,128]{2,1,0:T(8,128)(2,1)S(1)} %constant_dynamic-slice_fusion.wk_ref.refs_6_, f32[2048,256]{1,0:T(8,128)S(1)} %get-tuple-element.84.sum_ref), custom_call_target="tpu_custom_call" | custom-call | tf_op jit(solution)/shard_map/past/pallas_call | solution.py:401
  20.1 3.8 %collective-permute-done.7.refs_7_ = bf16[256,256]{1,0:T(8,128)(2,1)S(1)} collective-permute-done((bf16[256,256]{1,0:T(8,128)(2,1)S(1)}, bf16[256,256]{1,0:T(8,128)(2,1)S(1)}, u32[]{:S(2)}, u32[]{:S(2)}) %collective-permute-start.7) | collective-permute-done | bytes 131104 | tf_op jit(solution)/shard_map/ppermute | solution.py:435
  23.8 1.8 %mix_level.1 = (bf16[32,2048]{1,0:T(8,128)(2,1)S(1)}, bf16[32,2048]{1,0:T(8,128)(2,1)S(1)}, bf16[32,2048]{1,0:T(8,128)(2,1)S(1)}, bf16[32,2048]{1,0:T(8,128)(2,1...) custom-call(f32[2048,256]{1,0:T(8,128)S(1)} %near.2.refs_0_, ...), custom_call_target="tpu_custom_call" | custom-call | tf_op jit(solution)/shard_map/mix_level/pallas_call | solution.py:401
  25.6 0.5 %collective-permute-start.10 = (bf16[32,2048]{1,0:T(8,128)(2,1)S(1)}, bf16[32,2048]{1,0:T(8,128)(2,1)S(1)}, u32[]{:S(2)}, u32[]{:S(2)}) collective-permute-start(bf16[32,2048]{1,0:T(8,128)(2,1)S(1)} %get-tuple-element.92), channel_id=1, source_target_pairs={{0,2},{1,3},{2,0},{3,1},{4,6},{5,7},{6,4},{7,5},{8,10},{9,11},{10,... | collective-permute-start | bytes 393224 | tf_op jit(solution)/shard_map/ppermute | solution.py:537
  26.2 1.2 %collective-permute-start.13 = (bf16[32,2048]{1,0:T(8,128)(2,1)S(1)}, bf16[32,2048]{1,0:T(8,128)(2,1)S(1)}, u32[]{:S(2)}, u32[]{:S(2)}) collective-permute-start(bf16[32,2048]{1,0:T(8,128)(2,1)S(1)} %get-tuple-element.96), channel_id=1, source_target_pairs={{0,4},{1,5},{2,3},{3,2},{4,0},{5,1},{6,7},{7,6},{8,12},{9,13},{10,... | collective-permute-start | bytes 393224 | tf_op jit(solution)/shard_map/ppermute | solution.py:537
  27.6 1.3 %collective-permute-start.8 = (bf16[32,2048]{1,0:T(8,128)(2,1)S(1)}, bf16[32,2048]{1,0:T(8,128)(2,1)S(1)}, u32[]{:S(2)}, u32[]{:S(2)}) collective-permute-start(bf16[32,2048]{1,0:T(8,128)(2,1)S(1)} %get-tuple-element.88), channel_id=1, source_target_pairs={{0,5},{1,4},{2,7},{3,6},{4,1},{5,0},{6,3},{7,2},{8,13},{9,12},{10,... | collective-permute-start | bytes 393224 | tf_op jit(solution)/shard_map/ppermute | solution.py:537
  28.8 2.0 %collective-permute-start.9 = (bf16[32,2048]{1,0:T(8,128)(2,1)S(1)}, bf16[32,2048]{1,0:T(8,128)(2,1)S(1)}, u32[]{:S(2)}, u32[]{:S(2)}) collective-permute-start(bf16[32,2048]{1,0:T(8,128)(2,1)S(1)} %get-tuple-element.89), channel_id=1, source_target_pairs={{0,6},{1,7},{2,1},{3,0},{4,2},{5,3},{6,5},{7,4},{8,14},{9,15},{10,... | collective-permute-start | bytes 393224 | tf_op jit(solution)/shard_map/ppermute | solution.py:537
  30.9 0.7 %collective-permute-start.11 = (bf16[32,2048]{1,0:T(8,128)(2,1)S(1)}, bf16[32,2048]{1,0:T(8,128)(2,1)S(1)}, u32[]{:S(2)}, u32[]{:S(2)}) collective-permute-start(bf16[32,2048]{1,0:T(8,128)(2,1)S(1)} %get-tuple-element.93), channel_id=1, source_target_pairs={{0,7},{1,6},{2,5},{3,4},{4,3},{5,2},{6,1},{7,0},{8,15},{9,14},{10,... | collective-permute-start | bytes 393224 | tf_op jit(solution)/shard_map/ppermute | solution.py:537
  31.5 1.0 %collective-permute-start.12 = (bf16[32,2048]{1,0:T(8,128)(2,1)S(1)}, bf16[32,2048]{1,0:T(8,128)(2,1)S(1)}, u32[]{:S(2)}, u32[]{:S(2)}) collective-permute-start(bf16[32,2048]{1,0:T(8,128)(2,1)S(1)} %get-tuple-element.94), channel_id=1, source_target_pairs={{0,3},{1,2},{2,4},{3,5},{4,7},{5,6},{6,0},{7,1},{8,11},{9,10},{10,... | collective-permute-start | bytes 393224 | tf_op jit(solution)/shard_map/ppermute | solution.py:537
  32.9 0.8 %join.2.refs_4_ = bf16[32,16384]{1,0:T(8,128)(2,1)} custom-call(bf16[32,2048]{1,0:T(8,128)(2,1)S(1)} %get-tuple-element.95.refs_0_, bf16[32,2048]{1,0:T(8,128)(2,1)S(1)} %collective-permute-done.13.refs_1_, bf16[32,2048]{1,0:T(8,128)(2,1)S(1)} %collective-permute-done.14.refs_2_, bf16[32,2048]{1,0:T(8,128)(2,1)S(1)} %collective-permute-done.10.refs_3_), custom_call_target="tpu_custom_call" | custom-call | tf_op jit(solution)/shard_map/join/pallas_call | solution.py:546
  33.7 1.7 %collective-permute-done.8.refs_0_ = bf16[32,2048]{1,0:T(8,128)(2,1)S(1)} collective-permute-done((bf16[32,2048]{1,0:T(8,128)(2,1)S(1)}, bf16[32,2048]{1,0:T(8,128)(2,1)S(1)}, u32[]{:S(2)}, u32[]{:S(2)}) %collective-permute-start.8) | collective-permute-done | bytes 131104 | tf_op jit(solution)/shard_map/ppermute | solution.py:537
  35.4 3.1 %collective-permute-done.9.refs_1_ = bf16[32,2048]{1,0:T(8,128)(2,1)S(1)} collective-permute-done((bf16[32,2048]{1,0:T(8,128)(2,1)S(1)}, bf16[32,2048]{1,0:T(8,128)(2,1)S(1)}, u32[]{:S(2)}, u32[]{:S(2)}) %collective-permute-start.9) | collective-permute-done | bytes 131104 | tf_op jit(solution)/shard_map/ppermute | solution.py:537
  38.6 2.5 %collective-permute-done.11.refs_2_ = bf16[32,2048]{1,0:T(8,128)(2,1)S(1)} collective-permute-done((bf16[32,2048]{1,0:T(8,128)(2,1)S(1)}, bf16[32,2048]{1,0:T(8,128)(2,1)S(1)}, u32[]{:S(2)}, u32[]{:S(2)}) %collective-permute-start.11) | collective-permute-done | bytes 131104 | tf_op jit(solution)/shard_map/ppermute | solution.py:537
  41.1 0.8 %join.3 = bf16[32,16384]{1,0:T(8,128)(2,1)} custom-call(bf16[32,2048]{1,0:T(8,128)(2,1)S(1)} %collective-permute-done.8.refs_0_, bf16[32,2048]{1,0:T(8,128)(2,1)S(1)} %collective-permute-done.9.refs_1_, bf16[32,2048]{1,0:T(8,128)(2,1)S(1)} %collective-permute-done.11.refs_2_, ...), custom_call_target="tpu_custom_call", output_to_operand_aliasing={{}: (4, {})} | custom-call | tf_op jit(solution)/shard_map/join/pallas_call | solution.py:546
  (22 shorter events, 0.8 us)
Async XLA Ops:
  0.0 4.6 %copy-start = (bf16[64,128,64]{1,2,0:T(8,128)(2,1)S(1)}, bf16[64,128,64]{1,2,0:T(8,128)(2,1)}, u32[]{:S(2)}) copy-start(bf16[64,128,64]{1,2,0:T(8,128)(2,1)} %param.10) | copy-start | bytes 3145732
  0.9 1.2 %copy-start.2 = (bf16[64,8192]{1,0:T(8,128)(2,1)S(1)}, bf16[64,8192]{1,0:T(8,128)(2,1)}, u32[]{:S(2)}) copy-start(bf16[64,8192]{1,0:T(8,128)(2,1)} %q_ref) | copy-start | bytes 3145732
  1.0 3.6 %collective-permute-start.2 = (bf16[64,512]{1,0:T(8,128)(2,1)S(1)}, bf16[64,512]{1,0:T(8,128)(2,1)S(1)}, u32[]{:S(2)}, u32[]{:S(2)}) collective-permute-start(bf16[64,512]{1,0:T(8,128)(2,1)S(1)} %get-tuple-element.52), channel_id=1, source_target_pairs={{0,4},{1,5},{2,6},{3,7},{4,0},{5,1},{6,2},{7,3},{8,12},{9,13},{10,... | collective-permute-start | bytes 196616 | tf_op jit(solution)/shard_map/ppermute | solution.py:431
  2.2 14.5 %collective-permute-start = (bf16[64,2048]{1,0:T(8,128)(2,1)S(1)}, bf16[64,2048]{1,0:T(8,128)(2,1)S(1)}, u32[]{:S(2)}, u32[]{:S(2)}) collective-permute-start(bf16[64,2048]{1,0:T(8,128)(2,1)S(1)} %get-tuple-element.54), channel_id=1, source_target_pairs={{0,4},{1,5},{2,6},{3,7},{4,0},{5,1},{6,2},{7,3},{8,12},{9,13},{10,... | collective-permute-start | bytes 786440 | tf_op jit(solution)/shard_map/ppermute | solution.py:431
  2.6 14.2 %collective-permute-start.1 = (bf16[64,2048]{1,0:T(8,128)(2,1)S(1)}, bf16[64,2048]{1,0:T(8,128)(2,1)S(1)}, u32[]{:S(2)}, u32[]{:S(2)}) collective-permute-start(bf16[64,2048]{1,0:T(8,128)(2,1)S(1)} %get-tuple-element.55), channel_id=1, source_target_pairs={{0,6},{1,7},{2,4},{3,5},{4,2},{5,3},{6,0},{7,1},{8,14},{9,15},{10,... | collective-permute-start | bytes 786440 | tf_op jit(solution)/shard_map/ppermute | solution.py:431
  4.6 3.1 %collective-permute-start.3 = (bf16[128,256]{1,0:T(8,128)(2,1)S(1)}, bf16[128,256]{1,0:T(8,128)(2,1)S(1)}, u32[]{:S(2)}, u32[]{:S(2)}) collective-permute-start(bf16[128,256]{1,0:T(8,128)(2,1)S(1)} %pair_kv.1), channel_id=1, source_target_pairs={{0,2},{1,3},{2,0},{3,1},{4,6},{5,7},{6,4},{7,5},{8,10},{9,11},{10,... | collective-permute-start | bytes 196616 | tf_op jit(solution)/shard_map/ppermute | solution.py:431
  6.7 3.7 %collective-permute-start.4 = (bf16[64,2048]{1,0:T(8,128)(2,1)S(1)}, bf16[64,2048]{1,0:T(8,128)(2,1)S(1)}, u32[]{:S(2)}, u32[]{:S(2)}) collective-permute-start(bf16[64,2048]{1,0:T(8,128)(2,1)S(1)} %get-tuple-element.64), channel_id=1, source_target_pairs={{0,2},{1,3},{2,0},{3,1},{4,6},{5,7},{6,4},{7,5},{8,10},{9,11},{10,... | collective-permute-start | bytes 786440 | tf_op jit(solution)/shard_map/ppermute | solution.py:431
  7.8 4.6 %copy-start.1 = (f32[64]{0:T(128)S(1)}, f32[64]{0:T(128)}, u32[]{:S(2)}) copy-start(f32[64]{0:T(128)} %param.11) | copy-start | bytes 772
  7.8 6.5 %collective-permute-start.5 = (bf16[256,256]{1,0:T(8,128)(2,1)S(1)}, bf16[256,256]{1,0:T(8,128)(2,1)S(1)}, u32[]{:S(2)}, u32[]{:S(2)}) collective-permute-start(bf16[256,256]{1,0:T(8,128)(2,1)S(1)} %stack_kv.1.own_ref.refs_3_), channel_id=1, source_target_pairs={{0,8},{2,10},{4,12},{6,14},{8,16},{10,18},{12,20},{14,22},{16,24},... | collective-permute-start | bytes 393224 | tf_op jit(solution)/shard_map/ppermute | solution.py:435
  9.1 10.0 %collective-permute-start.6 = (bf16[256,256]{1,0:T(8,128)(2,1)S(1)}, bf16[256,256]{1,0:T(8,128)(2,1)S(1)}, u32[]{:S(2)}, u32[]{:S(2)}) collective-permute-start(bf16[256,256]{1,0:T(8,128)(2,1)S(1)} %stack_kv.1.own_ref.refs_3_), channel_id=1, source_target_pairs={{0,24},{2,26},{4,28},{6,30},{1,25},{3,27},{5,29},{7,31}} | collective-permute-start | bytes 393224 | tf_op jit(solution)/shard_map/ppermute | solution.py:435
  10.4 13.4 %collective-permute-start.7 = (bf16[256,256]{1,0:T(8,128)(2,1)S(1)}, bf16[256,256]{1,0:T(8,128)(2,1)S(1)}, u32[]{:S(2)}, u32[]{:S(2)}) collective-permute-start(bf16[256,256]{1,0:T(8,128)(2,1)S(1)} %stack_kv.1.own_ref.refs_3_), channel_id=1, source_target_pairs={{0,16},{2,18},{4,20},{6,22},{8,24},{10,26},{12,28},{14,30},{1,17},... | collective-permute-start | bytes 393224 | tf_op jit(solution)/shard_map/ppermute | solution.py:435
  25.6 5.2 %collective-permute-start.10 = (bf16[32,2048]{1,0:T(8,128)(2,1)S(1)}, bf16[32,2048]{1,0:T(8,128)(2,1)S(1)}, u32[]{:S(2)}, u32[]{:S(2)}) collective-permute-start(bf16[32,2048]{1,0:T(8,128)(2,1)S(1)} %get-tuple-element.92), channel_id=1, source_target_pairs={{0,2},{1,3},{2,0},{3,1},{4,6},{5,7},{6,4},{7,5},{8,10},{9,11},{10,... | collective-permute-start | bytes 393224 | tf_op jit(solution)/shard_map/ppermute | solution.py:537
  26.2 5.4 %collective-permute-start.13 = (bf16[32,2048]{1,0:T(8,128)(2,1)S(1)}, bf16[32,2048]{1,0:T(8,128)(2,1)S(1)}, u32[]{:S(2)}, u32[]{:S(2)}) collective-permute-start(bf16[32,2048]{1,0:T(8,128)(2,1)S(1)} %get-tuple-element.96), channel_id=1, source_target_pairs={{0,4},{1,5},{2,3},{3,2},{4,0},{5,1},{6,7},{7,6},{8,12},{9,13},{10,... | collective-permute-start | bytes 393224 | tf_op jit(solution)/shard_map/ppermute | solution.py:537
  27.4 5.5 %collective-permute-start.14 = (bf16[32,2048]{1,0:T(8,128)(2,1)S(1)}, bf16[32,2048]{1,0:T(8,128)(2,1)S(1)}, u32[]{:S(2)}, u32[]{:S(2)}) collective-permute-start(bf16[32,2048]{1,0:T(8,128)(2,1)S(1)} %get-tuple-element.97), channel_id=1, source_target_pairs={{0,1},{1,0},{2,6},{3,7},{4,5},{5,4},{6,2},{7,3},{8,9},{9,8},{10,14... | collective-permute-start | bytes 393224 | tf_op jit(solution)/shard_map/ppermute | solution.py:537
  27.6 7.9 %collective-permute-start.8 = (bf16[32,2048]{1,0:T(8,128)(2,1)S(1)}, bf16[32,2048]{1,0:T(8,128)(2,1)S(1)}, u32[]{:S(2)}, u32[]{:S(2)}) collective-permute-start(bf16[32,2048]{1,0:T(8,128)(2,1)S(1)} %get-tuple-element.88), channel_id=1, source_target_pairs={{0,5},{1,4},{2,7},{3,6},{4,1},{5,0},{6,3},{7,2},{8,13},{9,12},{10,... | collective-permute-start | bytes 393224 | tf_op jit(solution)/shard_map/ppermute | solution.py:537
  28.8 9.7 %collective-permute-start.9 = (bf16[32,2048]{1,0:T(8,128)(2,1)S(1)}, bf16[32,2048]{1,0:T(8,128)(2,1)S(1)}, u32[]{:S(2)}, u32[]{:S(2)}) collective-permute-start(bf16[32,2048]{1,0:T(8,128)(2,1)S(1)} %get-tuple-element.89), channel_id=1, source_target_pairs={{0,6},{1,7},{2,1},{3,0},{4,2},{5,3},{6,5},{7,4},{8,14},{9,15},{10,... | collective-permute-start | bytes 393224 | tf_op jit(solution)/shard_map/ppermute | solution.py:537
  30.9 10.2 %collective-permute-start.11 = (bf16[32,2048]{1,0:T(8,128)(2,1)S(1)}, bf16[32,2048]{1,0:T(8,128)(2,1)S(1)}, u32[]{:S(2)}, u32[]{:S(2)}) collective-permute-start(bf16[32,2048]{1,0:T(8,128)(2,1)S(1)} %get-tuple-element.93), channel_id=1, source_target_pairs={{0,7},{1,6},{2,5},{3,4},{4,3},{5,2},{6,1},{7,0},{8,15},{9,14},{10,... | collective-permute-start | bytes 393224 | tf_op jit(solution)/shard_map/ppermute | solution.py:537
  31.5 9.5 %collective-permute-start.12 = (bf16[32,2048]{1,0:T(8,128)(2,1)S(1)}, bf16[32,2048]{1,0:T(8,128)(2,1)S(1)}, u32[]{:S(2)}, u32[]{:S(2)}) collective-permute-start(bf16[32,2048]{1,0:T(8,128)(2,1)S(1)} %get-tuple-element.94), channel_id=1, source_target_pairs={{0,3},{1,2},{2,4},{3,5},{4,7},{5,6},{6,0},{7,1},{8,11},{9,10},{10,... | collective-permute-start | bytes 393224 | tf_op jit(solution)/shard_map/ppermute | solution.py:537

commit v3 on v2

--- a/solution.py
+++ b/solution.py
@@ -239,13 +239,21 @@
     write_key_features(own_ref[:, :DH], wk_ref, fk_ref.at[:, own_ref.shape[0] :])
 
 
-def last_features_kernel(last_ref, wk_ref, _, fk_ref, past_ref, step_ref):
+def last_features_kernel(
+    one_ref, two_ref, three_ref, wk_ref, far_ref, _, fk_ref, past_ref, step_ref, last_ref
+):
     size = last_ref.shape[0]
     half = size // 2
     level = spot()[1]
+    for n, ref in enumerate((one_ref, two_ref, three_ref)):
+
+        @pl.when(level == n + 1)
+        def _():
+            last_ref[...] = ref[...]
 
     @pl.when(level == 0)
     def _():
+        last_ref[...] = jnp.zeros_like(last_ref)
         fk_ref[:, :size] = jnp.zeros((fk_ref.shape[0], size), BF16)
         for ref in (past_ref, step_ref):
             ref[...] = jnp.zeros_like(ref)
@@ -253,27 +261,32 @@
     @pl.when(level > 0)
     def _():
         write_key_features(last_ref[:, :DH], wk_ref, fk_ref.at[:, :size])
-        for at, ref in ((0, past_ref), (half, step_ref)):
-            ref[...] = jnp.dot(
+        states = [
+            jnp.dot(
                 fk_ref[:, at : at + half],
                 with_ones(last_ref[at : at + half, DH:]),
                 preferred_element_type=F32,
             )
-
-
-def past_kernel(first_ref, wk_ref, sum_ref, past_ref, fk_scr):
+            for at in (0, half)
+        ]
+        past_ref[...] = far_ref[...] + states[0]
+        step_ref[...] = states[1]
+
+
+def far_kernel(one_ref, two_ref, wk_ref, far_ref, fk_scr):
     level = spot()[1]
+    size = one_ref.shape[0]
 
     @pl.when(level < 3)
     def _():
-        past_ref[...] = sum_ref[...]
-
-    @pl.when(level >= 3)
+        far_ref[...] = jnp.zeros_like(far_ref)
+
+    @pl.when(level == 3)
     def _():
-        write_key_features(first_ref[:, :DH], wk_ref, fk_scr)
-        past_ref[...] = sum_ref[...] + jnp.dot(
-            fk_scr[...], with_ones(first_ref[:, DH:]), preferred_element_type=F32
-        )
+        keys = jnp.concatenate([one_ref[:, :DH], two_ref[:, :DH]], axis=0)
+        write_key_features(keys, wk_ref, fk_scr)
+        values = jnp.concatenate([one_ref[:, DH:], two_ref[:, DH:]], axis=0)
+        far_ref[...] = jnp.dot(fk_scr[...], with_ones(values), preferred_element_type=F32)
 
 
 def query_features_kernel(a_ref, b_ref, w_ref, ratio_ref, q_out, fq_out, exp_scr):
@@ -361,12 +374,12 @@
     side = lax.axis_index("head")
     u = lax.div(place, 2)
 
-    @pl.when(level < 2)
+    @pl.when(level != 2)
     def _():
         state_scr[0] = past_ref[...].astype(BF16)
         state_scr[1] = (past_ref[...] + step_ref[...]).astype(BF16)
 
-    @pl.when(level >= 2)
+    @pl.when(level == 2)
     def _():
         write_key_features(before_ref[:, :dh], wk_ref, fk_scr)
         state = past_ref[...] + jnp.dot(
@@ -430,8 +443,8 @@
         ]
         return lax.ppermute(x, ("seq", "head"), pairs)
 
-    def levels_back(x, by):
-        pairs = [(i, i + by * WAYS) for i in range(seq - by * WAYS)]
+    def along(x, *moves):
+        pairs = [(a * WAYS + r, b * WAYS + r) for a, b in moves for r in range(WAYS)]
         return lax.ppermute(x, "seq", pairs)
 
     place = lax.rem(lax.axis_index("seq"), WAYS)
@@ -452,9 +465,10 @@
     wq, wk = [lax.dynamic_slice_in_dim(w, place * heads, heads) for w in (wq, wk)]
     pair, wq, wk = lax.optimization_barrier((pair, wq, wk))
     (kv,) = call(stack_kernel, [own, got, pair], [(2 * half, 2 * dh)], "stack_kv")
-    last, first = levels_back(kv, 1), levels_back(kv, 3)
+    one = along(kv, (0, 1), (1, 3))
     wq, kv, q[1] = lax.optimization_barrier((wq, kv, q[1]))
-    before = levels_back(kv, 2)
+    two = along(kv, (0, 3), (1, 2))
+    three = along(kv, (2, 3), (0, 2))
     (fk,) = call(own_features_kernel, [kv, wk], [(states, 4 * half)], "own_features", limit=16)
     wq, ratio = call(
         weights_kernel,
@@ -489,35 +503,34 @@
         )[0]
 
     q_own, fq_own = query_features(q[0], q[1])
-    last, fq_own, fk = lax.optimization_barrier((last, fq_own, fk))
-    fk, past, step = call(
+    one, two, fq_own, fk = lax.optimization_barrier((one, two, fq_own, fk))
+    (far,) = call(
+        far_kernel,
+        [one, two, wk],
+        [(states, 2 * dh)],
+        "far",
+        [pltpu.VMEM((states, 4 * half), BF16)],
+        20,
+        F32,
+    )
+    q[2], q[3], far = lax.optimization_barrier((q[2], q[3], far))
+    q_other, fq_other = query_features(q[2], q[3])
+    three, fq_other = lax.optimization_barrier((three, fq_other))
+    fk, past, step, last = call(
         last_features_kernel,
-        [last, wk, fk],
-        [(states, 4 * half), (states, 2 * dh), (states, 2 * dh)],
+        [one, two, three, wk, far, fk],
+        [(states, 4 * half), (states, 2 * dh), (states, 2 * dh), kv.shape],
         "last_features",
-        limit=20,
-        out_type=[BF16, F32, F32],
-        aliases={2: 0},
+        limit=24,
+        out_type=[BF16, F32, F32, BF16],
+        aliases={5: 0},
     )
     near_own = near(0, q_own, fq_own)
-    q[2], q[3], near_own = lax.optimization_barrier((q[2], q[3], near_own))
-    q_other, fq_other = query_features(q[2], q[3])
     near_other = near(1, q_other, fq_other)
-    first, near_other = lax.optimization_barrier((first, near_other))
-    (past,) = call(
-        past_kernel,
-        [first, wk, past],
-        [(states, 2 * dh)],
-        "past",
-        [pltpu.VMEM((states, 2 * half), BF16)],
-        16,
-        F32,
-    )
-    before, past = lax.optimization_barrier((before, past))
     part = tok // sides
     outs = call(
         mix_kernel_of_level,
-        [near_own, near_other, fq_own, fq_other, past, step, wk, before],
+        [near_own, near_other, fq_own, fq_other, past, step, wk, three],
         [(part, heads * dh)] * (WAYS * sides),
         "mix_level",
         [

time: 42.1 us -> 47.6 us (1.13)
  the two profiles are of different devices: /device:TPU:27 before, /device:TPU:19 now
where the time goes in v3:
time: 47.6 us; the launch traced here: 47.4 us
  starting transfers between devices  17.9 us (38%)
  waiting for transfers between devices  15.8 us (33%)
  Pallas kernels  10.6 us (22%)
  local copies, waits for them, and re-layouts  2.76 us (6%)
    pallas_call x13, Pallas kernels, call(): pl.pallas_call(kernel, in_specs=[whole_spec() for _ in ins], out_specs=[w...  8.94 us
    ppermute x3, waiting for transfers between devices, along(): return lax.ppermute(x, 'seq', pairs)  7.92 us
    ppermute x7, waiting for transfers between devices, sent(): return lax.ppermute(x, ('seq', 'head'), pairs)  7.91 us
    ppermute x7, starting transfers between devices, sent(): return lax.ppermute(x, ('seq', 'head'), pairs)  7.34 us
    ppermute x3, starting transfers between devices, along(): return lax.ppermute(x, 'seq', pairs)  5.79 us
    ppermute x5, starting transfers between devices, partner(): return lax.ppermute(x, ('seq', 'head'), pairs)  4.82 us
    pallas_call x2, Pallas kernels, joined(): pl.pallas_call(lambda *refs: join_kernel(slots, *refs), in_specs=[whole_s...  1.63 us
    dynamic_slice x2, local copies, waits for them, and re-layouts, by_levels(): lax.dynamic_slice_in_dim(w, place * heads, heads)  0.99 us
  transfers between devices with their start and end apart: 15, of which 5 were waited for; matrix products, arithmetic and copies ran while one was open for 2% of the time, Pallas kernels for 9%

profile of v3, /device:TPU:19, one launch (start us, length us, event | category | flops | bytes accessed | tf_op | source)
XLA Modules:
  0.0 47.4 jit_solution(9699436040260558465)
XLA Ops:
  0.0 0.9 %constant_dynamic-slice_fusion.2 = (bf16[64,256]{1,0:T(8,128)(2,1)S(1)}, bf16[64,256]{1,0:T(8,128)(2,1)S(1)}, bf16[64,256]{1,0:T(8,128)(2,1)S(1)}, bf16[64,256]{1,0:T(8,128)(2,1)S(1)}) fusion(bf16[64,512]{1,0:T(8,128)(2,1)} %param.8, s32[]{:T(128)S(6)} %select_n.19, s32[]{:T(128)S(6)} %select_n.18, bf16[64,512]{1,0:T(8,128)(2,1)} %param.7), kind=kLoop, calls=%fused_computation.2 | loop fusion | bytes 262152 | tf_op jit(solution)/shard_map/dynamic_slice | solution.py:453
  1.0 0.3 collective-permute-start
  1.3 0.8 %copy-done.2 = bf16[64,8192]{1,0:T(8,128)(2,1)S(1)} copy-done((bf16[64,8192]{1,0:T(8,128)(2,1)S(1)}, bf16[64,8192]{1,0:T(8,128)(2,1)}, u32[]{:S(2)}) %copy-start.2) | copy-done | bytes 1048600
  2.2 0.4 collective-permute-start.6
  2.6 1.9 %collective-permute-start.7 = (bf16[64,2048]{1,0:T(8,128)(2,1)S(1)}, bf16[64,2048]{1,0:T(8,128)(2,1)S(1)}, u32[]{:S(2)}, u32[]{:S(2)}) collective-permute-start(bf16[64,2048]{1,0:T(8,128)(2,1)S(1)} %get-tuple-element.75), channel_id=1, source_target_pairs={{0,6},{1,7},{2,4},{3,5},{4,2},{5,3},{6,0},{7,1},{8,14},{9,15},{10,... | collective-permute-start | bytes 786440 | tf_op jit(solution)/shard_map/ppermute | solution.py:444
  4.6 2.0 %collective-permute-start.1 = (bf16[128,256]{1,0:T(8,128)(2,1)S(1)}, bf16[128,256]{1,0:T(8,128)(2,1)S(1)}, u32[]{:S(2)}, u32[]{:S(2)}) collective-permute-start(bf16[128,256]{1,0:T(8,128)(2,1)S(1)} %pair_kv.1), channel_id=1, source_target_pairs={{0,2},{1,3},{2,0},{3,1},{4,6},{5,7},{6,4},{7,5},{8,10},{9,11},{10,... | collective-permute-start | bytes 196616 | tf_op jit(solution)/shard_map/ppermute | solution.py:444
  6.8 1.0 %constant_dynamic-slice_fusion.wk_ref.refs_6_ = bf16[16,64,128]{2,1,0:T(8,128)(2,1)S(1)} fusion(bf16[64,64,128]{2,1,0:T(8,128)(2,1)} %bitcast.5, s32[]{:T(128)S(6)} %select_n.20), kind=kLoop, calls=%fused_computation | loop fusion | bytes 524292 | tf_op jit(solution)/shard_map/dynamic_slice | solution.py:465
  7.8 0.7 %collective-permute-start.3 = (bf16[256,256]{1,0:T(8,128)(2,1)S(1)}, bf16[256,256]{1,0:T(8,128)(2,1)S(1)}, u32[]{:S(2)}, u32[]{:S(2)}) collective-permute-start(bf16[256,256]{1,0:T(8,128)(2,1)S(1)} %stack_kv.1.own_ref.refs_3_), channel_id=1, source_target_pairs={{0,8},{2,10},{4,12},{6,14},{8,24},{10,26},{12,28},{14,30},{1,9},{3... | collective-permute-start | bytes 393224 | tf_op jit(solution)/shard_map/ppermute | solution.py:448
  8.5 1.3 %collective-permute-start.4 = (bf16[256,256]{1,0:T(8,128)(2,1)S(1)}, bf16[256,256]{1,0:T(8,128)(2,1)S(1)}, u32[]{:S(2)}, u32[]{:S(2)}) collective-permute-start(bf16[256,256]{1,0:T(8,128)(2,1)S(1)} %stack_kv.1.own_ref.refs_3_), channel_id=1, source_target_pairs={{0,24},{2,26},{4,28},{6,30},{8,16},{10,18},{12,20},{14,22},{1,25},... | collective-permute-start | bytes 393224 | tf_op jit(solution)/shard_map/ppermute | solution.py:448
  9.8 3.8 %collective-permute-start.5 = (bf16[256,256]{1,0:T(8,128)(2,1)S(1)}, bf16[256,256]{1,0:T(8,128)(2,1)S(1)}, u32[]{:S(2)}, u32[]{:S(2)}) collective-permute-start(bf16[256,256]{1,0:T(8,128)(2,1)S(1)} %stack_kv.1.own_ref.refs_3_), channel_id=1, source_target_pairs={{16,24},{18,26},{20,28},{22,30},{0,16},{2,18},{4,20},{6,22},{17,25... | collective-permute-start | bytes 393224 | tf_op jit(solution)/shard_map/ppermute | solution.py:448
  13.6 0.7 %own_features.1._ = bf16[2048,512]{1,0:T(8,128)(2,1)S(1)} custom-call(bf16[256,256]{1,0:T(8,128)(2,1)S(1)} %stack_kv.1.own_ref.refs_3_, bf16[16,64,128]{2,1,0:T(8,128)(2,1)S(1)} %constant_dynamic-slice_fusion.wk_ref.refs_6_), custom_call_target="tpu_custom_call" | custom-call | tf_op jit(solution)/shard_map/own_features/pallas_call | solution.py:414
  14.3 0.4 weights.1
  14.7 1.1 %query_features.2 = (bf16[2048,128]{1,0:T(8,128)(2,1)S(1)}, bf16[2048,128]{1,0:T(8,128)(2,1)S(1)}) custom-call(bf16[64,2048]{1,0:T(8,128)(2,1)S(1)} %get-tuple-element.54.a_ref, bf16[64,2048]{1,0:T(8,128)(2,1)S(1)} %collective-permute-done.2.b_ref, bf16[16,128,128]{2,1,0:T(8,128)(2,1)S(1)} %get-tuple-element.65.w_ref, f32[16,128]{1,0:T(8,128)S(1)} %get-tuple-element.66.ratio_ref), custom_call_target="tpu_custom_call" | custom-call | tf_op jit(solution)/shard_map/query_features/pallas_call | solution.py:414
  15.8 7.9 %collective-permute-done.4.two_ref = bf16[256,256]{1,0:T(8,128)(2,1)S(1)} collective-permute-done((bf16[256,256]{1,0:T(8,128)(2,1)S(1)}, bf16[256,256]{1,0:T(8,128)(2,1)S(1)}, u32[]{:S(2)}, u32[]{:S(2)}) %collective-permute-start.4) | collective-permute-done | bytes 131104 | tf_op jit(solution)/shard_map/ppermute | solution.py:448
  23.8 0.1 far.1.far_ref
  23.9 1.1 %query_features.3 = (bf16[2048,128]{1,0:T(8,128)(2,1)S(1)}, bf16[2048,128]{1,0:T(8,128)(2,1)S(1)}) custom-call(bf16[64,2048]{1,0:T(8,128)(2,1)S(1)} %collective-permute-done.6.a_ref, bf16[64,2048]{1,0:T(8,128)(2,1)S(1)} %collective-permute-done.7.b_ref, bf16[16,128,128]{2,1,0:T(8,128)(2,1)S(1)} %get-tuple-element.65.w_ref, ...), custom_call_target="tpu_custom_call" | custom-call | tf_op jit(solution)/shard_map/query_features/pallas_call | solution.py:414
  25.1 1.4 %last_features.1 = (bf16[2048,512]{1,0:T(8,128)(2,1)S(1)}, f32[2048,256]{1,0:T(8,128)S(1)}, f32[2048,256]{1,0:T(8,128)S(1)}, bf16[256,256]{1,0:T(8,128)(2,1)S(1)}) custom-call(bf16[256,256]{1,0:T(8,128)(2,1)S(1)} %collective-permute-done.3.one_ref, bf16[256,256]{1,0:T(8,128)(2,1)S(1)} %collective-permute-done.4.two_ref, ...), custom_call_target="tpu_custom_call", output_to_operand_aliasing={{0}: (5, {})} | custom-call | tf_op jit(solution)/shard_map/last_features/pallas_call | solution.py:414
  26.4 1.1 %near.3.refs_1_ = f32[2048,256]{1,0:T(8,128)S(1)} custom-call(bf16[2048,128]{1,0:T(8,128)(2,1)S(1)} %get-tuple-element.84.refs_0_, bf16[2048,128]{1,0:T(8,128)(2,1)S(1)} %get-tuple-element.85.refs_1_.refs_3_, bf16[256,256]{1,0:T(8,128)(2,1)S(1)} %get-tuple-element.82.refs_2_, bf16[256,256]{1,0:T(8,128)(2,1)S(1)} %stack_kv.1.own_ref.refs_3_, ...), custom_call_target="tpu_custom_call" | custom-call | tf_op jit(solution)/shard_map/near/pallas_call | solution.py:414
  27.5 1.1 %near.2.refs_0_ = f32[2048,256]{1,0:T(8,128)S(1)} custom-call(bf16[2048,128]{1,0:T(8,128)(2,1)S(1)} %get-tuple-element.67.refs_0_, bf16[2048,128]{1,0:T(8,128)(2,1)S(1)} %get-tuple-element.71.refs_1_.refs_2_, bf16[256,256]{1,0:T(8,128)(2,1)S(1)} %get-tuple-element.82.refs_2_, bf16[256,256]{1,0:T(8,128)(2,1)S(1)} %stack_kv.1.own_ref.refs_3_, ...), custom_call_target="tpu_custom_call" | custom-call | tf_op jit(solution)/shard_map/near/pallas_call | solution.py:414
  28.6 1.8 %mix_level.1 = (bf16[32,2048]{1,0:T(8,128)(2,1)S(1)}, bf16[32,2048]{1,0:T(8,128)(2,1)S(1)}, bf16[32,2048]{1,0:T(8,128)(2,1)S(1)}, bf16[32,2048]{1,0:T(8,128)(2,1...) custom-call(f32[2048,256]{1,0:T(8,128)S(1)} %near.2.refs_0_, ...), custom_call_target="tpu_custom_call" | custom-call | tf_op jit(solution)/shard_map/mix_level/pallas_call | solution.py:414
  30.4 1.3 %collective-permute-start.10 = (bf16[32,2048]{1,0:T(8,128)(2,1)S(1)}, bf16[32,2048]{1,0:T(8,128)(2,1)S(1)}, u32[]{:S(2)}, u32[]{:S(2)}) collective-permute-start(bf16[32,2048]{1,0:T(8,128)(2,1)S(1)} %get-tuple-element.92), channel_id=1, source_target_pairs={{0,2},{1,3},{2,0},{3,1},{4,6},{5,7},{6,4},{7,5},{8,10},{9,11},{10,... | collective-permute-start | bytes 393224 | tf_op jit(solution)/shard_map/ppermute | solution.py:550
  31.8 1.2 %collective-permute-start.13 = (bf16[32,2048]{1,0:T(8,128)(2,1)S(1)}, bf16[32,2048]{1,0:T(8,128)(2,1)S(1)}, u32[]{:S(2)}, u32[]{:S(2)}) collective-permute-start(bf16[32,2048]{1,0:T(8,128)(2,1)S(1)} %get-tuple-element.96), channel_id=1, source_target_pairs={{0,4},{1,5},{2,3},{3,2},{4,0},{5,1},{6,7},{7,6},{8,12},{9,13},{10,... | collective-permute-start | bytes 393224 | tf_op jit(solution)/shard_map/ppermute | solution.py:550
  33.1 1.9 %collective-permute-start.9 = (bf16[32,2048]{1,0:T(8,128)(2,1)S(1)}, bf16[32,2048]{1,0:T(8,128)(2,1)S(1)}, u32[]{:S(2)}, u32[]{:S(2)}) collective-permute-start(bf16[32,2048]{1,0:T(8,128)(2,1)S(1)} %get-tuple-element.89), channel_id=1, source_target_pairs={{0,6},{1,7},{2,1},{3,0},{4,2},{5,3},{6,5},{7,4},{8,14},{9,15},{10,... | collective-permute-start | bytes 393224 | tf_op jit(solution)/shard_map/ppermute | solution.py:550
  34.9 0.1 collective-permute-start.14
  35.1 1.3 %collective-permute-start.11 = (bf16[32,2048]{1,0:T(8,128)(2,1)S(1)}, bf16[32,2048]{1,0:T(8,128)(2,1)S(1)}, u32[]{:S(2)}, u32[]{:S(2)}) collective-permute-start(bf16[32,2048]{1,0:T(8,128)(2,1)S(1)} %get-tuple-element.93), channel_id=1, source_target_pairs={{0,7},{1,6},{2,5},{3,4},{4,3},{5,2},{6,1},{7,0},{8,15},{9,14},{10,... | collective-permute-start | bytes 393224 | tf_op jit(solution)/shard_map/ppermute | solution.py:550
  36.4 1.4 %collective-permute-start.12 = (bf16[32,2048]{1,0:T(8,128)(2,1)S(1)}, bf16[32,2048]{1,0:T(8,128)(2,1)S(1)}, u32[]{:S(2)}, u32[]{:S(2)}) collective-permute-start(bf16[32,2048]{1,0:T(8,128)(2,1)S(1)} %get-tuple-element.94), channel_id=1, source_target_pairs={{0,3},{1,2},{2,4},{3,5},{4,7},{5,6},{6,0},{7,1},{8,11},{9,10},{10,... | collective-permute-start | bytes 393224 | tf_op jit(solution)/shard_map/ppermute | solution.py:550
  37.8 3.4 %collective-permute-done.14.refs_2_ = bf16[32,2048]{1,0:T(8,128)(2,1)S(1)} collective-permute-done((bf16[32,2048]{1,0:T(8,128)(2,1)S(1)}, bf16[32,2048]{1,0:T(8,128)(2,1)S(1)}, u32[]{:S(2)}, u32[]{:S(2)}) %collective-permute-start.14) | collective-permute-done | bytes 131104 | tf_op jit(solution)/shard_map/ppermute | solution.py:550
  41.2 0.8 %join.2.refs_4_ = bf16[32,16384]{1,0:T(8,128)(2,1)} custom-call(bf16[32,2048]{1,0:T(8,128)(2,1)S(1)} %get-tuple-element.95.refs_0_, bf16[32,2048]{1,0:T(8,128)(2,1)S(1)} %collective-permute-done.13.refs_1_, bf16[32,2048]{1,0:T(8,128)(2,1)S(1)} %collective-permute-done.14.refs_2_, bf16[32,2048]{1,0:T(8,128)(2,1)S(1)} %collective-permute-done.10.refs_3_), custom_call_target="tpu_custom_call" | custom-call | tf_op jit(solution)/shard_map/join/pallas_call | solution.py:559
  42.1 0.8 %collective-permute-done.9.refs_1_ = bf16[32,2048]{1,0:T(8,128)(2,1)S(1)} collective-permute-done((bf16[32,2048]{1,0:T(8,128)(2,1)S(1)}, bf16[32,2048]{1,0:T(8,128)(2,1)S(1)}, u32[]{:S(2)}, u32[]{:S(2)}) %collective-permute-start.9) | collective-permute-done | bytes 131104 | tf_op jit(solution)/shard_map/ppermute | solution.py:550
  42.8 3.6 %collective-permute-done.11.refs_2_ = bf16[32,2048]{1,0:T(8,128)(2,1)S(1)} collective-permute-done((bf16[32,2048]{1,0:T(8,128)(2,1)S(1)}, bf16[32,2048]{1,0:T(8,128)(2,1)S(1)}, u32[]{:S(2)}, u32[]{:S(2)}) %collective-permute-start.11) | collective-permute-done | bytes 131104 | tf_op jit(solution)/shard_map/ppermute | solution.py:550
  46.4 0.1 collective-permute-done.12.refs_3_
  46.5 0.8 %join.3 = bf16[32,16384]{1,0:T(8,128)(2,1)} custom-call(bf16[32,2048]{1,0:T(8,128)(2,1)S(1)} %collective-permute-done.8.refs_0_, bf16[32,2048]{1,0:T(8,128)(2,1)S(1)} %collective-permute-done.9.refs_1_, bf16[32,2048]{1,0:T(8,128)(2,1)S(1)} %collective-permute-done.11.refs_2_, ...), custom_call_target="tpu_custom_call", output_to_operand_aliasing={{}: (4, {})} | custom-call | tf_op jit(solution)/shard_map/join/pallas_call | solution.py:559
  (22 shorter events, 0.4 us)
Async XLA Ops:
  0.0 4.6 %copy-start = (bf16[64,128,64]{1,2,0:T(8,128)(2,1)S(1)}, bf16[64,128,64]{1,2,0:T(8,128)(2,1)}, u32[]{:S(2)}) copy-start(bf16[64,128,64]{1,2,0:T(8,128)(2,1)} %param.9) | copy-start | bytes 3145732
  0.9 1.2 %copy-start.2 = (bf16[64,8192]{1,0:T(8,128)(2,1)S(1)}, bf16[64,8192]{1,0:T(8,128)(2,1)}, u32[]{:S(2)}) copy-start(bf16[64,8192]{1,0:T(8,128)(2,1)} %q_ref) | copy-start | bytes 3145732
  1.0 3.6 %collective-permute-start = (bf16[64,512]{1,0:T(8,128)(2,1)S(1)}, bf16[64,512]{1,0:T(8,128)(2,1)S(1)}, u32[]{:S(2)}, u32[]{:S(2)}) collective-permute-start(bf16[64,512]{1,0:T(8,128)(2,1)S(1)} %get-tuple-element.52), channel_id=1, source_target_pairs={{0,4},{1,5},{2,6},{3,7},{4,0},{5,1},{6,2},{7,3},{8,12},{9,13},{10,... | collective-permute-start | bytes 196616 | tf_op jit(solution)/shard_map/ppermute | solution.py:444
  2.2 21.7 %collective-permute-start.6 = (bf16[64,2048]{1,0:T(8,128)(2,1)S(1)}, bf16[64,2048]{1,0:T(8,128)(2,1)S(1)}, u32[]{:S(2)}, u32[]{:S(2)}) collective-permute-start(bf16[64,2048]{1,0:T(8,128)(2,1)S(1)} %get-tuple-element.74), channel_id=1, source_target_pairs={{0,4},{1,5},{2,6},{3,7},{4,0},{5,1},{6,2},{7,3},{8,12},{9,13},{10,... | collective-permute-start | bytes 786440 | tf_op jit(solution)/shard_map/ppermute | solution.py:444
  2.6 21.3 %collective-permute-start.7 = (bf16[64,2048]{1,0:T(8,128)(2,1)S(1)}, bf16[64,2048]{1,0:T(8,128)(2,1)S(1)}, u32[]{:S(2)}, u32[]{:S(2)}) collective-permute-start(bf16[64,2048]{1,0:T(8,128)(2,1)S(1)} %get-tuple-element.75), channel_id=1, source_target_pairs={{0,6},{1,7},{2,4},{3,5},{4,2},{5,3},{6,0},{7,1},{8,14},{9,15},{10,... | collective-permute-start | bytes 786440 | tf_op jit(solution)/shard_map/ppermute | solution.py:444
  4.6 3.1 %collective-permute-start.1 = (bf16[128,256]{1,0:T(8,128)(2,1)S(1)}, bf16[128,256]{1,0:T(8,128)(2,1)S(1)}, u32[]{:S(2)}, u32[]{:S(2)}) collective-permute-start(bf16[128,256]{1,0:T(8,128)(2,1)S(1)} %pair_kv.1), channel_id=1, source_target_pairs={{0,2},{1,3},{2,0},{3,1},{4,6},{5,7},{6,4},{7,5},{8,10},{9,11},{10,... | collective-permute-start | bytes 196616 | tf_op jit(solution)/shard_map/ppermute | solution.py:444
  6.7 1.8 %collective-permute-start.2 = (bf16[64,2048]{1,0:T(8,128)(2,1)S(1)}, bf16[64,2048]{1,0:T(8,128)(2,1)S(1)}, u32[]{:S(2)}, u32[]{:S(2)}) collective-permute-start(bf16[64,2048]{1,0:T(8,128)(2,1)S(1)} %get-tuple-element.62), channel_id=1, source_target_pairs={{0,2},{1,3},{2,0},{3,1},{4,6},{5,7},{6,4},{7,5},{8,10},{9,11},{10,... | collective-permute-start | bytes 786440 | tf_op jit(solution)/shard_map/ppermute | solution.py:444
  7.8 6.5 %copy-start.1 = (f32[64]{0:T(128)S(1)}, f32[64]{0:T(128)}, u32[]{:S(2)}) copy-start(f32[64]{0:T(128)} %param.11) | copy-start | bytes 772
  7.8 8.0 %collective-permute-start.3 = (bf16[256,256]{1,0:T(8,128)(2,1)S(1)}, bf16[256,256]{1,0:T(8,128)(2,1)S(1)}, u32[]{:S(2)}, u32[]{:S(2)}) collective-permute-start(bf16[256,256]{1,0:T(8,128)(2,1)S(1)} %stack_kv.1.own_ref.refs_3_), channel_id=1, source_target_pairs={{0,8},{2,10},{4,12},{6,14},{8,24},{10,26},{12,28},{14,30},{1,9},{3... | collective-permute-start | bytes 393224 | tf_op jit(solution)/shard_map/ppermute | solution.py:448
  8.5 15.3 %collective-permute-start.4 = (bf16[256,256]{1,0:T(8,128)(2,1)S(1)}, bf16[256,256]{1,0:T(8,128)(2,1)S(1)}, u32[]{:S(2)}, u32[]{:S(2)}) collective-permute-start(bf16[256,256]{1,0:T(8,128)(2,1)S(1)} %stack_kv.1.own_ref.refs_3_), channel_id=1, source_target_pairs={{0,24},{2,26},{4,28},{6,30},{8,16},{10,18},{12,20},{14,22},{1,25},... | collective-permute-start | bytes 393224 | tf_op jit(solution)/shard_map/ppermute | solution.py:448
  9.8 15.3 %collective-permute-start.5 = (bf16[256,256]{1,0:T(8,128)(2,1)S(1)}, bf16[256,256]{1,0:T(8,128)(2,1)S(1)}, u32[]{:S(2)}, u32[]{:S(2)}) collective-permute-start(bf16[256,256]{1,0:T(8,128)(2,1)S(1)} %stack_kv.1.own_ref.refs_3_), channel_id=1, source_target_pairs={{16,24},{18,26},{20,28},{22,30},{0,16},{2,18},{4,20},{6,22},{17,25... | collective-permute-start | bytes 393224 | tf_op jit(solution)/shard_map/ppermute | solution.py:448
  30.4 4.6 %collective-permute-start.10 = (bf16[32,2048]{1,0:T(8,128)(2,1)S(1)}, bf16[32,2048]{1,0:T(8,128)(2,1)S(1)}, u32[]{:S(2)}, u32[]{:S(2)}) collective-permute-start(bf16[32,2048]{1,0:T(8,128)(2,1)S(1)} %get-tuple-element.92), channel_id=1, source_target_pairs={{0,2},{1,3},{2,0},{3,1},{4,6},{5,7},{6,4},{7,5},{8,10},{9,11},{10,... | collective-permute-start | bytes 393224 | tf_op jit(solution)/shard_map/ppermute | solution.py:550
  31.8 4.6 %collective-permute-start.13 = (bf16[32,2048]{1,0:T(8,128)(2,1)S(1)}, bf16[32,2048]{1,0:T(8,128)(2,1)S(1)}, u32[]{:S(2)}, u32[]{:S(2)}) collective-permute-start(bf16[32,2048]{1,0:T(8,128)(2,1)S(1)} %get-tuple-element.96), channel_id=1, source_target_pairs={{0,4},{1,5},{2,3},{3,2},{4,0},{5,1},{6,7},{7,6},{8,12},{9,13},{10,... | collective-permute-start | bytes 393224 | tf_op jit(solution)/shard_map/ppermute | solution.py:550
  33.0 9.0 %collective-permute-start.8 = (bf16[32,2048]{1,0:T(8,128)(2,1)S(1)}, bf16[32,2048]{1,0:T(8,128)(2,1)S(1)}, u32[]{:S(2)}, u32[]{:S(2)}) collective-permute-start(bf16[32,2048]{1,0:T(8,128)(2,1)S(1)} %get-tuple-element.88), channel_id=1, source_target_pairs={{0,5},{1,4},{2,7},{3,6},{4,1},{5,0},{6,3},{7,2},{8,13},{9,12},{10,... | collective-permute-start | bytes 393224 | tf_op jit(solution)/shard_map/ppermute | solution.py:550
  33.1 9.8 %collective-permute-start.9 = (bf16[32,2048]{1,0:T(8,128)(2,1)S(1)}, bf16[32,2048]{1,0:T(8,128)(2,1)S(1)}, u32[]{:S(2)}, u32[]{:S(2)}) collective-permute-start(bf16[32,2048]{1,0:T(8,128)(2,1)S(1)} %get-tuple-element.89), channel_id=1, source_target_pairs={{0,6},{1,7},{2,1},{3,0},{4,2},{5,3},{6,5},{7,4},{8,14},{9,15},{10,... | collective-permute-start | bytes 393224 | tf_op jit(solution)/shard_map/ppermute | solution.py:550
  34.9 6.3 %collective-permute-start.14 = (bf16[32,2048]{1,0:T(8,128)(2,1)S(1)}, bf16[32,2048]{1,0:T(8,128)(2,1)S(1)}, u32[]{:S(2)}, u32[]{:S(2)}) collective-permute-start(bf16[32,2048]{1,0:T(8,128)(2,1)S(1)} %get-tuple-element.97), channel_id=1, source_target_pairs={{0,1},{1,0},{2,6},{3,7},{4,5},{5,4},{6,2},{7,3},{8,9},{9,8},{10,14... | collective-permute-start | bytes 393224 | tf_op jit(solution)/shard_map/ppermute | solution.py:550
  35.1 11.3 %collective-permute-start.11 = (bf16[32,2048]{1,0:T(8,128)(2,1)S(1)}, bf16[32,2048]{1,0:T(8,128)(2,1)S(1)}, u32[]{:S(2)}, u32[]{:S(2)}) collective-permute-start(bf16[32,2048]{1,0:T(8,128)(2,1)S(1)} %get-tuple-element.93), channel_id=1, source_target_pairs={{0,7},{1,6},{2,5},{3,4},{4,3},{5,2},{6,1},{7,0},{8,15},{9,14},{10,... | collective-permute-start | bytes 393224 | tf_op jit(solution)/shard_map/ppermute | solution.py:550
  36.4 10.2 %collective-permute-start.12 = (bf16[32,2048]{1,0:T(8,128)(2,1)S(1)}, bf16[32,2048]{1,0:T(8,128)(2,1)S(1)}, u32[]{:S(2)}, u32[]{:S(2)}) collective-permute-start(bf16[32,2048]{1,0:T(8,128)(2,1)S(1)} %get-tuple-element.94), channel_id=1, source_target_pairs={{0,3},{1,2},{2,4},{3,5},{4,7},{5,6},{6,0},{7,1},{8,11},{9,10},{10,... | collective-permute-start | bytes 393224 | tf_op jit(solution)/shard_map/ppermute | solution.py:550

commit v4 on v2

--- a/solution.py
+++ b/solution.py
@@ -132,13 +132,13 @@
 
 SLOTS = (
     ((0, 0), (0, 0)),
+    ((2, 1), (2, 1)),
     ((2, 0), (0, 1)),
     ((0, 1), (2, 0)),
+    ((3, 1), (3, 1)),
+    ((3, 0), (1, 1)),
+    ((1, 1), (3, 0)),
     ((1, 0), (1, 0)),
-    ((2, 1), (2, 1)),
-    ((3, 0), (1, 1)),
-    ((3, 1), (3, 1)),
-    ((1, 1), (3, 0)),
 )
 
 
@@ -539,7 +539,7 @@
     outs = list(outs)
     for n in range(1, 6):
         outs[n] = sent(outs[n], SLOTS[n])
-    outs[6], outs[7], outs[3] = lax.optimization_barrier((outs[6], outs[7], outs[3]))
+    outs[6], outs[7], outs[1] = lax.optimization_barrier((outs[6], outs[7], outs[1]))
     outs[6], outs[7] = sent(outs[6], SLOTS[6]), sent(outs[7], SLOTS[7])
 
     def joined(slots, into):

time: 42.1 us -> 41.4 us (0.983)
  waiting for transfers between devices: 11.9 us -> 9.66 us
  starting transfers between devices: 15.6 us -> 17.2 us
    ppermute x7, waiting for transfers between devices: 7.67 us -> 5.42 us  [sent(): return lax.ppermute(x, ('seq', 'head'), pairs)]
    ppermute x7, starting transfers between devices: 6.93 us -> 8.49 us  [sent(): return lax.ppermute(x, ('seq', 'head'), pairs)]
where the time goes in v4:
time: 41.4 us; the launch traced here: 41.2 us
  starting transfers between devices  17.2 us (42%)
  Pallas kernels  11.4 us (28%)
  waiting for transfers between devices  9.66 us (23%)
  local copies, waits for them, and re-layouts  2.76 us (7%)
    pallas_call x13, Pallas kernels, call(): pl.pallas_call(kernel, in_specs=[whole_spec() for _ in ins], out_specs=[w...  9.75 us
    ppermute x7, starting transfers between devices, sent(): return lax.ppermute(x, ('seq', 'head'), pairs)  8.49 us
    ppermute x7, waiting for transfers between devices, sent(): return lax.ppermute(x, ('seq', 'head'), pairs)  5.42 us
    ppermute x5, starting transfers between devices, partner(): return lax.ppermute(x, ('seq', 'head'), pairs)  4.82 us
    ppermute x3, waiting for transfers between devices, levels_back(): return lax.ppermute(x, 'seq', pairs)  4.15 us
    ppermute x3, starting transfers between devices, levels_back(): return lax.ppermute(x, 'seq', pairs)  3.88 us
    pallas_call x2, Pallas kernels, joined(): pl.pallas_call(lambda *refs: join_kernel(slots, *refs), in_specs=[whole_s...  1.64 us
    dynamic_slice x2, local copies, waits for them, and re-layouts, by_levels(): lax.dynamic_slice_in_dim(w, place * heads, heads)  0.99 us
  transfers between devices with their start and end apart: 15, of which 7 were waited for; matrix products, arithmetic and copies ran while one was open for 2% of the time, Pallas kernels for 21%

profile of v4, /device:TPU:27, one launch (start us, length us, event | category | flops | bytes accessed | tf_op | source)
XLA Modules:
  0.0 41.2 jit_solution(15599077017931351840)
XLA Ops:
  0.0 0.9 %constant_dynamic-slice_fusion.2 = (bf16[64,256]{1,0:T(8,128)(2,1)S(1)}, bf16[64,256]{1,0:T(8,128)(2,1)S(1)}, bf16[64,256]{1,0:T(8,128)(2,1)S(1)}, bf16[64,256]{1,0:T(8,128)(2,1)S(1)}) fusion(bf16[64,512]{1,0:T(8,128)(2,1)} %param.8, s32[]{:T(128)S(6)} %select_n.19, s32[]{:T(128)S(6)} %select_n.18, bf16[64,512]{1,0:T(8,128)(2,1)} %param.7), kind=kLoop, calls=%fused_computation.2 | loop fusion | bytes 262152 | tf_op jit(solution)/shard_map/dynamic_slice | solution.py:440
  1.0 0.3 collective-permute-start.2
  1.3 0.8 %copy-done.2 = bf16[64,8192]{1,0:T(8,128)(2,1)S(1)} copy-done((bf16[64,8192]{1,0:T(8,128)(2,1)S(1)}, bf16[64,8192]{1,0:T(8,128)(2,1)}, u32[]{:S(2)}) %copy-start.2) | copy-done | bytes 1048600
  2.2 0.4 %collective-permute-start = (bf16[64,2048]{1,0:T(8,128)(2,1)S(1)}, bf16[64,2048]{1,0:T(8,128)(2,1)S(1)}, u32[]{:S(2)}, u32[]{:S(2)}) collective-permute-start(bf16[64,2048]{1,0:T(8,128)(2,1)S(1)} %get-tuple-element.54), channel_id=1, source_target_pairs={{0,4},{1,5},{2,6},{3,7},{4,0},{5,1},{6,2},{7,3},{8,12},{9,13},{10,... | collective-permute-start | bytes 786440 | tf_op jit(solution)/shard_map/ppermute | solution.py:431
  2.6 1.9 %collective-permute-start.1 = (bf16[64,2048]{1,0:T(8,128)(2,1)S(1)}, bf16[64,2048]{1,0:T(8,128)(2,1)S(1)}, u32[]{:S(2)}, u32[]{:S(2)}) collective-permute-start(bf16[64,2048]{1,0:T(8,128)(2,1)S(1)} %get-tuple-element.55), channel_id=1, source_target_pairs={{0,6},{1,7},{2,4},{3,5},{4,2},{5,3},{6,0},{7,1},{8,14},{9,15},{10,... | collective-permute-start | bytes 786440 | tf_op jit(solution)/shard_map/ppermute | solution.py:431
  4.6 2.0 %collective-permute-start.3 = (bf16[128,256]{1,0:T(8,128)(2,1)S(1)}, bf16[128,256]{1,0:T(8,128)(2,1)S(1)}, u32[]{:S(2)}, u32[]{:S(2)}) collective-permute-start(bf16[128,256]{1,0:T(8,128)(2,1)S(1)} %pair_kv.1), channel_id=1, source_target_pairs={{0,2},{1,3},{2,0},{3,1},{4,6},{5,7},{6,4},{7,5},{8,10},{9,11},{10,... | collective-permute-start | bytes 196616 | tf_op jit(solution)/shard_map/ppermute | solution.py:431
  6.8 1.0 %constant_dynamic-slice_fusion.1.wq_ref = bf16[16,64,128]{2,1,0:T(8,128)(2,1)S(1)} fusion(bf16[64,64,128]{2,1,0:T(8,128)(2,1)} %bitcast.5, s32[]{:T(128)S(6)} %select_n.20), kind=kLoop, calls=%fused_computation.1 | loop fusion | bytes 524292 | tf_op jit(solution)/shard_map/dynamic_slice | solution.py:452
  7.8 1.3 %collective-permute-start.5 = (bf16[256,256]{1,0:T(8,128)(2,1)S(1)}, bf16[256,256]{1,0:T(8,128)(2,1)S(1)}, u32[]{:S(2)}, u32[]{:S(2)}) collective-permute-start(bf16[256,256]{1,0:T(8,128)(2,1)S(1)} %stack_kv.1.own_ref.refs_3_), channel_id=1, source_target_pairs={{0,8},{2,10},{4,12},{6,14},{8,16},{10,18},{12,20},{14,22},{16,24},... | collective-permute-start | bytes 393224 | tf_op jit(solution)/shard_map/ppermute | solution.py:435
  9.1 1.3 %collective-permute-start.6 = (bf16[256,256]{1,0:T(8,128)(2,1)S(1)}, bf16[256,256]{1,0:T(8,128)(2,1)S(1)}, u32[]{:S(2)}, u32[]{:S(2)}) collective-permute-start(bf16[256,256]{1,0:T(8,128)(2,1)S(1)} %stack_kv.1.own_ref.refs_3_), channel_id=1, source_target_pairs={{0,24},{2,26},{4,28},{6,30},{1,25},{3,27},{5,29},{7,31}} | collective-permute-start | bytes 393224 | tf_op jit(solution)/shard_map/ppermute | solution.py:435
  10.4 1.3 %collective-permute-start.7 = (bf16[256,256]{1,0:T(8,128)(2,1)S(1)}, bf16[256,256]{1,0:T(8,128)(2,1)S(1)}, u32[]{:S(2)}, u32[]{:S(2)}) collective-permute-start(bf16[256,256]{1,0:T(8,128)(2,1)S(1)} %stack_kv.1.own_ref.refs_3_), channel_id=1, source_target_pairs={{0,16},{2,18},{4,20},{6,22},{8,24},{10,26},{12,28},{14,30},{1,17},... | collective-permute-start | bytes 393224 | tf_op jit(solution)/shard_map/ppermute | solution.py:435
  11.7 0.7 %own_features.1._ = bf16[2048,512]{1,0:T(8,128)(2,1)S(1)} custom-call(bf16[256,256]{1,0:T(8,128)(2,1)S(1)} %stack_kv.1.own_ref.refs_3_, bf16[16,64,128]{2,1,0:T(8,128)(2,1)S(1)} %constant_dynamic-slice_fusion.wk_ref.refs_6_), custom_call_target="tpu_custom_call" | custom-call | tf_op jit(solution)/shard_map/own_features/pallas_call | solution.py:401
  12.4 0.4 weights.1
  12.8 1.1 %query_features.2 = (bf16[2048,128]{1,0:T(8,128)(2,1)S(1)}, bf16[2048,128]{1,0:T(8,128)(2,1)S(1)}) custom-call(bf16[64,2048]{1,0:T(8,128)(2,1)S(1)} %get-tuple-element.56.a_ref, bf16[64,2048]{1,0:T(8,128)(2,1)S(1)} %collective-permute-done.4.b_ref, bf16[16,128,128]{2,1,0:T(8,128)(2,1)S(1)} %get-tuple-element.67.w_ref, f32[16,128]{1,0:T(8,128)S(1)} %get-tuple-element.68.ratio_ref), custom_call_target="tpu_custom_call" | custom-call | tf_op jit(solution)/shard_map/query_features/pallas_call | solution.py:401
  13.9 0.4 collective-permute-done.5.last_ref.refs_2_
  14.3 1.3 %last_features.1 = (bf16[2048,512]{1,0:T(8,128)(2,1)S(1)}, f32[2048,256]{1,0:T(8,128)S(1)}, f32[2048,256]{1,0:T(8,128)S(1)}) custom-call(bf16[256,256]{1,0:T(8,128)(2,1)S(1)} %collective-permute-done.5.last_ref.refs_2_, bf16[16,64,128]{2,1,0:T(8,128)(2,1)S(1)} %constant_dynamic-slice_fusion.wk_ref.refs_6_, ...), custom_call_target="tpu_custom_call", output_to_operand_aliasing={{0}: (2, {})} | custom-call | tf_op jit(solution)/shard_map/last_features/pallas_call | solution.py:401
  15.6 1.1 %near.2.refs_0_ = f32[2048,256]{1,0:T(8,128)S(1)} custom-call(bf16[2048,128]{1,0:T(8,128)(2,1)S(1)} %get-tuple-element.69.refs_0_, bf16[2048,128]{1,0:T(8,128)(2,1)S(1)} %get-tuple-element.73.refs_1_.refs_2_, bf16[256,256]{1,0:T(8,128)(2,1)S(1)} %collective-permute-done.5.last_ref.refs_2_, bf16[256,256]{1,0:T(8,128)(2,1)S(1)} %stack_kv.1.own_ref.refs_3_, ...), custom_call_target="tpu_custom_call" | custom-call | tf_op jit(solution)/shard_map/near/pallas_call | solution.py:401
  16.8 1.1 %query_features.3 = (bf16[2048,128]{1,0:T(8,128)(2,1)S(1)}, bf16[2048,128]{1,0:T(8,128)(2,1)S(1)}) custom-call(bf16[64,2048]{1,0:T(8,128)(2,1)S(1)} %collective-permute-done.a_ref, bf16[64,2048]{1,0:T(8,128)(2,1)S(1)} %collective-permute-done.1.b_ref, bf16[16,128,128]{2,1,0:T(8,128)(2,1)S(1)} %get-tuple-element.67.w_ref, ...), custom_call_target="tpu_custom_call" | custom-call | tf_op jit(solution)/shard_map/query_features/pallas_call | solution.py:401
  18.0 1.1 %near.3.refs_1_ = f32[2048,256]{1,0:T(8,128)S(1)} custom-call(bf16[2048,128]{1,0:T(8,128)(2,1)S(1)} %get-tuple-element.80.refs_0_, bf16[2048,128]{1,0:T(8,128)(2,1)S(1)} %get-tuple-element.81.refs_1_.refs_3_, bf16[256,256]{1,0:T(8,128)(2,1)S(1)} %collective-permute-done.5.last_ref.refs_2_, bf16[256,256]{1,0:T(8,128)(2,1)S(1)} %stack_kv.1.own_ref.refs_3_, ...), custom_call_target="tpu_custom_call" | custom-call | tf_op jit(solution)/shard_map/near/pallas_call | solution.py:401
  19.1 1.0 %past.1.refs_4_ = f32[2048,256]{1,0:T(8,128)S(1)} custom-call(bf16[256,256]{1,0:T(8,128)(2,1)S(1)} %collective-permute-done.6.first_ref, bf16[16,64,128]{2,1,0:T(8,128)(2,1)S(1)} %constant_dynamic-slice_fusion.wk_ref.refs_6_, f32[2048,256]{1,0:T(8,128)S(1)} %get-tuple-element.84.sum_ref), custom_call_target="tpu_custom_call" | custom-call | tf_op jit(solution)/shard_map/past/pallas_call | solution.py:401
  20.1 3.8 %collective-permute-done.7.refs_7_ = bf16[256,256]{1,0:T(8,128)(2,1)S(1)} collective-permute-done((bf16[256,256]{1,0:T(8,128)(2,1)S(1)}, bf16[256,256]{1,0:T(8,128)(2,1)S(1)}, u32[]{:S(2)}, u32[]{:S(2)}) %collective-permute-start.7) | collective-permute-done | bytes 131104 | tf_op jit(solution)/shard_map/ppermute | solution.py:435
  23.8 1.8 %mix_level.1 = (bf16[32,2048]{1,0:T(8,128)(2,1)S(1)}, bf16[32,2048]{1,0:T(8,128)(2,1)S(1)}, bf16[32,2048]{1,0:T(8,128)(2,1)S(1)}, bf16[32,2048]{1,0:T(8,128)(2,1...) custom-call(f32[2048,256]{1,0:T(8,128)S(1)} %near.2.refs_0_, ...), custom_call_target="tpu_custom_call" | custom-call | tf_op jit(solution)/shard_map/mix_level/pallas_call | solution.py:401
  25.6 1.2 %collective-permute-start.10 = (bf16[32,2048]{1,0:T(8,128)(2,1)S(1)}, bf16[32,2048]{1,0:T(8,128)(2,1)S(1)}, u32[]{:S(2)}, u32[]{:S(2)}) collective-permute-start(bf16[32,2048]{1,0:T(8,128)(2,1)S(1)} %get-tuple-element.92), channel_id=1, source_target_pairs={{0,5},{1,4},{2,7},{3,6},{4,1},{5,0},{6,3},{7,2},{8,13},{9,12},{10,... | collective-permute-start | bytes 393224 | tf_op jit(solution)/shard_map/ppermute | solution.py:537
  27.0 1.3 %collective-permute-start.14 = (bf16[32,2048]{1,0:T(8,128)(2,1)S(1)}, bf16[32,2048]{1,0:T(8,128)(2,1)S(1)}, u32[]{:S(2)}, u32[]{:S(2)}) collective-permute-start(bf16[32,2048]{1,0:T(8,128)(2,1)S(1)} %get-tuple-element.98), channel_id=1, source_target_pairs={{0,1},{1,0},{2,6},{3,7},{4,5},{5,4},{6,2},{7,3},{8,9},{9,8},{10,14... | collective-permute-start | bytes 393224 | tf_op jit(solution)/shard_map/ppermute | solution.py:537
  28.3 2.3 %collective-permute-start.8 = (bf16[32,2048]{1,0:T(8,128)(2,1)S(1)}, bf16[32,2048]{1,0:T(8,128)(2,1)S(1)}, u32[]{:S(2)}, u32[]{:S(2)}) collective-permute-start(bf16[32,2048]{1,0:T(8,128)(2,1)S(1)} %get-tuple-element.88), channel_id=1, source_target_pairs={{0,7},{1,6},{2,5},{3,4},{4,3},{5,2},{6,1},{7,0},{8,15},{9,14},{10,... | collective-permute-start | bytes 393224 | tf_op jit(solution)/shard_map/ppermute | solution.py:537
  30.8 0.4 collective-permute-done.10.refs_1_
  31.2 1.5 %collective-permute-start.11 = (bf16[32,2048]{1,0:T(8,128)(2,1)S(1)}, bf16[32,2048]{1,0:T(8,128)(2,1)S(1)}, u32[]{:S(2)}, u32[]{:S(2)}) collective-permute-start(bf16[32,2048]{1,0:T(8,128)(2,1)S(1)} %get-tuple-element.93), channel_id=1, source_target_pairs={{0,3},{1,2},{2,4},{3,5},{4,7},{5,6},{6,0},{7,1},{8,11},{9,10},{10,... | collective-permute-start | bytes 393224 | tf_op jit(solution)/shard_map/ppermute | solution.py:537
  32.7 1.8 %collective-permute-done.13.refs_2_ = bf16[32,2048]{1,0:T(8,128)(2,1)S(1)} collective-permute-done((bf16[32,2048]{1,0:T(8,128)(2,1)S(1)}, bf16[32,2048]{1,0:T(8,128)(2,1)S(1)}, u32[]{:S(2)}, u32[]{:S(2)}) %collective-permute-start.13) | collective-permute-done | bytes 131104 | tf_op jit(solution)/shard_map/ppermute | solution.py:537
  34.5 1.8 %collective-permute-start.12 = (bf16[32,2048]{1,0:T(8,128)(2,1)S(1)}, bf16[32,2048]{1,0:T(8,128)(2,1)S(1)}, u32[]{:S(2)}, u32[]{:S(2)}) collective-permute-start(bf16[32,2048]{1,0:T(8,128)(2,1)S(1)} %get-tuple-element.94), channel_id=1, source_target_pairs={{0,2},{1,3},{2,0},{3,1},{4,6},{5,7},{6,4},{7,5},{8,10},{9,11},{10,... | collective-permute-start | bytes 393224 | tf_op jit(solution)/shard_map/ppermute | solution.py:537
  36.3 0.8 %join.2.refs_4_ = bf16[32,16384]{1,0:T(8,128)(2,1)} custom-call(bf16[32,2048]{1,0:T(8,128)(2,1)S(1)} %get-tuple-element.95.refs_0_, bf16[32,2048]{1,0:T(8,128)(2,1)S(1)} %collective-permute-done.10.refs_1_, bf16[32,2048]{1,0:T(8,128)(2,1)S(1)} %collective-permute-done.13.refs_2_, bf16[32,2048]{1,0:T(8,128)(2,1)S(1)} %collective-permute-done.14.refs_3_), custom_call_target="tpu_custom_call" | custom-call | tf_op jit(solution)/shard_map/join/pallas_call | solution.py:546
  37.2 1.0 %collective-permute-done.8.refs_0_ = bf16[32,2048]{1,0:T(8,128)(2,1)S(1)} collective-permute-done((bf16[32,2048]{1,0:T(8,128)(2,1)S(1)}, bf16[32,2048]{1,0:T(8,128)(2,1)S(1)}, u32[]{:S(2)}, u32[]{:S(2)}) %collective-permute-start.8) | collective-permute-done | bytes 131104 | tf_op jit(solution)/shard_map/ppermute | solution.py:537
  38.2 2.2 %collective-permute-done.9.refs_1_ = bf16[32,2048]{1,0:T(8,128)(2,1)S(1)} collective-permute-done((bf16[32,2048]{1,0:T(8,128)(2,1)S(1)}, bf16[32,2048]{1,0:T(8,128)(2,1)S(1)}, u32[]{:S(2)}, u32[]{:S(2)}) %collective-permute-start.9) | collective-permute-done | bytes 131104 | tf_op jit(solution)/shard_map/ppermute | solution.py:537
  40.4 0.8 %join.3 = bf16[32,16384]{1,0:T(8,128)(2,1)} custom-call(bf16[32,2048]{1,0:T(8,128)(2,1)S(1)} %collective-permute-done.8.refs_0_, bf16[32,2048]{1,0:T(8,128)(2,1)S(1)} %collective-permute-done.9.refs_1_, bf16[32,2048]{1,0:T(8,128)(2,1)S(1)} %collective-permute-done.11.refs_2_, ...), custom_call_target="tpu_custom_call", output_to_operand_aliasing={{}: (4, {})} | custom-call | tf_op jit(solution)/shard_map/join/pallas_call | solution.py:546
  (22 shorter events, 0.7 us)
Async XLA Ops:
  0.0 4.6 %copy-start = (bf16[64,128,64]{1,2,0:T(8,128)(2,1)S(1)}, bf16[64,128,64]{1,2,0:T(8,128)(2,1)}, u32[]{:S(2)}) copy-start(bf16[64,128,64]{1,2,0:T(8,128)(2,1)} %param.10) | copy-start | bytes 3145732
  0.9 1.2 %copy-start.2 = (bf16[64,8192]{1,0:T(8,128)(2,1)S(1)}, bf16[64,8192]{1,0:T(8,128)(2,1)}, u32[]{:S(2)}) copy-start(bf16[64,8192]{1,0:T(8,128)(2,1)} %q_ref) | copy-start | bytes 3145732
  1.0 3.6 %collective-permute-start.2 = (bf16[64,512]{1,0:T(8,128)(2,1)S(1)}, bf16[64,512]{1,0:T(8,128)(2,1)S(1)}, u32[]{:S(2)}, u32[]{:S(2)}) collective-permute-start(bf16[64,512]{1,0:T(8,128)(2,1)S(1)} %get-tuple-element.52), channel_id=1, source_target_pairs={{0,4},{1,5},{2,6},{3,7},{4,0},{5,1},{6,2},{7,3},{8,12},{9,13},{10,... | collective-permute-start | bytes 196616 | tf_op jit(solution)/shard_map/ppermute | solution.py:431
  2.2 14.5 %collective-permute-start = (bf16[64,2048]{1,0:T(8,128)(2,1)S(1)}, bf16[64,2048]{1,0:T(8,128)(2,1)S(1)}, u32[]{:S(2)}, u32[]{:S(2)}) collective-permute-start(bf16[64,2048]{1,0:T(8,128)(2,1)S(1)} %get-tuple-element.54), channel_id=1, source_target_pairs={{0,4},{1,5},{2,6},{3,7},{4,0},{5,1},{6,2},{7,3},{8,12},{9,13},{10,... | collective-permute-start | bytes 786440 | tf_op jit(solution)/shard_map/ppermute | solution.py:431
  2.6 14.2 %collective-permute-start.1 = (bf16[64,2048]{1,0:T(8,128)(2,1)S(1)}, bf16[64,2048]{1,0:T(8,128)(2,1)S(1)}, u32[]{:S(2)}, u32[]{:S(2)}) collective-permute-start(bf16[64,2048]{1,0:T(8,128)(2,1)S(1)} %get-tuple-element.55), channel_id=1, source_target_pairs={{0,6},{1,7},{2,4},{3,5},{4,2},{5,3},{6,0},{7,1},{8,14},{9,15},{10,... | collective-permute-start | bytes 786440 | tf_op jit(solution)/shard_map/ppermute | solution.py:431
  4.6 3.1 %collective-permute-start.3 = (bf16[128,256]{1,0:T(8,128)(2,1)S(1)}, bf16[128,256]{1,0:T(8,128)(2,1)S(1)}, u32[]{:S(2)}, u32[]{:S(2)}) collective-permute-start(bf16[128,256]{1,0:T(8,128)(2,1)S(1)} %pair_kv.1), channel_id=1, source_target_pairs={{0,2},{1,3},{2,0},{3,1},{4,6},{5,7},{6,4},{7,5},{8,10},{9,11},{10,... | collective-permute-start | bytes 196616 | tf_op jit(solution)/shard_map/ppermute | solution.py:431
  6.7 3.7 %collective-permute-start.4 = (bf16[64,2048]{1,0:T(8,128)(2,1)S(1)}, bf16[64,2048]{1,0:T(8,128)(2,1)S(1)}, u32[]{:S(2)}, u32[]{:S(2)}) collective-permute-start(bf16[64,2048]{1,0:T(8,128)(2,1)S(1)} %get-tuple-element.64), channel_id=1, source_target_pairs={{0,2},{1,3},{2,0},{3,1},{4,6},{5,7},{6,4},{7,5},{8,10},{9,11},{10,... | collective-permute-start | bytes 786440 | tf_op jit(solution)/shard_map/ppermute | solution.py:431
  7.8 4.6 %copy-start.1 = (f32[64]{0:T(128)S(1)}, f32[64]{0:T(128)}, u32[]{:S(2)}) copy-start(f32[64]{0:T(128)} %param.11) | copy-start | bytes 772
  7.8 6.5 %collective-permute-start.5 = (bf16[256,256]{1,0:T(8,128)(2,1)S(1)}, bf16[256,256]{1,0:T(8,128)(2,1)S(1)}, u32[]{:S(2)}, u32[]{:S(2)}) collective-permute-start(bf16[256,256]{1,0:T(8,128)(2,1)S(1)} %stack_kv.1.own_ref.refs_3_), channel_id=1, source_target_pairs={{0,8},{2,10},{4,12},{6,14},{8,16},{10,18},{12,20},{14,22},{16,24},... | collective-permute-start | bytes 393224 | tf_op jit(solution)/shard_map/ppermute | solution.py:435
  9.1 10.0 %collective-permute-start.6 = (bf16[256,256]{1,0:T(8,128)(2,1)S(1)}, bf16[256,256]{1,0:T(8,128)(2,1)S(1)}, u32[]{:S(2)}, u32[]{:S(2)}) collective-permute-start(bf16[256,256]{1,0:T(8,128)(2,1)S(1)} %stack_kv.1.own_ref.refs_3_), channel_id=1, source_target_pairs={{0,24},{2,26},{4,28},{6,30},{1,25},{3,27},{5,29},{7,31}} | collective-permute-start | bytes 393224 | tf_op jit(solution)/shard_map/ppermute | solution.py:435
  10.4 13.4 %collective-permute-start.7 = (bf16[256,256]{1,0:T(8,128)(2,1)S(1)}, bf16[256,256]{1,0:T(8,128)(2,1)S(1)}, u32[]{:S(2)}, u32[]{:S(2)}) collective-permute-start(bf16[256,256]{1,0:T(8,128)(2,1)S(1)} %stack_kv.1.own_ref.refs_3_), channel_id=1, source_target_pairs={{0,16},{2,18},{4,20},{6,22},{8,24},{10,26},{12,28},{14,30},{1,17},... | collective-permute-start | bytes 393224 | tf_op jit(solution)/shard_map/ppermute | solution.py:435
  25.6 5.6 %collective-permute-start.10 = (bf16[32,2048]{1,0:T(8,128)(2,1)S(1)}, bf16[32,2048]{1,0:T(8,128)(2,1)S(1)}, u32[]{:S(2)}, u32[]{:S(2)}) collective-permute-start(bf16[32,2048]{1,0:T(8,128)(2,1)S(1)} %get-tuple-element.92), channel_id=1, source_target_pairs={{0,5},{1,4},{2,7},{3,6},{4,1},{5,0},{6,3},{7,2},{8,13},{9,12},{10,... | collective-permute-start | bytes 393224 | tf_op jit(solution)/shard_map/ppermute | solution.py:537
  26.8 7.7 %collective-permute-start.13 = (bf16[32,2048]{1,0:T(8,128)(2,1)S(1)}, bf16[32,2048]{1,0:T(8,128)(2,1)S(1)}, u32[]{:S(2)}, u32[]{:S(2)}) collective-permute-start(bf16[32,2048]{1,0:T(8,128)(2,1)S(1)} %get-tuple-element.97), channel_id=1, source_target_pairs={{0,4},{1,5},{2,3},{3,2},{4,0},{5,1},{6,7},{7,6},{8,12},{9,13},{10,... | collective-permute-start | bytes 393224 | tf_op jit(solution)/shard_map/ppermute | solution.py:537
  27.0 9.3 %collective-permute-start.14 = (bf16[32,2048]{1,0:T(8,128)(2,1)S(1)}, bf16[32,2048]{1,0:T(8,128)(2,1)S(1)}, u32[]{:S(2)}, u32[]{:S(2)}) collective-permute-start(bf16[32,2048]{1,0:T(8,128)(2,1)S(1)} %get-tuple-element.98), channel_id=1, source_target_pairs={{0,1},{1,0},{2,6},{3,7},{4,5},{5,4},{6,2},{7,3},{8,9},{9,8},{10,14... | collective-permute-start | bytes 393224 | tf_op jit(solution)/shard_map/ppermute | solution.py:537
  28.3 9.9 %collective-permute-start.8 = (bf16[32,2048]{1,0:T(8,128)(2,1)S(1)}, bf16[32,2048]{1,0:T(8,128)(2,1)S(1)}, u32[]{:S(2)}, u32[]{:S(2)}) collective-permute-start(bf16[32,2048]{1,0:T(8,128)(2,1)S(1)} %get-tuple-element.88), channel_id=1, source_target_pairs={{0,7},{1,6},{2,5},{3,4},{4,3},{5,2},{6,1},{7,0},{8,15},{9,14},{10,... | collective-permute-start | bytes 393224 | tf_op jit(solution)/shard_map/ppermute | solution.py:537
  30.6 9.7 %collective-permute-start.9 = (bf16[32,2048]{1,0:T(8,128)(2,1)S(1)}, bf16[32,2048]{1,0:T(8,128)(2,1)S(1)}, u32[]{:S(2)}, u32[]{:S(2)}) collective-permute-start(bf16[32,2048]{1,0:T(8,128)(2,1)S(1)} %get-tuple-element.89), channel_id=1, source_target_pairs={{0,6},{1,7},{2,1},{3,0},{4,2},{5,3},{6,5},{7,4},{8,14},{9,15},{10,... | collective-permute-start | bytes 393224 | tf_op jit(solution)/shard_map/ppermute | solution.py:537
  31.2 9.2 %collective-permute-start.11 = (bf16[32,2048]{1,0:T(8,128)(2,1)S(1)}, bf16[32,2048]{1,0:T(8,128)(2,1)S(1)}, u32[]{:S(2)}, u32[]{:S(2)}) collective-permute-start(bf16[32,2048]{1,0:T(8,128)(2,1)S(1)} %get-tuple-element.93), channel_id=1, source_target_pairs={{0,3},{1,2},{2,4},{3,5},{4,7},{5,6},{6,0},{7,1},{8,11},{9,10},{10,... | collective-permute-start | bytes 393224 | tf_op jit(solution)/shard_map/ppermute | solution.py:537
  34.5 5.9 %collective-permute-start.12 = (bf16[32,2048]{1,0:T(8,128)(2,1)S(1)}, bf16[32,2048]{1,0:T(8,128)(2,1)S(1)}, u32[]{:S(2)}, u32[]{:S(2)}) collective-permute-start(bf16[32,2048]{1,0:T(8,128)(2,1)S(1)} %get-tuple-element.94), channel_id=1, source_target_pairs={{0,2},{1,3},{2,0},{3,1},{4,6},{5,7},{6,4},{7,5},{8,10},{9,11},{10,... | collective-permute-start | bytes 393224 | tf_op jit(solution)/shard_map/ppermute | solution.py:537

commit v5 on v4

--- a/solution.py
+++ b/solution.py
@@ -232,7 +232,7 @@
             for q in range(1, 4):
                 total = total + expd[q * feat // 4 : (q + 1) * feat // 4]
             total = jnp.sum(total.astype(F32), axis=0, keepdims=True)
-            fk_ref[row : row + feat, :] = expd * pl.reciprocal(total).astype(BF16)
+            fk_ref[row : row + feat, :] = expd * pl.reciprocal(total, approx=True).astype(BF16)
 
 
 def own_features_kernel(own_ref, wk_ref, fk_ref):

time: 41.4 us -> 41.4 us (level)
  no operation moved by 1% of the time
where the time goes in v5:
time: 41.4 us; the launch traced here: 41.2 us
  starting transfers between devices  17.2 us (42%)
  Pallas kernels  11.4 us (28%)
  waiting for transfers between devices  9.66 us (23%)
  local copies, waits for them, and re-layouts  2.76 us (7%)
    pallas_call x13, Pallas kernels, call(): pl.pallas_call(kernel, in_specs=[whole_spec() for _ in ins], out_specs=[w...  9.75 us
    ppermute x7, starting transfers between devices, sent(): return lax.ppermute(x, ('seq', 'head'), pairs)  8.49 us
    ppermute x7, waiting for transfers between devices, sent(): return lax.ppermute(x, ('seq', 'head'), pairs)  5.42 us
    ppermute x5, starting transfers between devices, partner(): return lax.ppermute(x, ('seq', 'head'), pairs)  4.82 us
    ppermute x3, waiting for transfers between devices, levels_back(): return lax.ppermute(x, 'seq', pairs)  4.15 us
    ppermute x3, starting transfers between devices, levels_back(): return lax.ppermute(x, 'seq', pairs)  3.88 us
    pallas_call x2, Pallas kernels, joined(): pl.pallas_call(lambda *refs: join_kernel(slots, *refs), in_specs=[whole_s...  1.64 us
    dynamic_slice x2, local copies, waits for them, and re-layouts, by_levels(): lax.dynamic_slice_in_dim(w, place * heads, heads)  0.99 us
  transfers between devices with their start and end apart: 15, of which 7 were waited for; matrix products, arithmetic and copies ran while one was open for 2% of the time, Pallas kernels for 21%

profile of v5, /device:TPU:27, one launch (start us, length us, event | category | flops | bytes accessed | tf_op | source)
XLA Modules:
  0.0 41.2 jit_solution(15599077017931351840)
XLA Ops:
  0.0 0.9 %constant_dynamic-slice_fusion.2 = (bf16[64,256]{1,0:T(8,128)(2,1)S(1)}, bf16[64,256]{1,0:T(8,128)(2,1)S(1)}, bf16[64,256]{1,0:T(8,128)(2,1)S(1)}, bf16[64,256]{1,0:T(8,128)(2,1)S(1)}) fusion(bf16[64,512]{1,0:T(8,128)(2,1)} %param.8, s32[]{:T(128)S(6)} %select_n.19, s32[]{:T(128)S(6)} %select_n.18, bf16[64,512]{1,0:T(8,128)(2,1)} %param.7), kind=kLoop, calls=%fused_computation.2 | loop fusion | bytes 262152 | tf_op jit(solution)/shard_map/dynamic_slice | solution.py:440
  1.0 0.3 collective-permute-start.2
  1.3 0.8 %copy-done.2 = bf16[64,8192]{1,0:T(8,128)(2,1)S(1)} copy-done((bf16[64,8192]{1,0:T(8,128)(2,1)S(1)}, bf16[64,8192]{1,0:T(8,128)(2,1)}, u32[]{:S(2)}) %copy-start.2) | copy-done | bytes 1048600
  2.2 0.4 %collective-permute-start = (bf16[64,2048]{1,0:T(8,128)(2,1)S(1)}, bf16[64,2048]{1,0:T(8,128)(2,1)S(1)}, u32[]{:S(2)}, u32[]{:S(2)}) collective-permute-start(bf16[64,2048]{1,0:T(8,128)(2,1)S(1)} %get-tuple-element.54), channel_id=1, source_target_pairs={{0,4},{1,5},{2,6},{3,7},{4,0},{5,1},{6,2},{7,3},{8,12},{9,13},{10,... | collective-permute-start | bytes 786440 | tf_op jit(solution)/shard_map/ppermute | solution.py:431
  2.6 1.9 %collective-permute-start.1 = (bf16[64,2048]{1,0:T(8,128)(2,1)S(1)}, bf16[64,2048]{1,0:T(8,128)(2,1)S(1)}, u32[]{:S(2)}, u32[]{:S(2)}) collective-permute-start(bf16[64,2048]{1,0:T(8,128)(2,1)S(1)} %get-tuple-element.55), channel_id=1, source_target_pairs={{0,6},{1,7},{2,4},{3,5},{4,2},{5,3},{6,0},{7,1},{8,14},{9,15},{10,... | collective-permute-start | bytes 786440 | tf_op jit(solution)/shard_map/ppermute | solution.py:431
  4.6 2.0 %collective-permute-start.3 = (bf16[128,256]{1,0:T(8,128)(2,1)S(1)}, bf16[128,256]{1,0:T(8,128)(2,1)S(1)}, u32[]{:S(2)}, u32[]{:S(2)}) collective-permute-start(bf16[128,256]{1,0:T(8,128)(2,1)S(1)} %pair_kv.1), channel_id=1, source_target_pairs={{0,2},{1,3},{2,0},{3,1},{4,6},{5,7},{6,4},{7,5},{8,10},{9,11},{10,... | collective-permute-start | bytes 196616 | tf_op jit(solution)/shard_map/ppermute | solution.py:431
  6.8 1.0 %constant_dynamic-slice_fusion.1.wq_ref = bf16[16,64,128]{2,1,0:T(8,128)(2,1)S(1)} fusion(bf16[64,64,128]{2,1,0:T(8,128)(2,1)} %bitcast.5, s32[]{:T(128)S(6)} %select_n.20), kind=kLoop, calls=%fused_computation.1 | loop fusion | bytes 524292 | tf_op jit(solution)/shard_map/dynamic_slice | solution.py:452
  7.8 1.3 %collective-permute-start.5 = (bf16[256,256]{1,0:T(8,128)(2,1)S(1)}, bf16[256,256]{1,0:T(8,128)(2,1)S(1)}, u32[]{:S(2)}, u32[]{:S(2)}) collective-permute-start(bf16[256,256]{1,0:T(8,128)(2,1)S(1)} %stack_kv.1.own_ref.refs_3_), channel_id=1, source_target_pairs={{0,8},{2,10},{4,12},{6,14},{8,16},{10,18},{12,20},{14,22},{16,24},... | collective-permute-start | bytes 393224 | tf_op jit(solution)/shard_map/ppermute | solution.py:435
  9.1 1.3 %collective-permute-start.6 = (bf16[256,256]{1,0:T(8,128)(2,1)S(1)}, bf16[256,256]{1,0:T(8,128)(2,1)S(1)}, u32[]{:S(2)}, u32[]{:S(2)}) collective-permute-start(bf16[256,256]{1,0:T(8,128)(2,1)S(1)} %stack_kv.1.own_ref.refs_3_), channel_id=1, source_target_pairs={{0,24},{2,26},{4,28},{6,30},{1,25},{3,27},{5,29},{7,31}} | collective-permute-start | bytes 393224 | tf_op jit(solution)/shard_map/ppermute | solution.py:435
  10.4 1.3 %collective-permute-start.7 = (bf16[256,256]{1,0:T(8,128)(2,1)S(1)}, bf16[256,256]{1,0:T(8,128)(2,1)S(1)}, u32[]{:S(2)}, u32[]{:S(2)}) collective-permute-start(bf16[256,256]{1,0:T(8,128)(2,1)S(1)} %stack_kv.1.own_ref.refs_3_), channel_id=1, source_target_pairs={{0,16},{2,18},{4,20},{6,22},{8,24},{10,26},{12,28},{14,30},{1,17},... | collective-permute-start | bytes 393224 | tf_op jit(solution)/shard_map/ppermute | solution.py:435
  11.7 0.7 %own_features.1._ = bf16[2048,512]{1,0:T(8,128)(2,1)S(1)} custom-call(bf16[256,256]{1,0:T(8,128)(2,1)S(1)} %stack_kv.1.own_ref.refs_3_, bf16[16,64,128]{2,1,0:T(8,128)(2,1)S(1)} %constant_dynamic-slice_fusion.wk_ref.refs_6_), custom_call_target="tpu_custom_call" | custom-call | tf_op jit(solution)/shard_map/own_features/pallas_call | solution.py:401
  12.4 0.4 weights.1
  12.8 1.1 %query_features.2 = (bf16[2048,128]{1,0:T(8,128)(2,1)S(1)}, bf16[2048,128]{1,0:T(8,128)(2,1)S(1)}) custom-call(bf16[64,2048]{1,0:T(8,128)(2,1)S(1)} %get-tuple-element.56.a_ref, bf16[64,2048]{1,0:T(8,128)(2,1)S(1)} %collective-permute-done.4.b_ref, bf16[16,128,128]{2,1,0:T(8,128)(2,1)S(1)} %get-tuple-element.67.w_ref, f32[16,128]{1,0:T(8,128)S(1)} %get-tuple-element.68.ratio_ref), custom_call_target="tpu_custom_call" | custom-call | tf_op jit(solution)/shard_map/query_features/pallas_call | solution.py:401
  13.9 0.4 collective-permute-done.5.last_ref.refs_2_
  14.3 1.3 %last_features.1 = (bf16[2048,512]{1,0:T(8,128)(2,1)S(1)}, f32[2048,256]{1,0:T(8,128)S(1)}, f32[2048,256]{1,0:T(8,128)S(1)}) custom-call(bf16[256,256]{1,0:T(8,128)(2,1)S(1)} %collective-permute-done.5.last_ref.refs_2_, bf16[16,64,128]{2,1,0:T(8,128)(2,1)S(1)} %constant_dynamic-slice_fusion.wk_ref.refs_6_, ...), custom_call_target="tpu_custom_call", output_to_operand_aliasing={{0}: (2, {})} | custom-call | tf_op jit(solution)/shard_map/last_features/pallas_call | solution.py:401
  15.6 1.1 %near.2.refs_0_ = f32[2048,256]{1,0:T(8,128)S(1)} custom-call(bf16[2048,128]{1,0:T(8,128)(2,1)S(1)} %get-tuple-element.69.refs_0_, bf16[2048,128]{1,0:T(8,128)(2,1)S(1)} %get-tuple-element.73.refs_1_.refs_2_, bf16[256,256]{1,0:T(8,128)(2,1)S(1)} %collective-permute-done.5.last_ref.refs_2_, bf16[256,256]{1,0:T(8,128)(2,1)S(1)} %stack_kv.1.own_ref.refs_3_, ...), custom_call_target="tpu_custom_call" | custom-call | tf_op jit(solution)/shard_map/near/pallas_call | solution.py:401
  16.8 1.1 %query_features.3 = (bf16[2048,128]{1,0:T(8,128)(2,1)S(1)}, bf16[2048,128]{1,0:T(8,128)(2,1)S(1)}) custom-call(bf16[64,2048]{1,0:T(8,128)(2,1)S(1)} %collective-permute-done.a_ref, bf16[64,2048]{1,0:T(8,128)(2,1)S(1)} %collective-permute-done.1.b_ref, bf16[16,128,128]{2,1,0:T(8,128)(2,1)S(1)} %get-tuple-element.67.w_ref, ...), custom_call_target="tpu_custom_call" | custom-call | tf_op jit(solution)/shard_map/query_features/pallas_call | solution.py:401
  18.0 1.1 %near.3.refs_1_ = f32[2048,256]{1,0:T(8,128)S(1)} custom-call(bf16[2048,128]{1,0:T(8,128)(2,1)S(1)} %get-tuple-element.80.refs_0_, bf16[2048,128]{1,0:T(8,128)(2,1)S(1)} %get-tuple-element.81.refs_1_.refs_3_, bf16[256,256]{1,0:T(8,128)(2,1)S(1)} %collective-permute-done.5.last_ref.refs_2_, bf16[256,256]{1,0:T(8,128)(2,1)S(1)} %stack_kv.1.own_ref.refs_3_, ...), custom_call_target="tpu_custom_call" | custom-call | tf_op jit(solution)/shard_map/near/pallas_call | solution.py:401
  19.1 1.0 %past.1.refs_4_ = f32[2048,256]{1,0:T(8,128)S(1)} custom-call(bf16[256,256]{1,0:T(8,128)(2,1)S(1)} %collective-permute-done.6.first_ref, bf16[16,64,128]{2,1,0:T(8,128)(2,1)S(1)} %constant_dynamic-slice_fusion.wk_ref.refs_6_, f32[2048,256]{1,0:T(8,128)S(1)} %get-tuple-element.84.sum_ref), custom_call_target="tpu_custom_call" | custom-call | tf_op jit(solution)/shard_map/past/pallas_call | solution.py:401
  20.1 3.8 %collective-permute-done.7.refs_7_ = bf16[256,256]{1,0:T(8,128)(2,1)S(1)} collective-permute-done((bf16[256,256]{1,0:T(8,128)(2,1)S(1)}, bf16[256,256]{1,0:T(8,128)(2,1)S(1)}, u32[]{:S(2)}, u32[]{:S(2)}) %collective-permute-start.7) | collective-permute-done | bytes 131104 | tf_op jit(solution)/shard_map/ppermute | solution.py:435
  23.8 1.8 %mix_level.1 = (bf16[32,2048]{1,0:T(8,128)(2,1)S(1)}, bf16[32,2048]{1,0:T(8,128)(2,1)S(1)}, bf16[32,2048]{1,0:T(8,128)(2,1)S(1)}, bf16[32,2048]{1,0:T(8,128)(2,1...) custom-call(f32[2048,256]{1,0:T(8,128)S(1)} %near.2.refs_0_, ...), custom_call_target="tpu_custom_call" | custom-call | tf_op jit(solution)/shard_map/mix_level/pallas_call | solution.py:401
  25.6 1.2 %collective-permute-start.10 = (bf16[32,2048]{1,0:T(8,128)(2,1)S(1)}, bf16[32,2048]{1,0:T(8,128)(2,1)S(1)}, u32[]{:S(2)}, u32[]{:S(2)}) collective-permute-start(bf16[32,2048]{1,0:T(8,128)(2,1)S(1)} %get-tuple-element.92), channel_id=1, source_target_pairs={{0,5},{1,4},{2,7},{3,6},{4,1},{5,0},{6,3},{7,2},{8,13},{9,12},{10,... | collective-permute-start | bytes 393224 | tf_op jit(solution)/shard_map/ppermute | solution.py:537
  27.0 1.3 %collective-permute-start.14 = (bf16[32,2048]{1,0:T(8,128)(2,1)S(1)}, bf16[32,2048]{1,0:T(8,128)(2,1)S(1)}, u32[]{:S(2)}, u32[]{:S(2)}) collective-permute-start(bf16[32,2048]{1,0:T(8,128)(2,1)S(1)} %get-tuple-element.98), channel_id=1, source_target_pairs={{0,1},{1,0},{2,6},{3,7},{4,5},{5,4},{6,2},{7,3},{8,9},{9,8},{10,14... | collective-permute-start | bytes 393224 | tf_op jit(solution)/shard_map/ppermute | solution.py:537
  28.3 2.3 %collective-permute-start.8 = (bf16[32,2048]{1,0:T(8,128)(2,1)S(1)}, bf16[32,2048]{1,0:T(8,128)(2,1)S(1)}, u32[]{:S(2)}, u32[]{:S(2)}) collective-permute-start(bf16[32,2048]{1,0:T(8,128)(2,1)S(1)} %get-tuple-element.88), channel_id=1, source_target_pairs={{0,7},{1,6},{2,5},{3,4},{4,3},{5,2},{6,1},{7,0},{8,15},{9,14},{10,... | collective-permute-start | bytes 393224 | tf_op jit(solution)/shard_map/ppermute | solution.py:537
  30.8 0.4 collective-permute-done.10.refs_1_
  31.2 1.5 %collective-permute-start.11 = (bf16[32,2048]{1,0:T(8,128)(2,1)S(1)}, bf16[32,2048]{1,0:T(8,128)(2,1)S(1)}, u32[]{:S(2)}, u32[]{:S(2)}) collective-permute-start(bf16[32,2048]{1,0:T(8,128)(2,1)S(1)} %get-tuple-element.93), channel_id=1, source_target_pairs={{0,3},{1,2},{2,4},{3,5},{4,7},{5,6},{6,0},{7,1},{8,11},{9,10},{10,... | collective-permute-start | bytes 393224 | tf_op jit(solution)/shard_map/ppermute | solution.py:537
  32.7 1.8 %collective-permute-done.13.refs_2_ = bf16[32,2048]{1,0:T(8,128)(2,1)S(1)} collective-permute-done((bf16[32,2048]{1,0:T(8,128)(2,1)S(1)}, bf16[32,2048]{1,0:T(8,128)(2,1)S(1)}, u32[]{:S(2)}, u32[]{:S(2)}) %collective-permute-start.13) | collective-permute-done | bytes 131104 | tf_op jit(solution)/shard_map/ppermute | solution.py:537
  34.5 1.8 %collective-permute-start.12 = (bf16[32,2048]{1,0:T(8,128)(2,1)S(1)}, bf16[32,2048]{1,0:T(8,128)(2,1)S(1)}, u32[]{:S(2)}, u32[]{:S(2)}) collective-permute-start(bf16[32,2048]{1,0:T(8,128)(2,1)S(1)} %get-tuple-element.94), channel_id=1, source_target_pairs={{0,2},{1,3},{2,0},{3,1},{4,6},{5,7},{6,4},{7,5},{8,10},{9,11},{10,... | collective-permute-start | bytes 393224 | tf_op jit(solution)/shard_map/ppermute | solution.py:537
  36.3 0.8 %join.2.refs_4_ = bf16[32,16384]{1,0:T(8,128)(2,1)} custom-call(bf16[32,2048]{1,0:T(8,128)(2,1)S(1)} %get-tuple-element.95.refs_0_, bf16[32,2048]{1,0:T(8,128)(2,1)S(1)} %collective-permute-done.10.refs_1_, bf16[32,2048]{1,0:T(8,128)(2,1)S(1)} %collective-permute-done.13.refs_2_, bf16[32,2048]{1,0:T(8,128)(2,1)S(1)} %collective-permute-done.14.refs_3_), custom_call_target="tpu_custom_call" | custom-call | tf_op jit(solution)/shard_map/join/pallas_call | solution.py:546
  37.2 1.0 %collective-permute-done.8.refs_0_ = bf16[32,2048]{1,0:T(8,128)(2,1)S(1)} collective-permute-done((bf16[32,2048]{1,0:T(8,128)(2,1)S(1)}, bf16[32,2048]{1,0:T(8,128)(2,1)S(1)}, u32[]{:S(2)}, u32[]{:S(2)}) %collective-permute-start.8) | collective-permute-done | bytes 131104 | tf_op jit(solution)/shard_map/ppermute | solution.py:537
  38.2 2.2 %collective-permute-done.9.refs_1_ = bf16[32,2048]{1,0:T(8,128)(2,1)S(1)} collective-permute-done((bf16[32,2048]{1,0:T(8,128)(2,1)S(1)}, bf16[32,2048]{1,0:T(8,128)(2,1)S(1)}, u32[]{:S(2)}, u32[]{:S(2)}) %collective-permute-start.9) | collective-permute-done | bytes 131104 | tf_op jit(solution)/shard_map/ppermute | solution.py:537
  40.4 0.8 %join.3 = bf16[32,16384]{1,0:T(8,128)(2,1)} custom-call(bf16[32,2048]{1,0:T(8,128)(2,1)S(1)} %collective-permute-done.8.refs_0_, bf16[32,2048]{1,0:T(8,128)(2,1)S(1)} %collective-permute-done.9.refs_1_, bf16[32,2048]{1,0:T(8,128)(2,1)S(1)} %collective-permute-done.11.refs_2_, ...), custom_call_target="tpu_custom_call", output_to_operand_aliasing={{}: (4, {})} | custom-call | tf_op jit(solution)/shard_map/join/pallas_call | solution.py:546
  (22 shorter events, 0.7 us)
Async XLA Ops:
  0.0 4.6 %copy-start = (bf16[64,128,64]{1,2,0:T(8,128)(2,1)S(1)}, bf16[64,128,64]{1,2,0:T(8,128)(2,1)}, u32[]{:S(2)}) copy-start(bf16[64,128,64]{1,2,0:T(8,128)(2,1)} %param.10) | copy-start | bytes 3145732
  0.9 1.2 %copy-start.2 = (bf16[64,8192]{1,0:T(8,128)(2,1)S(1)}, bf16[64,8192]{1,0:T(8,128)(2,1)}, u32[]{:S(2)}) copy-start(bf16[64,8192]{1,0:T(8,128)(2,1)} %q_ref) | copy-start | bytes 3145732
  1.0 3.6 %collective-permute-start.2 = (bf16[64,512]{1,0:T(8,128)(2,1)S(1)}, bf16[64,512]{1,0:T(8,128)(2,1)S(1)}, u32[]{:S(2)}, u32[]{:S(2)}) collective-permute-start(bf16[64,512]{1,0:T(8,128)(2,1)S(1)} %get-tuple-element.52), channel_id=1, source_target_pairs={{0,4},{1,5},{2,6},{3,7},{4,0},{5,1},{6,2},{7,3},{8,12},{9,13},{10,... | collective-permute-start | bytes 196616 | tf_op jit(solution)/shard_map/ppermute | solution.py:431
  2.2 14.5 %collective-permute-start = (bf16[64,2048]{1,0:T(8,128)(2,1)S(1)}, bf16[64,2048]{1,0:T(8,128)(2,1)S(1)}, u32[]{:S(2)}, u32[]{:S(2)}) collective-permute-start(bf16[64,2048]{1,0:T(8,128)(2,1)S(1)} %get-tuple-element.54), channel_id=1, source_target_pairs={{0,4},{1,5},{2,6},{3,7},{4,0},{5,1},{6,2},{7,3},{8,12},{9,13},{10,... | collective-permute-start | bytes 786440 | tf_op jit(solution)/shard_map/ppermute | solution.py:431
  2.6 14.2 %collective-permute-start.1 = (bf16[64,2048]{1,0:T(8,128)(2,1)S(1)}, bf16[64,2048]{1,0:T(8,128)(2,1)S(1)}, u32[]{:S(2)}, u32[]{:S(2)}) collective-permute-start(bf16[64,2048]{1,0:T(8,128)(2,1)S(1)} %get-tuple-element.55), channel_id=1, source_target_pairs={{0,6},{1,7},{2,4},{3,5},{4,2},{5,3},{6,0},{7,1},{8,14},{9,15},{10,... | collective-permute-start | bytes 786440 | tf_op jit(solution)/shard_map/ppermute | solution.py:431
  4.6 3.1 %collective-permute-start.3 = (bf16[128,256]{1,0:T(8,128)(2,1)S(1)}, bf16[128,256]{1,0:T(8,128)(2,1)S(1)}, u32[]{:S(2)}, u32[]{:S(2)}) collective-permute-start(bf16[128,256]{1,0:T(8,128)(2,1)S(1)} %pair_kv.1), channel_id=1, source_target_pairs={{0,2},{1,3},{2,0},{3,1},{4,6},{5,7},{6,4},{7,5},{8,10},{9,11},{10,... | collective-permute-start | bytes 196616 | tf_op jit(solution)/shard_map/ppermute | solution.py:431
  6.7 3.7 %collective-permute-start.4 = (bf16[64,2048]{1,0:T(8,128)(2,1)S(1)}, bf16[64,2048]{1,0:T(8,128)(2,1)S(1)}, u32[]{:S(2)}, u32[]{:S(2)}) collective-permute-start(bf16[64,2048]{1,0:T(8,128)(2,1)S(1)} %get-tuple-element.64), channel_id=1, source_target_pairs={{0,2},{1,3},{2,0},{3,1},{4,6},{5,7},{6,4},{7,5},{8,10},{9,11},{10,... | collective-permute-start | bytes 786440 | tf_op jit(solution)/shard_map/ppermute | solution.py:431
  7.8 4.6 %copy-start.1 = (f32[64]{0:T(128)S(1)}, f32[64]{0:T(128)}, u32[]{:S(2)}) copy-start(f32[64]{0:T(128)} %param.11) | copy-start | bytes 772
  7.8 6.5 %collective-permute-start.5 = (bf16[256,256]{1,0:T(8,128)(2,1)S(1)}, bf16[256,256]{1,0:T(8,128)(2,1)S(1)}, u32[]{:S(2)}, u32[]{:S(2)}) collective-permute-start(bf16[256,256]{1,0:T(8,128)(2,1)S(1)} %stack_kv.1.own_ref.refs_3_), channel_id=1, source_target_pairs={{0,8},{2,10},{4,12},{6,14},{8,16},{10,18},{12,20},{14,22},{16,24},... | collective-permute-start | bytes 393224 | tf_op jit(solution)/shard_map/ppermute | solution.py:435
  9.1 10.0 %collective-permute-start.6 = (bf16[256,256]{1,0:T(8,128)(2,1)S(1)}, bf16[256,256]{1,0:T(8,128)(2,1)S(1)}, u32[]{:S(2)}, u32[]{:S(2)}) collective-permute-start(bf16[256,256]{1,0:T(8,128)(2,1)S(1)} %stack_kv.1.own_ref.refs_3_), channel_id=1, source_target_pairs={{0,24},{2,26},{4,28},{6,30},{1,25},{3,27},{5,29},{7,31}} | collective-permute-start | bytes 393224 | tf_op jit(solution)/shard_map/ppermute | solution.py:435
  10.4 13.4 %collective-permute-start.7 = (bf16[256,256]{1,0:T(8,128)(2,1)S(1)}, bf16[256,256]{1,0:T(8,128)(2,1)S(1)}, u32[]{:S(2)}, u32[]{:S(2)}) collective-permute-start(bf16[256,256]{1,0:T(8,128)(2,1)S(1)} %stack_kv.1.own_ref.refs_3_), channel_id=1, source_target_pairs={{0,16},{2,18},{4,20},{6,22},{8,24},{10,26},{12,28},{14,30},{1,17},... | collective-permute-start | bytes 393224 | tf_op jit(solution)/shard_map/ppermute | solution.py:435
  25.6 5.6 %collective-permute-start.10 = (bf16[32,2048]{1,0:T(8,128)(2,1)S(1)}, bf16[32,2048]{1,0:T(8,128)(2,1)S(1)}, u32[]{:S(2)}, u32[]{:S(2)}) collective-permute-start(bf16[32,2048]{1,0:T(8,128)(2,1)S(1)} %get-tuple-element.92), channel_id=1, source_target_pairs={{0,5},{1,4},{2,7},{3,6},{4,1},{5,0},{6,3},{7,2},{8,13},{9,12},{10,... | collective-permute-start | bytes 393224 | tf_op jit(solution)/shard_map/ppermute | solution.py:537
  26.8 7.7 %collective-permute-start.13 = (bf16[32,2048]{1,0:T(8,128)(2,1)S(1)}, bf16[32,2048]{1,0:T(8,128)(2,1)S(1)}, u32[]{:S(2)}, u32[]{:S(2)}) collective-permute-start(bf16[32,2048]{1,0:T(8,128)(2,1)S(1)} %get-tuple-element.97), channel_id=1, source_target_pairs={{0,4},{1,5},{2,3},{3,2},{4,0},{5,1},{6,7},{7,6},{8,12},{9,13},{10,... | collective-permute-start | bytes 393224 | tf_op jit(solution)/shard_map/ppermute | solution.py:537
  27.0 9.3 %collective-permute-start.14 = (bf16[32,2048]{1,0:T(8,128)(2,1)S(1)}, bf16[32,2048]{1,0:T(8,128)(2,1)S(1)}, u32[]{:S(2)}, u32[]{:S(2)}) collective-permute-start(bf16[32,2048]{1,0:T(8,128)(2,1)S(1)} %get-tuple-element.98), channel_id=1, source_target_pairs={{0,1},{1,0},{2,6},{3,7},{4,5},{5,4},{6,2},{7,3},{8,9},{9,8},{10,14... | collective-permute-start | bytes 393224 | tf_op jit(solution)/shard_map/ppermute | solution.py:537
  28.3 9.9 %collective-permute-start.8 = (bf16[32,2048]{1,0:T(8,128)(2,1)S(1)}, bf16[32,2048]{1,0:T(8,128)(2,1)S(1)}, u32[]{:S(2)}, u32[]{:S(2)}) collective-permute-start(bf16[32,2048]{1,0:T(8,128)(2,1)S(1)} %get-tuple-element.88), channel_id=1, source_target_pairs={{0,7},{1,6},{2,5},{3,4},{4,3},{5,2},{6,1},{7,0},{8,15},{9,14},{10,... | collective-permute-start | bytes 393224 | tf_op jit(solution)/shard_map/ppermute | solution.py:537
  30.6 9.7 %collective-permute-start.9 = (bf16[32,2048]{1,0:T(8,128)(2,1)S(1)}, bf16[32,2048]{1,0:T(8,128)(2,1)S(1)}, u32[]{:S(2)}, u32[]{:S(2)}) collective-permute-start(bf16[32,2048]{1,0:T(8,128)(2,1)S(1)} %get-tuple-element.89), channel_id=1, source_target_pairs={{0,6},{1,7},{2,1},{3,0},{4,2},{5,3},{6,5},{7,4},{8,14},{9,15},{10,... | collective-permute-start | bytes 393224 | tf_op jit(solution)/shard_map/ppermute | solution.py:537
  31.2 9.2 %collective-permute-start.11 = (bf16[32,2048]{1,0:T(8,128)(2,1)S(1)}, bf16[32,2048]{1,0:T(8,128)(2,1)S(1)}, u32[]{:S(2)}, u32[]{:S(2)}) collective-permute-start(bf16[32,2048]{1,0:T(8,128)(2,1)S(1)} %get-tuple-element.93), channel_id=1, source_target_pairs={{0,3},{1,2},{2,4},{3,5},{4,7},{5,6},{6,0},{7,1},{8,11},{9,10},{10,... | collective-permute-start | bytes 393224 | tf_op jit(solution)/shard_map/ppermute | solution.py:537
  34.5 5.9 %collective-permute-start.12 = (bf16[32,2048]{1,0:T(8,128)(2,1)S(1)}, bf16[32,2048]{1,0:T(8,128)(2,1)S(1)}, u32[]{:S(2)}, u32[]{:S(2)}) collective-permute-start(bf16[32,2048]{1,0:T(8,128)(2,1)S(1)} %get-tuple-element.94), channel_id=1, source_target_pairs={{0,2},{1,3},{2,0},{3,1},{4,6},{5,7},{6,4},{7,5},{8,10},{9,11},{10,... | collective-permute-start | bytes 393224 | tf_op jit(solution)/shard_map/ppermute | solution.py:537

commit v6 on v5

--- a/solution.py
+++ b/solution.py
@@ -222,12 +222,12 @@
     heads, feat, dh = wk_ref.shape
     logits = dot_t(wk_ref[...].reshape(heads * feat, dh), keys)
     for h in range(heads):
-        part = logits[h * feat : (h + 1) * feat]
+        part = logits[h * feat : (h + 1) * feat] * math.log2(math.e)
         top = jnp.max(part, axis=0, keepdims=True)
         low = jnp.min(part, axis=0, keepdims=True)
         for n, shifted in enumerate((part - top, low - part)):
             row = (2 * h + n) * feat
-            expd = jnp.exp(shifted.astype(BF16))
+            expd = jnp.exp2(shifted.astype(BF16))
             total = expd[: feat // 4]
             for q in range(1, 4):
                 total = total + expd[q * feat // 4 : (q + 1) * feat // 4]

time: 41.4 us -> 41.5 us (level)
  transfers between devices with their start and end apart: 15 -> 15, of which waited for: 7 -> 7; matrix products, arithmetic and copies ran while one was open for 2% -> 2% of each run, Pallas kernels for 21% -> 22%
where the time goes in v6:
time: 41.5 us; the launch traced here: 41.3 us
  starting transfers between devices  17.2 us (41%)
  Pallas kernels  11.6 us (28%)
  waiting for transfers between devices  9.48 us (23%)
  local copies, waits for them, and re-layouts  2.76 us (7%)
    pallas_call x13, Pallas kernels, call(): pl.pallas_call(kernel, in_specs=[whole_spec() for _ in ins], out_specs=[w...  10 us
    ppermute x7, starting transfers between devices, sent(): return lax.ppermute(x, ('seq', 'head'), pairs)  8.49 us
    ppermute x7, waiting for transfers between devices, sent(): return lax.ppermute(x, ('seq', 'head'), pairs)  5.42 us
    ppermute x5, starting transfers between devices, partner(): return lax.ppermute(x, ('seq', 'head'), pairs)  4.82 us
    ppermute x3, waiting for transfers between devices, levels_back(): return lax.ppermute(x, 'seq', pairs)  4 us
    ppermute x3, starting transfers between devices, levels_back(): return lax.ppermute(x, 'seq', pairs)  3.88 us
    pallas_call x2, Pallas kernels, joined(): pl.pallas_call(lambda *refs: join_kernel(slots, *refs), in_specs=[whole_s...  1.64 us
    dynamic_slice x2, local copies, waits for them, and re-layouts, by_levels(): lax.dynamic_slice_in_dim(w, place * heads, heads)  0.99 us
  transfers between devices with their start and end apart: 15, of which 7 were waited for; matrix products, arithmetic and copies ran while one was open for 2% of the time, Pallas kernels for 22%

profile of v6, /device:TPU:27, one launch (start us, length us, event | category | flops | bytes accessed | tf_op | source)
XLA Modules:
  0.0 41.3 jit_solution(8260191594851320269)
XLA Ops:
  0.0 0.9 %constant_dynamic-slice_fusion.2 = (bf16[64,256]{1,0:T(8,128)(2,1)S(1)}, bf16[64,256]{1,0:T(8,128)(2,1)S(1)}, bf16[64,256]{1,0:T(8,128)(2,1)S(1)}, bf16[64,256]{1,0:T(8,128)(2,1)S(1)}) fusion(bf16[64,512]{1,0:T(8,128)(2,1)} %param.8, s32[]{:T(128)S(6)} %select_n.19, s32[]{:T(128)S(6)} %select_n.18, bf16[64,512]{1,0:T(8,128)(2,1)} %param.7), kind=kLoop, calls=%fused_computation.2 | loop fusion | bytes 262152 | tf_op jit(solution)/shard_map/dynamic_slice | solution.py:440
  1.0 0.3 collective-permute-start.2
  1.3 0.8 %copy-done.2 = bf16[64,8192]{1,0:T(8,128)(2,1)S(1)} copy-done((bf16[64,8192]{1,0:T(8,128)(2,1)S(1)}, bf16[64,8192]{1,0:T(8,128)(2,1)}, u32[]{:S(2)}) %copy-start.2) | copy-done | bytes 1048600
  2.2 0.4 %collective-permute-start = (bf16[64,2048]{1,0:T(8,128)(2,1)S(1)}, bf16[64,2048]{1,0:T(8,128)(2,1)S(1)}, u32[]{:S(2)}, u32[]{:S(2)}) collective-permute-start(bf16[64,2048]{1,0:T(8,128)(2,1)S(1)} %get-tuple-element.54), channel_id=1, source_target_pairs={{0,4},{1,5},{2,6},{3,7},{4,0},{5,1},{6,2},{7,3},{8,12},{9,13},{10,... | collective-permute-start | bytes 786440 | tf_op jit(solution)/shard_map/ppermute | solution.py:431
  2.6 1.9 %collective-permute-start.1 = (bf16[64,2048]{1,0:T(8,128)(2,1)S(1)}, bf16[64,2048]{1,0:T(8,128)(2,1)S(1)}, u32[]{:S(2)}, u32[]{:S(2)}) collective-permute-start(bf16[64,2048]{1,0:T(8,128)(2,1)S(1)} %get-tuple-element.55), channel_id=1, source_target_pairs={{0,6},{1,7},{2,4},{3,5},{4,2},{5,3},{6,0},{7,1},{8,14},{9,15},{10,... | collective-permute-start | bytes 786440 | tf_op jit(solution)/shard_map/ppermute | solution.py:431
  4.6 2.0 %collective-permute-start.3 = (bf16[128,256]{1,0:T(8,128)(2,1)S(1)}, bf16[128,256]{1,0:T(8,128)(2,1)S(1)}, u32[]{:S(2)}, u32[]{:S(2)}) collective-permute-start(bf16[128,256]{1,0:T(8,128)(2,1)S(1)} %pair_kv.1), channel_id=1, source_target_pairs={{0,2},{1,3},{2,0},{3,1},{4,6},{5,7},{6,4},{7,5},{8,10},{9,11},{10,... | collective-permute-start | bytes 196616 | tf_op jit(solution)/shard_map/ppermute | solution.py:431
  6.8 1.0 %constant_dynamic-slice_fusion.1.wq_ref = bf16[16,64,128]{2,1,0:T(8,128)(2,1)S(1)} fusion(bf16[64,64,128]{2,1,0:T(8,128)(2,1)} %bitcast.5, s32[]{:T(128)S(6)} %select_n.20), kind=kLoop, calls=%fused_computation.1 | loop fusion | bytes 524292 | tf_op jit(solution)/shard_map/dynamic_slice | solution.py:452
  7.8 1.3 %collective-permute-start.5 = (bf16[256,256]{1,0:T(8,128)(2,1)S(1)}, bf16[256,256]{1,0:T(8,128)(2,1)S(1)}, u32[]{:S(2)}, u32[]{:S(2)}) collective-permute-start(bf16[256,256]{1,0:T(8,128)(2,1)S(1)} %stack_kv.1.own_ref.refs_3_), channel_id=1, source_target_pairs={{0,8},{2,10},{4,12},{6,14},{8,16},{10,18},{12,20},{14,22},{16,24},... | collective-permute-start | bytes 393224 | tf_op jit(solution)/shard_map/ppermute | solution.py:435
  9.1 1.3 %collective-permute-start.6 = (bf16[256,256]{1,0:T(8,128)(2,1)S(1)}, bf16[256,256]{1,0:T(8,128)(2,1)S(1)}, u32[]{:S(2)}, u32[]{:S(2)}) collective-permute-start(bf16[256,256]{1,0:T(8,128)(2,1)S(1)} %stack_kv.1.own_ref.refs_3_), channel_id=1, source_target_pairs={{0,24},{2,26},{4,28},{6,30},{1,25},{3,27},{5,29},{7,31}} | collective-permute-start | bytes 393224 | tf_op jit(solution)/shard_map/ppermute | solution.py:435
  10.4 1.3 %collective-permute-start.7 = (bf16[256,256]{1,0:T(8,128)(2,1)S(1)}, bf16[256,256]{1,0:T(8,128)(2,1)S(1)}, u32[]{:S(2)}, u32[]{:S(2)}) collective-permute-start(bf16[256,256]{1,0:T(8,128)(2,1)S(1)} %stack_kv.1.own_ref.refs_3_), channel_id=1, source_target_pairs={{0,16},{2,18},{4,20},{6,22},{8,24},{10,26},{12,28},{14,30},{1,17},... | collective-permute-start | bytes 393224 | tf_op jit(solution)/shard_map/ppermute | solution.py:435
  11.7 0.8 %own_features.1._ = bf16[2048,512]{1,0:T(8,128)(2,1)S(1)} custom-call(bf16[256,256]{1,0:T(8,128)(2,1)S(1)} %stack_kv.1.own_ref.refs_3_, bf16[16,64,128]{2,1,0:T(8,128)(2,1)S(1)} %constant_dynamic-slice_fusion.wk_ref.refs_6_), custom_call_target="tpu_custom_call" | custom-call | tf_op jit(solution)/shard_map/own_features/pallas_call | solution.py:401
  12.5 0.4 weights.1
  12.9 1.1 %query_features.2 = (bf16[2048,128]{1,0:T(8,128)(2,1)S(1)}, bf16[2048,128]{1,0:T(8,128)(2,1)S(1)}) custom-call(bf16[64,2048]{1,0:T(8,128)(2,1)S(1)} %get-tuple-element.56.a_ref, bf16[64,2048]{1,0:T(8,128)(2,1)S(1)} %collective-permute-done.4.b_ref, bf16[16,128,128]{2,1,0:T(8,128)(2,1)S(1)} %get-tuple-element.67.w_ref, f32[16,128]{1,0:T(8,128)S(1)} %get-tuple-element.68.ratio_ref), custom_call_target="tpu_custom_call" | custom-call | tf_op jit(solution)/shard_map/query_features/pallas_call | solution.py:401
  14.0 0.3 collective-permute-done.5.last_ref.refs_2_
  14.3 1.4 %last_features.1 = (bf16[2048,512]{1,0:T(8,128)(2,1)S(1)}, f32[2048,256]{1,0:T(8,128)S(1)}, f32[2048,256]{1,0:T(8,128)S(1)}) custom-call(bf16[256,256]{1,0:T(8,128)(2,1)S(1)} %collective-permute-done.5.last_ref.refs_2_, bf16[16,64,128]{2,1,0:T(8,128)(2,1)S(1)} %constant_dynamic-slice_fusion.wk_ref.refs_6_, ...), custom_call_target="tpu_custom_call", output_to_operand_aliasing={{0}: (2, {})} | custom-call | tf_op jit(solution)/shard_map/last_features/pallas_call | solution.py:401
  15.7 1.1 %near.2.refs_0_ = f32[2048,256]{1,0:T(8,128)S(1)} custom-call(bf16[2048,128]{1,0:T(8,128)(2,1)S(1)} %get-tuple-element.69.refs_0_, bf16[2048,128]{1,0:T(8,128)(2,1)S(1)} %get-tuple-element.73.refs_1_.refs_2_, bf16[256,256]{1,0:T(8,128)(2,1)S(1)} %collective-permute-done.5.last_ref.refs_2_, bf16[256,256]{1,0:T(8,128)(2,1)S(1)} %stack_kv.1.own_ref.refs_3_, ...), custom_call_target="tpu_custom_call" | custom-call | tf_op jit(solution)/shard_map/near/pallas_call | solution.py:401
  16.8 1.1 %query_features.3 = (bf16[2048,128]{1,0:T(8,128)(2,1)S(1)}, bf16[2048,128]{1,0:T(8,128)(2,1)S(1)}) custom-call(bf16[64,2048]{1,0:T(8,128)(2,1)S(1)} %collective-permute-done.a_ref, bf16[64,2048]{1,0:T(8,128)(2,1)S(1)} %collective-permute-done.1.b_ref, bf16[16,128,128]{2,1,0:T(8,128)(2,1)S(1)} %get-tuple-element.67.w_ref, ...), custom_call_target="tpu_custom_call" | custom-call | tf_op jit(solution)/shard_map/query_features/pallas_call | solution.py:401
  18.0 1.1 %near.3.refs_1_ = f32[2048,256]{1,0:T(8,128)S(1)} custom-call(bf16[2048,128]{1,0:T(8,128)(2,1)S(1)} %get-tuple-element.80.refs_0_, bf16[2048,128]{1,0:T(8,128)(2,1)S(1)} %get-tuple-element.81.refs_1_.refs_3_, bf16[256,256]{1,0:T(8,128)(2,1)S(1)} %collective-permute-done.5.last_ref.refs_2_, bf16[256,256]{1,0:T(8,128)(2,1)S(1)} %stack_kv.1.own_ref.refs_3_, ...), custom_call_target="tpu_custom_call" | custom-call | tf_op jit(solution)/shard_map/near/pallas_call | solution.py:401
  19.1 1.1 %past.1.refs_4_ = f32[2048,256]{1,0:T(8,128)S(1)} custom-call(bf16[256,256]{1,0:T(8,128)(2,1)S(1)} %collective-permute-done.6.first_ref, bf16[16,64,128]{2,1,0:T(8,128)(2,1)S(1)} %constant_dynamic-slice_fusion.wk_ref.refs_6_, f32[2048,256]{1,0:T(8,128)S(1)} %get-tuple-element.84.sum_ref), custom_call_target="tpu_custom_call" | custom-call | tf_op jit(solution)/shard_map/past/pallas_call | solution.py:401
  20.1 3.7 %collective-permute-done.7.refs_7_ = bf16[256,256]{1,0:T(8,128)(2,1)S(1)} collective-permute-done((bf16[256,256]{1,0:T(8,128)(2,1)S(1)}, bf16[256,256]{1,0:T(8,128)(2,1)S(1)}, u32[]{:S(2)}, u32[]{:S(2)}) %collective-permute-start.7) | collective-permute-done | bytes 131104 | tf_op jit(solution)/shard_map/ppermute | solution.py:435
  23.8 1.9 %mix_level.1 = (bf16[32,2048]{1,0:T(8,128)(2,1)S(1)}, bf16[32,2048]{1,0:T(8,128)(2,1)S(1)}, bf16[32,2048]{1,0:T(8,128)(2,1)S(1)}, bf16[32,2048]{1,0:T(8,128)(2,1...) custom-call(f32[2048,256]{1,0:T(8,128)S(1)} %near.2.refs_0_, ...), custom_call_target="tpu_custom_call" | custom-call | tf_op jit(solution)/shard_map/mix_level/pallas_call | solution.py:401
  25.7 1.2 %collective-permute-start.10 = (bf16[32,2048]{1,0:T(8,128)(2,1)S(1)}, bf16[32,2048]{1,0:T(8,128)(2,1)S(1)}, u32[]{:S(2)}, u32[]{:S(2)}) collective-permute-start(bf16[32,2048]{1,0:T(8,128)(2,1)S(1)} %get-tuple-element.92), channel_id=1, source_target_pairs={{0,5},{1,4},{2,7},{3,6},{4,1},{5,0},{6,3},{7,2},{8,13},{9,12},{10,... | collective-permute-start | bytes 393224 | tf_op jit(solution)/shard_map/ppermute | solution.py:537
  27.1 1.3 %collective-permute-start.14 = (bf16[32,2048]{1,0:T(8,128)(2,1)S(1)}, bf16[32,2048]{1,0:T(8,128)(2,1)S(1)}, u32[]{:S(2)}, u32[]{:S(2)}) collective-permute-start(bf16[32,2048]{1,0:T(8,128)(2,1)S(1)} %get-tuple-element.98), channel_id=1, source_target_pairs={{0,1},{1,0},{2,6},{3,7},{4,5},{5,4},{6,2},{7,3},{8,9},{9,8},{10,14... | collective-permute-start | bytes 393224 | tf_op jit(solution)/shard_map/ppermute | solution.py:537
  28.4 2.3 %collective-permute-start.8 = (bf16[32,2048]{1,0:T(8,128)(2,1)S(1)}, bf16[32,2048]{1,0:T(8,128)(2,1)S(1)}, u32[]{:S(2)}, u32[]{:S(2)}) collective-permute-start(bf16[32,2048]{1,0:T(8,128)(2,1)S(1)} %get-tuple-element.88), channel_id=1, source_target_pairs={{0,7},{1,6},{2,5},{3,4},{4,3},{5,2},{6,1},{7,0},{8,15},{9,14},{10,... | collective-permute-start | bytes 393224 | tf_op jit(solution)/shard_map/ppermute | solution.py:537
  30.9 0.4 collective-permute-done.10.refs_1_
  31.3 1.5 %collective-permute-start.11 = (bf16[32,2048]{1,0:T(8,128)(2,1)S(1)}, bf16[32,2048]{1,0:T(8,128)(2,1)S(1)}, u32[]{:S(2)}, u32[]{:S(2)}) collective-permute-start(bf16[32,2048]{1,0:T(8,128)(2,1)S(1)} %get-tuple-element.93), channel_id=1, source_target_pairs={{0,3},{1,2},{2,4},{3,5},{4,7},{5,6},{6,0},{7,1},{8,11},{9,10},{10,... | collective-permute-start | bytes 393224 | tf_op jit(solution)/shard_map/ppermute | solution.py:537
  32.8 1.8 %collective-permute-done.13.refs_2_ = bf16[32,2048]{1,0:T(8,128)(2,1)S(1)} collective-permute-done((bf16[32,2048]{1,0:T(8,128)(2,1)S(1)}, bf16[32,2048]{1,0:T(8,128)(2,1)S(1)}, u32[]{:S(2)}, u32[]{:S(2)}) %collective-permute-start.13) | collective-permute-done | bytes 131104 | tf_op jit(solution)/shard_map/ppermute | solution.py:537
  34.6 1.8 %collective-permute-start.12 = (bf16[32,2048]{1,0:T(8,128)(2,1)S(1)}, bf16[32,2048]{1,0:T(8,128)(2,1)S(1)}, u32[]{:S(2)}, u32[]{:S(2)}) collective-permute-start(bf16[32,2048]{1,0:T(8,128)(2,1)S(1)} %get-tuple-element.94), channel_id=1, source_target_pairs={{0,2},{1,3},{2,0},{3,1},{4,6},{5,7},{6,4},{7,5},{8,10},{9,11},{10,... | collective-permute-start | bytes 393224 | tf_op jit(solution)/shard_map/ppermute | solution.py:537
  36.4 0.8 %join.2.refs_4_ = bf16[32,16384]{1,0:T(8,128)(2,1)} custom-call(bf16[32,2048]{1,0:T(8,128)(2,1)S(1)} %get-tuple-element.95.refs_0_, bf16[32,2048]{1,0:T(8,128)(2,1)S(1)} %collective-permute-done.10.refs_1_, bf16[32,2048]{1,0:T(8,128)(2,1)S(1)} %collective-permute-done.13.refs_2_, bf16[32,2048]{1,0:T(8,128)(2,1)S(1)} %collective-permute-done.14.refs_3_), custom_call_target="tpu_custom_call" | custom-call | tf_op jit(solution)/shard_map/join/pallas_call | solution.py:546
  37.2 1.0 %collective-permute-done.8.refs_0_ = bf16[32,2048]{1,0:T(8,128)(2,1)S(1)} collective-permute-done((bf16[32,2048]{1,0:T(8,128)(2,1)S(1)}, bf16[32,2048]{1,0:T(8,128)(2,1)S(1)}, u32[]{:S(2)}, u32[]{:S(2)}) %collective-permute-start.8) | collective-permute-done | bytes 131104 | tf_op jit(solution)/shard_map/ppermute | solution.py:537
  38.3 2.2 %collective-permute-done.9.refs_1_ = bf16[32,2048]{1,0:T(8,128)(2,1)S(1)} collective-permute-done((bf16[32,2048]{1,0:T(8,128)(2,1)S(1)}, bf16[32,2048]{1,0:T(8,128)(2,1)S(1)}, u32[]{:S(2)}, u32[]{:S(2)}) %collective-permute-start.9) | collective-permute-done | bytes 131104 | tf_op jit(solution)/shard_map/ppermute | solution.py:537
  40.4 0.8 %join.3 = bf16[32,16384]{1,0:T(8,128)(2,1)} custom-call(bf16[32,2048]{1,0:T(8,128)(2,1)S(1)} %collective-permute-done.8.refs_0_, bf16[32,2048]{1,0:T(8,128)(2,1)S(1)} %collective-permute-done.9.refs_1_, bf16[32,2048]{1,0:T(8,128)(2,1)S(1)} %collective-permute-done.11.refs_2_, ...), custom_call_target="tpu_custom_call", output_to_operand_aliasing={{}: (4, {})} | custom-call | tf_op jit(solution)/shard_map/join/pallas_call | solution.py:546
  (22 shorter events, 0.7 us)
Async XLA Ops:
  0.0 4.6 %copy-start = (bf16[64,128,64]{1,2,0:T(8,128)(2,1)S(1)}, bf16[64,128,64]{1,2,0:T(8,128)(2,1)}, u32[]{:S(2)}) copy-start(bf16[64,128,64]{1,2,0:T(8,128)(2,1)} %param.10) | copy-start | bytes 3145732
  0.9 1.2 %copy-start.2 = (bf16[64,8192]{1,0:T(8,128)(2,1)S(1)}, bf16[64,8192]{1,0:T(8,128)(2,1)}, u32[]{:S(2)}) copy-start(bf16[64,8192]{1,0:T(8,128)(2,1)} %q_ref) | copy-start | bytes 3145732
  1.0 3.6 %collective-permute-start.2 = (bf16[64,512]{1,0:T(8,128)(2,1)S(1)}, bf16[64,512]{1,0:T(8,128)(2,1)S(1)}, u32[]{:S(2)}, u32[]{:S(2)}) collective-permute-start(bf16[64,512]{1,0:T(8,128)(2,1)S(1)} %get-tuple-element.52), channel_id=1, source_target_pairs={{0,4},{1,5},{2,6},{3,7},{4,0},{5,1},{6,2},{7,3},{8,12},{9,13},{10,... | collective-permute-start | bytes 196616 | tf_op jit(solution)/shard_map/ppermute | solution.py:431
  2.2 14.5 %collective-permute-start = (bf16[64,2048]{1,0:T(8,128)(2,1)S(1)}, bf16[64,2048]{1,0:T(8,128)(2,1)S(1)}, u32[]{:S(2)}, u32[]{:S(2)}) collective-permute-start(bf16[64,2048]{1,0:T(8,128)(2,1)S(1)} %get-tuple-element.54), channel_id=1, source_target_pairs={{0,4},{1,5},{2,6},{3,7},{4,0},{5,1},{6,2},{7,3},{8,12},{9,13},{10,... | collective-permute-start | bytes 786440 | tf_op jit(solution)/shard_map/ppermute | solution.py:431
  2.6 14.2 %collective-permute-start.1 = (bf16[64,2048]{1,0:T(8,128)(2,1)S(1)}, bf16[64,2048]{1,0:T(8,128)(2,1)S(1)}, u32[]{:S(2)}, u32[]{:S(2)}) collective-permute-start(bf16[64,2048]{1,0:T(8,128)(2,1)S(1)} %get-tuple-element.55), channel_id=1, source_target_pairs={{0,6},{1,7},{2,4},{3,5},{4,2},{5,3},{6,0},{7,1},{8,14},{9,15},{10,... | collective-permute-start | bytes 786440 | tf_op jit(solution)/shard_map/ppermute | solution.py:431
  4.6 3.1 %collective-permute-start.3 = (bf16[128,256]{1,0:T(8,128)(2,1)S(1)}, bf16[128,256]{1,0:T(8,128)(2,1)S(1)}, u32[]{:S(2)}, u32[]{:S(2)}) collective-permute-start(bf16[128,256]{1,0:T(8,128)(2,1)S(1)} %pair_kv.1), channel_id=1, source_target_pairs={{0,2},{1,3},{2,0},{3,1},{4,6},{5,7},{6,4},{7,5},{8,10},{9,11},{10,... | collective-permute-start | bytes 196616 | tf_op jit(solution)/shard_map/ppermute | solution.py:431
  6.7 3.7 %collective-permute-start.4 = (bf16[64,2048]{1,0:T(8,128)(2,1)S(1)}, bf16[64,2048]{1,0:T(8,128)(2,1)S(1)}, u32[]{:S(2)}, u32[]{:S(2)}) collective-permute-start(bf16[64,2048]{1,0:T(8,128)(2,1)S(1)} %get-tuple-element.64), channel_id=1, source_target_pairs={{0,2},{1,3},{2,0},{3,1},{4,6},{5,7},{6,4},{7,5},{8,10},{9,11},{10,... | collective-permute-start | bytes 786440 | tf_op jit(solution)/shard_map/ppermute | solution.py:431
  7.8 4.7 %copy-start.1 = (f32[64]{0:T(128)S(1)}, f32[64]{0:T(128)}, u32[]{:S(2)}) copy-start(f32[64]{0:T(128)} %param.11) | copy-start | bytes 772
  7.8 6.5 %collective-permute-start.5 = (bf16[256,256]{1,0:T(8,128)(2,1)S(1)}, bf16[256,256]{1,0:T(8,128)(2,1)S(1)}, u32[]{:S(2)}, u32[]{:S(2)}) collective-permute-start(bf16[256,256]{1,0:T(8,128)(2,1)S(1)} %stack_kv.1.own_ref.refs_3_), channel_id=1, source_target_pairs={{0,8},{2,10},{4,12},{6,14},{8,16},{10,18},{12,20},{14,22},{16,24},... | collective-permute-start | bytes 393224 | tf_op jit(solution)/shard_map/ppermute | solution.py:435
  9.1 10.0 %collective-permute-start.6 = (bf16[256,256]{1,0:T(8,128)(2,1)S(1)}, bf16[256,256]{1,0:T(8,128)(2,1)S(1)}, u32[]{:S(2)}, u32[]{:S(2)}) collective-permute-start(bf16[256,256]{1,0:T(8,128)(2,1)S(1)} %stack_kv.1.own_ref.refs_3_), channel_id=1, source_target_pairs={{0,24},{2,26},{4,28},{6,30},{1,25},{3,27},{5,29},{7,31}} | collective-permute-start | bytes 393224 | tf_op jit(solution)/shard_map/ppermute | solution.py:435
  10.4 13.4 %collective-permute-start.7 = (bf16[256,256]{1,0:T(8,128)(2,1)S(1)}, bf16[256,256]{1,0:T(8,128)(2,1)S(1)}, u32[]{:S(2)}, u32[]{:S(2)}) collective-permute-start(bf16[256,256]{1,0:T(8,128)(2,1)S(1)} %stack_kv.1.own_ref.refs_3_), channel_id=1, source_target_pairs={{0,16},{2,18},{4,20},{6,22},{8,24},{10,26},{12,28},{14,30},{1,17},... | collective-permute-start | bytes 393224 | tf_op jit(solution)/shard_map/ppermute | solution.py:435
  25.7 5.6 %collective-permute-start.10 = (bf16[32,2048]{1,0:T(8,128)(2,1)S(1)}, bf16[32,2048]{1,0:T(8,128)(2,1)S(1)}, u32[]{:S(2)}, u32[]{:S(2)}) collective-permute-start(bf16[32,2048]{1,0:T(8,128)(2,1)S(1)} %get-tuple-element.92), channel_id=1, source_target_pairs={{0,5},{1,4},{2,7},{3,6},{4,1},{5,0},{6,3},{7,2},{8,13},{9,12},{10,... | collective-permute-start | bytes 393224 | tf_op jit(solution)/shard_map/ppermute | solution.py:537
  26.9 7.7 %collective-permute-start.13 = (bf16[32,2048]{1,0:T(8,128)(2,1)S(1)}, bf16[32,2048]{1,0:T(8,128)(2,1)S(1)}, u32[]{:S(2)}, u32[]{:S(2)}) collective-permute-start(bf16[32,2048]{1,0:T(8,128)(2,1)S(1)} %get-tuple-element.97), channel_id=1, source_target_pairs={{0,4},{1,5},{2,3},{3,2},{4,0},{5,1},{6,7},{7,6},{8,12},{9,13},{10,... | collective-permute-start | bytes 393224 | tf_op jit(solution)/shard_map/ppermute | solution.py:537
  27.1 9.3 %collective-permute-start.14 = (bf16[32,2048]{1,0:T(8,128)(2,1)S(1)}, bf16[32,2048]{1,0:T(8,128)(2,1)S(1)}, u32[]{:S(2)}, u32[]{:S(2)}) collective-permute-start(bf16[32,2048]{1,0:T(8,128)(2,1)S(1)} %get-tuple-element.98), channel_id=1, source_target_pairs={{0,1},{1,0},{2,6},{3,7},{4,5},{5,4},{6,2},{7,3},{8,9},{9,8},{10,14... | collective-permute-start | bytes 393224 | tf_op jit(solution)/shard_map/ppermute | solution.py:537
  28.4 9.9 %collective-permute-start.8 = (bf16[32,2048]{1,0:T(8,128)(2,1)S(1)}, bf16[32,2048]{1,0:T(8,128)(2,1)S(1)}, u32[]{:S(2)}, u32[]{:S(2)}) collective-permute-start(bf16[32,2048]{1,0:T(8,128)(2,1)S(1)} %get-tuple-element.88), channel_id=1, source_target_pairs={{0,7},{1,6},{2,5},{3,4},{4,3},{5,2},{6,1},{7,0},{8,15},{9,14},{10,... | collective-permute-start | bytes 393224 | tf_op jit(solution)/shard_map/ppermute | solution.py:537
  30.7 9.7 %collective-permute-start.9 = (bf16[32,2048]{1,0:T(8,128)(2,1)S(1)}, bf16[32,2048]{1,0:T(8,128)(2,1)S(1)}, u32[]{:S(2)}, u32[]{:S(2)}) collective-permute-start(bf16[32,2048]{1,0:T(8,128)(2,1)S(1)} %get-tuple-element.89), channel_id=1, source_target_pairs={{0,6},{1,7},{2,1},{3,0},{4,2},{5,3},{6,5},{7,4},{8,14},{9,15},{10,... | collective-permute-start | bytes 393224 | tf_op jit(solution)/shard_map/ppermute | solution.py:537
  31.3 9.2 %collective-permute-start.11 = (bf16[32,2048]{1,0:T(8,128)(2,1)S(1)}, bf16[32,2048]{1,0:T(8,128)(2,1)S(1)}, u32[]{:S(2)}, u32[]{:S(2)}) collective-permute-start(bf16[32,2048]{1,0:T(8,128)(2,1)S(1)} %get-tuple-element.93), channel_id=1, source_target_pairs={{0,3},{1,2},{2,4},{3,5},{4,7},{5,6},{6,0},{7,1},{8,11},{9,10},{10,... | collective-permute-start | bytes 393224 | tf_op jit(solution)/shard_map/ppermute | solution.py:537
  34.6 5.9 %collective-permute-start.12 = (bf16[32,2048]{1,0:T(8,128)(2,1)S(1)}, bf16[32,2048]{1,0:T(8,128)(2,1)S(1)}, u32[]{:S(2)}, u32[]{:S(2)}) collective-permute-start(bf16[32,2048]{1,0:T(8,128)(2,1)S(1)} %get-tuple-element.94), channel_id=1, source_target_pairs={{0,2},{1,3},{2,0},{3,1},{4,6},{5,7},{6,4},{7,5},{8,10},{9,11},{10,... | collective-permute-start | bytes 393224 | tf_op jit(solution)/shard_map/ppermute | solution.py:537
